TPU v7x, 128 devices: a whole 4x4x4 slice. The times are simulated.
128 devices in a mesh: gx: 8 (over x, z_lo), gy: 16 (over z_hi, y, core).
Axes of the slice: x: 4, y: 4, z: 4 (z_hi: 2, z_lo: 2; z = z_hi * 2 + z_lo), core: 2. Of those that a mesh axis runs over, the one named last changes fastest.
Arguments:
- tangents: float32 [5, 3, 32, 64, 2048], P(None, None, 'gx', None, 'gy'), may hold values from -72 to 72, as said below
- base_flow: float32 [2, 3, 32, 64, 2048], P(None, None, 'gx', None, 'gy'), may hold values from -4 to 4
- objective_weight: float32 [3, 32, 64, 2048], P(None, 'gx', None, 'gy'), may hold values from -5.6 to 5.6, as said below
Outputs:
- renormed: float32 [5, 3, 32, 64, 2048], P(None, None, 'gx', None, 'gy')
- rfactor: float32 [4, 4], replicated
- coefficients: float32 [4], replicated
- objective: float32 [5], replicated
Inputs may be any that keep to these rules, and one draw needn't show every extreme that they name: `tangents`: finite tangent velocities. `objective_weight`: finite weights.
All inputs are finite; a program needn't handle non-finite values.
Results may differ from a plain program's by a relative error of at most 0.000077.
Values sent between devices are 32-bit elements; how exact they have to be, the bound alone decides.
No kernel may reach another device: no remote copies, remote signals or barrier semaphores. Data moves between devices by JAX's collectives and lax.ppermute only.
A program may use at most 128 MiB of HBM per device.

v0:
```python
import jax
import jax.numpy as jnp
from jax import lax
from jax.sharding import PartitionSpec as P

time_step = 0.2
viscosity = 0.05


def padded_2(cells, sides, width):
    for axis, dim in sides:
        count = lax.axis_size(axis)
        head = lax.slice_in_dim(cells, 0, width, axis=dim)
        tail = lax.slice_in_dim(cells, cells.shape[dim] - width, cells.shape[dim], axis=dim)
        cells = jnp.concatenate(
            [
                lax.ppermute(tail, axis, [(i, (i + 1) % count) for i in range(count)]),
                cells,
                lax.ppermute(head, axis, [((i + 1) % count, i) for i in range(count)]),
            ],
            axis=dim,
        )
    return cells


def take_cells(values_in, step_x, step_y, step_z):
    width_x = values_in.shape[-3] - 2
    width_y = values_in.shape[-1] - 2
    if step_z != 0:
        padded = jnp.pad(values_in, [(0, 0)] * (values_in.ndim - 2) + [(1, 1), (0, 0)])
        values_in = padded[..., 1 + step_z : 1 + step_z + values_in.shape[-2], :]
    return values_in[..., 1 + step_x : 1 + step_x + width_x, :, 1 + step_y : 1 + step_y + width_y]


def gradients(values_in):
    return (
        0.5 * (take_cells(values_in, 1, 0, 0) - take_cells(values_in, -1, 0, 0)),
        0.5 * (take_cells(values_in, 0, 1, 0) - take_cells(values_in, 0, -1, 0)),
        0.5 * (take_cells(values_in, 0, 0, 1) - take_cells(values_in, 0, 0, -1)),
    )


def laplacian(values_in):
    summed = take_cells(values_in, 1, 0, 0) + take_cells(values_in, -1, 0, 0)
    summed = summed + take_cells(values_in, 0, 1, 0) + take_cells(values_in, 0, -1, 0)
    summed = summed + take_cells(values_in, 0, 0, 1) + take_cells(values_in, 0, 0, -1)
    return summed - 6.0 * take_cells(values_in, 0, 0, 0)


def rate_all(wide, flow_wide, source_mask):
    field_grad = gradients(wide)
    flow_grad = gradients(flow_wide)
    field_centre = take_cells(wide, 0, 0, 0)
    flow_centre = take_cells(flow_wide, 0, 0, 0)
    advect = (
        flow_centre[0] * field_grad[0]
        + flow_centre[1] * field_grad[1]
        + flow_centre[2] * field_grad[2]
    )
    produce = (
        field_centre[:, 0:1] * flow_grad[0]
        + field_centre[:, 1:2] * flow_grad[1]
        + field_centre[:, 2:3] * flow_grad[2]
    )
    return -advect - produce + viscosity * laplacian(wide) + source_mask * laplacian(flow_wide)


def with_rims(fields, flow_in):
    joined = jnp.concatenate([fields.reshape((15,) + fields.shape[2:]), flow_in], 0)
    padded = padded_2(joined, (("gx", 1), ("gy", 3)), 1)
    return (padded[:15].reshape((5, 3) + padded.shape[1:]), padded[15:])


def lower_inverse(lower_factor):
    count_rows = lower_factor.shape[0]
    identity_rows = jnp.eye(count_rows, dtype=lower_factor.dtype)
    inverse_rows = []
    for row_index in range(count_rows):
        row_value = identity_rows[row_index]
        for column in range(row_index):
            row_value = row_value - lower_factor[row_index, column] * inverse_rows[column]
        inverse_rows.append(row_value / lower_factor[row_index, row_index])
    return jnp.stack(inverse_rows)


def per_device(tangents, base_flow, objective_weight):
    highest = lax.Precision.HIGHEST
    local_shape = tangents.shape
    source_mask = (jnp.arange(5) == 4).astype(jnp.float32).reshape(5, 1, 1, 1, 1)
    wide, flow_wide = with_rims(tangents, base_flow[0])
    first = tangents + time_step * rate_all(wide, flow_wide, source_mask)
    wide, flow_wide = with_rims(first, base_flow[1])
    second_rate = rate_all(wide, flow_wide, source_mask)
    second = 0.5 * (tangents + first + time_step * second_rate)
    first_local = jnp.sum(objective_weight[None] * first, axis=(1, 2, 3, 4))
    second_local = jnp.sum(objective_weight[None] * second, axis=(1, 2, 3, 4))
    matrix = second.reshape(5, -1)
    gram_local = jnp.dot(matrix, matrix.T, precision=highest)
    total_cells = (
        local_shape[2] * local_shape[3] * local_shape[4] * lax.axis_size("gx") * lax.axis_size("gy")
    )
    first_total = lax.psum(first_local, ("gx", "gy"))
    gram_total, carried_total = lax.psum((gram_local, second_local), ("gx", "gy"))
    objective = 0.5 * (first_total + carried_total) / total_cells
    gram_matrix = gram_total / (3.0 * total_cells)
    lower_factor = jnp.linalg.cholesky(gram_matrix[:4, :4])
    inverse = lower_inverse(lower_factor)
    coefficients = jnp.dot(inverse, gram_matrix[:4, 4], precision=highest)
    ortho = jnp.dot(inverse, matrix[:4], precision=highest)
    last_row = matrix[4] - jnp.dot(coefficients, ortho, precision=highest)
    renormed = jnp.concatenate([ortho, last_row[None]], 0).reshape(local_shape)
    return (renormed, lower_factor.T, coefficients, objective)


def solution(mesh):
    placed = (
        P(None, None, "gx", None, "gy"),
        P(None, None, "gx", None, "gy"),
        P(None, "gx", None, "gy"),
    )
    return jax.shard_map(
        per_device,
        mesh=mesh,
        in_specs=placed,
        out_specs=(P(None, None, "gx", None, "gy"), P(), P(), P()),
        check_vma=False,
    )
```

profile of v0, /device:TPU:1, one launch (start us, length us, event | category | flops | bytes accessed | tf_op | source)
XLA Modules:
  0.0 235.3 jit_solution(13409901271503922823)
XLA Ops:
  0.6 1.2 slice_bitcast_fusion.7
  1.8 1.4 pad_maximum_fusion.8
  3.3 4.7 %collective-permute-start.1 = (f32[18,1,64,128]{3,2,1,0:T(8,128)S(1)}, f32[18,1,64,128]{3,2,1,0:T(8,128)S(1)}, u32[]{:S(2)}, u32[]{:S(2)}) collective-permute-start(f32[18,1,64,128]{3,2,1,0:T(8,128)S(1)} %get-tuple-element.57), channel_id=1, source_target_pairs={{16,0},{32,16},{48,32},{64,48},{80,64},{96,80},{112,96},{0,112},{1... | collective-permute-start | bytes 1769480 | tf_op jit(solution)/shard_map/ppermute | solution.py:19
  8.0 0.9 multiply_bitcast_fusion.2
  8.9 22.6 %collective-permute-done.1 = f32[18,1,64,128]{3,2,1,0:T(8,128)S(1)} collective-permute-done((f32[18,1,64,128]{3,2,1,0:T(8,128)S(1)}, f32[18,1,64,128]{3,2,1,0:T(8,128)S(1)}, u32[]{:S(2)}, u32[]{:S(2)}) %collective-permute-start.1) | collective-permute-done | bytes 589856 | tf_op jit(solution)/shard_map/ppermute | solution.py:19
  31.5 0.9 collective-permute-done
  32.4 0.8 copy-done.8
  33.5 4.1 %fusion.32 = (f32[18,6,64,1]{3,2,1,0:T(8,128)}, f32[18,6,64,1]{3,2,1,0:T(8,128)}) fusion(f32[18,6,64,128]{3,2,1,0:T(8,128)S(1)} %pad_maximum_fusion.2), kind=kLoop, calls=%fused_computation.119 | loop fusion | bytes 110592 | tf_op jit(solution)/shard_map/slice | solution.py:14
  37.6 3.0 %copy.69 = f32[18,6,64,1]{2,1,3,0:T(8,128)S(1)} copy(f32[18,6,64,1]{3,2,1,0:T(8,128)} %get-tuple-element.53) | data formatting | bytes 55296
  41.2 3.6 %copy.68 = f32[18,6,64,1]{2,1,3,0:T(8,128)} copy(f32[18,6,64,1]{3,2,1,0:T(8,128)} %get-tuple-element.52) | data formatting | bytes 55296
  44.8 1.3 collective-permute-start.2
  46.1 3.2 %copy.52 = f32[18,6,64,1]{3,2,1,0:T(8,128)} copy(f32[18,6,64,1]{2,1,3,0:T(8,128)} %collective-permute-done.3) | data formatting | bytes 55296 | tf_op jit(solution)/shard_map/ppermute | solution.py:19
  49.2 2.3 collective-permute-done.2
  51.6 3.2 %copy.51 = f32[18,6,64,1]{3,2,1,0:T(8,128)} copy(f32[18,6,64,1]{2,1,3,0:T(8,128)} %collective-permute-done.2) | data formatting | bytes 55296 | tf_op jit(solution)/shard_map/ppermute | solution.py:17
  54.8 7.0 %pad_maximum_fusion = f32[18,6,64,130]{3,2,1,0:T(8,128)S(1)} fusion(f32[18,6,64,1]{3,2,1,0:T(8,128)} %copy.52, f32[18,1,64,128]{3,2,1,0:T(8,128)S(1)} %collective-permute-done.1, f32[3,4,64,128]{3,2,1,0:T(8,128)S(1)} %get-tuple-element.68, f32[15,4,64,128]{3,2,1,0:T(8,128)S(1)} %bitcast.73, f32[18,1,64,128]{3,2,1,0:T(8,128)} %copy-done.8, f32[18,6,64,1]{3,2,1,0:T(8,128)} %copy.51), kind=kLoop, calls=%fused_computation | loop fusion | flops 4492800 | bytes 7188480 | tf_op jit(solution)/shard_map/concatenate | solution.py:15
  61.8 0.7 slice.409
  63.1 0.7 copy-done.5
  63.9 1.3 copy-done.3
  67.4 3.8 %multiply_reduce_fusion.1 = (f32[5]{0:T(128)S(1)}, f32[5,3,4,64,128]{4,3,2,1,0:T(8,128)S(1)}) fusion(f32[3,4,64,128]{3,2,1,0:T(8,128)S(1)} %copy-done.14, f32[5,3,4,64,128]{4,3,2,1,0:T(8,128)S(1)} %copy-done, f32[3,4,64,128]{3,2,1,0:T(8,128)S(1)} %get-tuple-element.61, f32[5]{0:T(128)S(1)} %compare_convert_fusion, f32[5,3,6,64,130]{4,3,2,1,0:T(8,128)S(1)} %bitcast.84, ...), kind=kLoop, calls=%fused_computation.28 | loop fusion | flops 14745595 | bytes 23986708 | tf_op jit(solution)/shard_map/reduce_sum | solution.py:95
  71.4 2.0 collective-permute-start.5
  73.4 0.8 broadcast_multiply_fusion.1
  74.2 21.3 %collective-permute-done.5 = f32[18,1,64,128]{3,2,1,0:T(8,128)S(1)} collective-permute-done((f32[18,1,64,128]{3,2,1,0:T(8,128)S(1)}, f32[18,1,64,128]{3,2,1,0:T(8,128)S(1)}, u32[]{:S(2)}, u32[]{:S(2)}) %collective-permute-start.5) | collective-permute-done | bytes 589856 | tf_op jit(solution)/shard_map/ppermute | solution.py:19
  95.5 2.9 %collective-permute-done.4 = f32[18,1,64,128]{3,2,1,0:T(8,128)S(1)} collective-permute-done((f32[18,1,64,128]{3,2,1,0:T(8,128)S(1)}, f32[18,1,64,128]{3,2,1,0:T(8,128)S(1)}, u32[]{:S(2)}, u32[]{:S(2)}) %collective-permute-start.4) | collective-permute-done | bytes 589856 | tf_op jit(solution)/shard_map/ppermute | solution.py:17
  98.8 4.1 %fusion.31 = (f32[18,6,64,1]{3,2,1,0:T(8,128)}, f32[18,6,64,1]{3,2,1,0:T(8,128)}) fusion(f32[18,6,64,128]{3,2,1,0:T(8,128)S(1)} %pad_maximum_fusion.3), kind=kLoop, calls=%fused_computation.118 | loop fusion | bytes 110592 | tf_op jit(solution)/shard_map/slice | solution.py:14
  102.9 3.6 %copy.71 = f32[18,6,64,1]{2,1,3,0:T(8,128)} copy(f32[18,6,64,1]{3,2,1,0:T(8,128)} %get-tuple-element.48) | data formatting | bytes 55296
  106.5 1.6 collective-permute-start.7
  108.1 3.6 %copy.70 = f32[18,6,64,1]{2,1,3,0:T(8,128)} copy(f32[18,6,64,1]{3,2,1,0:T(8,128)} %get-tuple-element.47) | data formatting | bytes 55296
  111.9 3.2 %copy.58 = f32[18,6,64,1]{3,2,1,0:T(8,128)} copy(f32[18,6,64,1]{2,1,3,0:T(8,128)} %collective-permute-done.7) | data formatting | bytes 55296 | tf_op jit(solution)/shard_map/ppermute | solution.py:19
  115.0 2.5 %collective-permute-done.6 = f32[18,6,64,1]{2,1,3,0:T(8,128)} collective-permute-done((f32[18,6,64,1]{2,1,3,0:T(8,128)}, f32[18,6,64,1]{2,1,3,0:T(8,128)}, u32[]{:S(2)}, u32[]{:S(2)}) %collective-permute-start.6) | collective-permute-done | bytes 27680 | tf_op jit(solution)/shard_map/ppermute | solution.py:17
  117.6 3.2 %copy.57 = f32[18,6,64,1]{3,2,1,0:T(8,128)} copy(f32[18,6,64,1]{2,1,3,0:T(8,128)} %collective-permute-done.6) | data formatting | bytes 55296 | tf_op jit(solution)/shard_map/ppermute | solution.py:17
  120.8 7.2 %pad_maximum_fusion.1 = f32[18,6,64,130]{3,2,1,0:T(8,128)S(1)} fusion(f32[18,6,64,1]{3,2,1,0:T(8,128)} %copy.58, f32[18,1,64,128]{3,2,1,0:T(8,128)S(1)} %collective-permute-done.5, f32[3,4,64,128]{3,2,1,0:T(8,128)S(1)} %get-tuple-element.69, f32[15,4,64,128]{3,2,1,0:T(8,128)} %bitcast.78, f32[18,1,64,128]{3,2,1,0:T(8,128)S(1)} %collective-permute-done.4, ...), kind=kLoop, calls=%fused_computation.1 | loop fusion | flops 4492800 | bytes 7188480 | tf_op jit(solution)/shard_map/concatenate | solution.py:15
  129.0 1.0 copy-done.4
  130.0 1.1 copy-done.6
  131.1 0.7 copy-done.2
  132.4 1.2 subtract_multiply_fusion.2
  133.9 0.6 copy-done.13
  134.7 4.7 %multiply_reduce_fusion = (f32[5]{0:T(128)S(1)}, f32[5,3,4,64,128]{4,3,2,1,0:T(8,128)S(1)}) fusion(f32[3,4,64,128]{3,2,1,0:T(8,128)S(1)} %copy-done.15, f32[3,4,64,128]{3,2,1,0:T(8,128)S(1)} %get-tuple-element.59, f32[5]{0:T(128)S(1)} %compare_convert_fusion, f32[5,3,6,64,130]{4,3,2,1,0:T(8,128)S(1)} %bitcast.82, ...), kind=kLoop, calls=%fused_computation.27 | loop fusion | flops 15237115 | bytes 25952788 | tf_op jit(solution)/shard_map/reduce_sum | solution.py:96
  139.6 6.8 %fusion.18 = f32[5,5]{0,1:T(8,128)S(1)} fusion(f32[5,3,4,64,128]{4,3,2,1,0:T(8,128)S(1)} %broadcast_multiply_fusion), kind=kOutput, calls=%fused_computation.43 | convolution fusion | flops 29491200 | bytes 1966180 | tf_op jit(solution)/shard_map/dot_general | solution.py:98
  146.6 68.4 %all-reduce.4 = (f32[5,5]{0,1:T(8,128)S(1)}, f32[5]{0:T(128)S(1)}) all-reduce(f32[5,5]{0,1:T(8,128)S(1)} %fusion.18, f32[5]{0:T(128)S(1)} %add.167), channel_id=1, replica_groups=mesh['gx'=8,'gy'=16] {'gx','gy'}, use_global_device_ids=true, to_apply=%region_0.1 | all-reduce | flops 30 | bytes 240 | tf_op jit(solution)/shard_map/psum | solution.py:103
  216.2 0.6 select_select_fusion
  216.8 0.7 fusion.35
  217.5 0.7 fusion.33
  218.2 6.3 %subtract_divide_fusion = (f32[1,4]{1,0:T(1,128)S(1)}, f32[1,4]{1,0:T(1,128)S(1)}, f32[1,4]{1,0:T(1,128)S(1)}, f32[1,4]{1,0:T(1,128)S(1)}) fusion(f32[4,4]{1,0:T(4,128)S(1)} %fusion.22, f32[]{:T(128)} %bitcast.29, f32[]{:T(128)} %bitcast.28, f32[]{:T(128)} %bitcast.27, f32[]{:T(128)} %bitcast.26, f32[]{:T(128)} %bitcast.25, f32[]{:T(128)} %bitcast.24, ...), kind=kLoop, calls=%fused_computation.109 | loop fusion | flops 64 | bytes 168 | tf_op jit(solution)/shard_map/div | solution.py:82
  224.6 3.5 %fusion.14 = f32[4,98304]{1,0:T(4,128)S(1)} fusion(f32[1,4,768,128]{3,2,1,0:T(8,128)S(1)} %bitcast.87, f32[1,4]{1,0:T(1,128)S(1)} %get-tuple-element.18, f32[1,4]{1,0:T(1,128)S(1)} %get-tuple-element.19, f32[1,4]{1,0:T(1,128)S(1)} %get-tuple-element.20, f32[1,4]{1,0:T(1,128)S(1)} %get-tuple-element.21), kind=kOutput, calls=%fused_computation.29 | convolution fusion | flops 18874416 | bytes 3145792 | tf_op jit(solution)/shard_map/dot_general | solution.py:109
  228.1 3.4 %fusion.23 = f32[1,98304]{1,0:T(1,128)} fusion(f32[4,98304]{1,0:T(4,128)S(1)} %fusion.14, f32[1,4]{1,0:T(1,128)S(1)} %fusion.25), kind=kOutput, calls=%fused_computation.107 | convolution fusion | flops 4718592 | bytes 1966096 | tf_op jit(solution)/shard_map/dot_general | solution.py:110
  231.7 0.7 copy.65
  232.9 1.0 sub.109
  233.9 1.4 pad_maximum_fusion.4
  (69 shorter events, 8.7 us)
Async XLA Ops:
  1.8 6.2 %copy-start.10 = (f32[2,3,4,64,128]{4,3,2,1,0:T(8,128)S(1)}, f32[2,3,4,64,128]{4,3,2,1,0:T(8,128)}, u32[]{:S(2)}) copy-start(f32[2,3,4,64,128]{4,3,2,1,0:T(8,128)} %param.4) | copy-start | bytes 2359300
  1.8 31.4 %copy-start = (f32[5,3,4,64,128]{4,3,2,1,0:T(8,128)S(1)}, f32[5,3,4,64,128]{4,3,2,1,0:T(8,128)}, u32[]{:S(2)}) copy-start(f32[5,3,4,64,128]{4,3,2,1,0:T(8,128)} %param.3) | copy-start | bytes 5898244
  3.3 28.2 %collective-permute-start.1 = (f32[18,1,64,128]{3,2,1,0:T(8,128)S(1)}, f32[18,1,64,128]{3,2,1,0:T(8,128)S(1)}, u32[]{:S(2)}, u32[]{:S(2)}) collective-permute-start(f32[18,1,64,128]{3,2,1,0:T(8,128)S(1)} %get-tuple-element.57), channel_id=1, source_target_pairs={{16,0},{32,16},{48,32},{64,48},{80,64},{96,80},{112,96},{0,112},{1... | collective-permute-start | bytes 1769480 | tf_op jit(solution)/shard_map/ppermute | solution.py:19
  8.0 24.4 %collective-permute-start = (f32[18,1,64,128]{3,2,1,0:T(8,128)S(1)}, f32[18,1,64,128]{3,2,1,0:T(8,128)S(1)}, u32[]{:S(2)}, u32[]{:S(2)}) collective-permute-start(f32[18,1,64,128]{3,2,1,0:T(8,128)S(1)} %get-tuple-element.56), channel_id=1, source_target_pairs={{0,16},{16,32},{32,48},{48,64},{64,80},{80,96},{96,112},{112,0},{1... | collective-permute-start | bytes 1769480 | tf_op jit(solution)/shard_map/ppermute | solution.py:17
  32.4 0.8 copy-start.8
  40.6 5.4 %collective-permute-start.3 = (f32[18,6,64,1]{2,1,3,0:T(8,128)S(1)}, f32[18,6,64,1]{2,1,3,0:T(8,128)}, u32[]{:S(2)}, u32[]{:S(2)}) collective-permute-start(f32[18,6,64,1]{2,1,3,0:T(8,128)S(1)} %copy.69), channel_id=1, source_target_pairs={{1,0},{2,1},{3,2},{4,3},{5,4},{6,5},{7,6},{8,7},{9,8},{10,9},{11,1... | collective-permute-start | bytes 82952 | tf_op jit(solution)/shard_map/ppermute | solution.py:19
  44.8 6.8 %collective-permute-start.2 = (f32[18,6,64,1]{2,1,3,0:T(8,128)}, f32[18,6,64,1]{2,1,3,0:T(8,128)}, u32[]{:S(2)}, u32[]{:S(2)}) collective-permute-start(f32[18,6,64,1]{2,1,3,0:T(8,128)} %copy.68), channel_id=1, source_target_pairs={{0,1},{1,2},{2,3},{3,4},{4,5},{5,6},{6,7},{7,8},{8,9},{9,10},{10,1... | collective-permute-start | bytes 82952 | tf_op jit(solution)/shard_map/ppermute | solution.py:17
  61.8 2.0 copy-start.5
  61.8 2.1 copy-start.9
  62.6 2.7 %copy-start.3 = (f32[18,6,64,1]{3,2,1,0:T(8,128)S(1)}, f32[18,6,64,1]{3,2,1,0:T(8,128)}, u32[]{:S(2)}) copy-start(f32[18,6,64,1]{3,2,1,0:T(8,128)} %copy.52) | copy-start | bytes 82948
  65.8 1.1 copy-start.11
  66.3 1.1 copy-start.14
  66.3 1.1 copy-start.18
  66.3 1.1 copy-start.19
  71.3 27.1 %copy-start.1 = (f32[5,3,4,64,128]{4,3,2,1,0:T(8,128)}, f32[5,3,4,64,128]{4,3,2,1,0:T(8,128)S(1)}, u32[]{:S(2)}) copy-start(f32[5,3,4,64,128]{4,3,2,1,0:T(8,128)S(1)} %get-tuple-element.25) | copy-start | bytes 5898244
  71.4 24.1 %collective-permute-start.5 = (f32[18,1,64,128]{3,2,1,0:T(8,128)S(1)}, f32[18,1,64,128]{3,2,1,0:T(8,128)S(1)}, u32[]{:S(2)}, u32[]{:S(2)}) collective-permute-start(f32[18,1,64,128]{3,2,1,0:T(8,128)S(1)} %get-tuple-element.55), channel_id=1, source_target_pairs={{16,0},{32,16},{48,32},{64,48},{80,64},{96,80},{112,96},{0,112},{1... | collective-permute-start | bytes 1769480 | tf_op jit(solution)/shard_map/ppermute | solution.py:19
  73.4 25.0 %collective-permute-start.4 = (f32[18,1,64,128]{3,2,1,0:T(8,128)S(1)}, f32[18,1,64,128]{3,2,1,0:T(8,128)S(1)}, u32[]{:S(2)}, u32[]{:S(2)}) collective-permute-start(f32[18,1,64,128]{3,2,1,0:T(8,128)S(1)} %get-tuple-element.54), channel_id=1, source_target_pairs={{0,16},{16,32},{32,48},{48,64},{64,80},{80,96},{96,112},{112,0},{1... | collective-permute-start | bytes 1769480 | tf_op jit(solution)/shard_map/ppermute | solution.py:17
  106.5 5.4 %collective-permute-start.7 = (f32[18,6,64,1]{2,1,3,0:T(8,128)}, f32[18,6,64,1]{2,1,3,0:T(8,128)}, u32[]{:S(2)}, u32[]{:S(2)}) collective-permute-start(f32[18,6,64,1]{2,1,3,0:T(8,128)} %copy.71), channel_id=1, source_target_pairs={{1,0},{2,1},{3,2},{4,3},{5,4},{6,5},{7,6},{8,7},{9,8},{10,9},{11,1... | collective-permute-start | bytes 82952 | tf_op jit(solution)/shard_map/ppermute | solution.py:19
  111.7 5.9 %collective-permute-start.6 = (f32[18,6,64,1]{2,1,3,0:T(8,128)}, f32[18,6,64,1]{2,1,3,0:T(8,128)}, u32[]{:S(2)}, u32[]{:S(2)}) collective-permute-start(f32[18,6,64,1]{2,1,3,0:T(8,128)} %copy.70), channel_id=1, source_target_pairs={{0,1},{1,2},{2,3},{3,4},{4,5},{5,6},{6,7},{7,8},{8,9},{9,10},{10,1... | collective-permute-start | bytes 82952 | tf_op jit(solution)/shard_map/ppermute | solution.py:17
  128.0 2.0 copy-start.4
  128.0 3.1 %copy-start.6 = (f32[18,6,64,1]{3,2,1,0:T(8,128)S(1)}, f32[18,6,64,1]{3,2,1,0:T(8,128)}, u32[]{:S(2)}) copy-start(f32[18,6,64,1]{3,2,1,0:T(8,128)} %copy.57) | copy-start | bytes 82948
  128.5 3.3 %copy-start.2 = (f32[5,3,4,64,128]{4,3,2,1,0:T(8,128)S(1)}, f32[5,3,4,64,128]{4,3,2,1,0:T(8,128)}, u32[]{:S(2)}) copy-start(f32[5,3,4,64,128]{4,3,2,1,0:T(8,128)} %copy-done.1) | copy-start | bytes 5898244
  132.3 1.2 copy-start.12
  133.6 1.0 copy-start.13
  133.6 1.1 copy-start.15
  133.6 1.1 copy-start.16
  133.6 1.2 copy-start.17
  139.6 6.8 %copy-start.7 = (f32[5,3,4,64,128]{4,3,2,1,0:T(8,128)}, f32[5,3,4,64,128]{4,3,2,1,0:T(8,128)S(1)}, u32[]{:S(2)}) copy-start(f32[5,3,4,64,128]{4,3,2,1,0:T(8,128)S(1)} %broadcast_multiply_fusion) | copy-start | bytes 5898244
  224.6 7.0 %copy-start.20 = (f32[1,4]{1,0:T(1,128)}, f32[1,4]{1,0:T(1,128)S(1)}, u32[]{:S(2)}) copy-start(f32[1,4]{1,0:T(1,128)S(1)} %fusion.25) | copy-start | bytes 52
  231.6 1.3 slice-start
where the time goes:
time: 236 us; the launch traced here: 235 us
  blocking collectives  68.4 us (29%)
  waiting for transfers between devices  52.6 us (22%)
  local copies, waits for them, and re-layouts  47.2 us (20%)
  other arithmetic  42 us (18%)
  matrix products  13.9 us (6%)
  starting transfers between devices  10.3 us (4%)
    psum x1, blocking collectives, per_device(): lax.psum((gram_local, second_local), ('gx', 'gy'))  68.4 us
    ppermute x4, waiting for transfers between devices, padded_2(): lax.ppermute(head, axis, [((i + 1) % count, i) for i in range(count)])  43.9 us
    unnamed x48, local copies, waits for them, and re-layouts  21.9 us
    concatenate x4, other arithmetic, padded_2(): jnp.concatenate([lax.ppermute(tail, axis, [(i, (i + 1) % count) for i in...  14.9 us
    ppermute x4, starting transfers between devices, padded_2(): lax.ppermute(head, axis, [((i + 1) % count, i) for i in range(count)])  8.91 us
    ppermute x4, waiting for transfers between devices, padded_2(): lax.ppermute(tail, axis, [(i, (i + 1) % count) for i in range(count)])  8.67 us
    slice x2, local copies, waits for them, and re-layouts, padded_2(): lax.slice_in_dim(cells, cells.shape[dim] - width, cells.shape[dim], axis=...  8.16 us
    dot_general x1, matrix products, per_device(): gram_local = jnp.dot(matrix, matrix.T, precision=highest)  6.8 us
  transfers between devices with their start and end apart: 8, of which 6 were waited for; matrix products, arithmetic and copies ran while one was open for 6% of the time, Pallas kernels for 0%

commit v1 on v0

v1 whole, which is shorter than its diff:
```python
import functools

import jax
import jax.numpy as jnp
from jax import lax
from jax.experimental import pallas as pl
from jax.experimental.pallas import tpu as pltpu
from jax.sharding import PartitionSpec as P

time_step = 0.2
viscosity = 0.05

groups = ((0, 1, 2), (3, 4))

f32 = jnp.float32
vmem = pl.BlockSpec(memory_space=pltpu.VMEM)
tile = (8, 128)


def shaped(*dims):
    return jax.ShapeDtypeStruct(dims, f32)


def call(body, outs, args, scratch=(), flops=1000000, limit=24):
    return pl.pallas_call(
        body,
        out_shape=outs,
        in_specs=[vmem] * len(args),
        out_specs=jax.tree.map(lambda _: vmem, outs),
        scratch_shapes=list(scratch),
        compiler_params=pltpu.CompilerParams(vmem_limit_bytes=limit << 20),
        cost_estimate=pl.CostEstimate(flops=flops, bytes_accessed=4000000, transcendentals=0),
    )(*args)


def lanes():
    return lax.broadcasted_iota(jnp.int32, tile, 1)


def rows_of(zt):
    return pl.ds(pl.multiple_of(zt * 8, 8), 8)


def sides():
    even = lax.rem(lax.axis_index("gx"), 2) == 0
    z_plane = jnp.where(even, 3, 0)
    z_sign = jnp.where(even, f32(-1), f32(1))
    return ((z_plane, z_sign), (3 - z_plane, -z_sign))


def gy_even():
    return lax.rem(lax.axis_index("gy"), 2) == 0


def column(values, lane):
    return jnp.broadcast_to(values[:, lane : lane + 1], tile)


def faces_kernel(t, u, *outs):
    (z_plane, _), (x_plane, _) = sides()
    last = len(groups) - 1
    for g, members in enumerate(groups):
        sources = [(t, 3 * k + i) for k in members for i in range(3)]
        sources += [(u, i) for i in range(3)] if g == 0 else []
        sources += [(u, 3 + i) for i in range(3)] if g == last else []
        for j, (ref, field) in enumerate(sources):
            outs[2 * g][j] = ref[field, z_plane]
            outs[2 * g + 1][j] = ref[field, x_plane]


def pack_columns(load, count, inner, outer):
    even = gy_even()
    lane = lanes()

    def at_rows(zt, carry):
        rows = rows_of(zt)

        def at_plane(x, packed):
            low, high = packed
            for f in range(count):
                values = load(f, x, rows)
                here = lane == x * 32 + f
                low = jnp.where(here, column(values, 0), low)
                high = jnp.where(here, column(values, 127), high)
            return low, high

        low, high = lax.fori_loop(0, 4, at_plane, (jnp.zeros(tile, f32), jnp.zeros(tile, f32)))
        inner[rows] = jnp.where(even, high, low)
        outer[rows] = jnp.where(even, low, high)
        return carry

    lax.fori_loop(0, 8, at_rows, 0)


def pack_first_kernel(t, u, inner, outer):
    def load(f, x, rows):
        return t[f, x, rows] if f < 15 else u[f - 15, x, rows]

    pack_columns(load, 21, inner, outer)


def fill_padding(padded):
    for f in range(18):
        padded[f, 0] = jnp.zeros((80, 128), f32)
        padded[f, 5] = jnp.zeros((80, 128), f32)

        def at_plane(x, carry):
            padded[f, x, 0:8] = jnp.zeros(tile, f32)
            padded[f, x, 72:80] = jnp.zeros(tile, f32)
            return carry

        lax.fori_loop(1, 5, at_plane, 0)


def section(padded, columns, flow_lane, scale, base, extra, store):
    even = gy_even()
    lane = lanes()
    at_low, at_high = lane == 0, lane == 127

    def at_plane(x, carry):
        for zt in range(8):
            first_row = 8 + 8 * zt
            rows = slice(8 * zt, 8 * zt + 8)
            turn = lax.rem(128 - 32 * x, 128)
            inner, outer = columns[0][rows], columns[1][rows]
            high_side = pltpu.roll(jnp.where(even, inner, outer), turn, axis=1)
            low_side = pltpu.roll(jnp.where(even, outer, inner), turn, axis=1)

            def stencil(f, at):
                def load(dx, dz):
                    return padded[f, x + 1 + dx, first_row + dz : first_row + dz + 8]

                centre = load(0, 0)
                up = jnp.where(at_high, column(high_side, at), pltpu.roll(centre, 127, axis=1))
                down = jnp.where(at_low, column(low_side, at), pltpu.roll(centre, 1, axis=1))
                return centre, load(1, 0), load(-1, 0), up, down, load(0, 1), load(0, -1)

            speed, made, bulk = [], [], []
            for i in range(3):
                flow = stencil(15 + i, flow_lane + i)
                speed.append(flow[0])
                made.append([(-0.5 * scale) * (flow[1 + 2 * j] - flow[2 + 2 * j]) for j in range(3)])
                total = flow[1] + flow[2] + flow[3] + flow[4] + flow[5] + flow[6]
                bulk.append(scale * (total - 6.0 * flow[0]))
            halves = [(0.5 * scale) * u for u in speed]
            ahead = [scale * viscosity - h for h in halves]
            behind = [scale * viscosity + h for h in halves]
            for k in range(5):
                around = [stencil(3 * k + i, 3 * k + i) for i in range(3)]
                for i in range(3):
                    own = around[i]
                    value = (base - 6.0 * viscosity * scale) * own[0]
                    for j in range(3):
                        value += ahead[j] * own[1 + 2 * j] + behind[j] * own[2 + 2 * j]
                        value += made[i][j] * around[j][0]
                    if k == 4:
                        value += bulk[i]
                    if extra is not None:
                        value += 0.5 * extra[3 * k + i, x, rows]
                    store(3 * k + i, x, rows, value)
        return carry

    lax.fori_loop(0, 4, at_plane, 0)


def first_kernel(t, u, inner, outer, *rest):
    outs, padded = rest[:-1], rest[-1]
    fill_padding(padded)

    def copy_plane(x, carry):
        for f in range(15):
            padded[f, x + 1, 8:72] = t[f, x]
        for i in range(3):
            padded[15 + i, x + 1, 8:72] = u[i, x]
        return carry

    lax.fori_loop(0, 4, copy_plane, 0)
    place = {k: (g, n) for g, members in enumerate(groups) for n, k in enumerate(members)}

    def store(f, x, rows, value):
        g, n = place[f // 3]
        outs[g][3 * n + f % 3, x, rows] = value

    section(padded, (inner, outer), 15, time_step, 1.0, None, store)


def halo_terms(scale, sign, speed, tangent, flow_halo):
    weight = scale * viscosity + (0.5 * scale) * sign * speed
    return weight, [
        (0.5 * scale) * sign * v + (scale if k == 4 else 0.0) for k, v in tangent
    ]


def first_faces_kernel(g, part, t, u, z_in, x_in, z_flow, x_flow, z_out, x_out):
    members = groups[g]
    flow_at = 3 * len(groups[0])
    for (plane, sign), got, flow_got, out in zip(sides(), (z_in, x_in), (z_flow, x_flow), (z_out, x_out)):

        def at_rows(zt, carry):
            rows = rows_of(zt)
            flow_halo = [flow_got[flow_at + i, rows] for i in range(3)]
            speed = u[0, plane, rows]
            tangent = [(k, t[3 * k, plane, rows]) for k in members]
            weight, made = halo_terms(time_step, sign, speed, tangent, flow_halo)
            for n in range(len(members)):
                for i in range(3):
                    j = 3 * n + i
                    out[j, rows] = part[j, plane, rows] + weight * got[j, rows] + made[n] * flow_halo[i]
            return carry

        lax.fori_loop(0, 8, at_rows, 0)


def split_refs(refs, *counts):
    pieces, at = [], 0
    for count in counts:
        pieces.append(refs[at : at + count])
        at += count
    pieces.append(refs[at:])
    return pieces


def whole_first(parts, z_faces, x_faces, first):
    (z_plane, _), (x_plane, _) = sides()
    for g, members in enumerate(groups):
        for n, k in enumerate(members):
            for i in range(3):
                f, j = 3 * k + i, 3 * n + i
                first(f, 1, parts[g][j, 1])
                first(f, 2, parts[g][j, 2])
                first(f, z_plane, z_faces[g][j])
                first(f, x_plane, x_faces[g][j])


def pack_second_kernel(*refs):
    count = len(groups)
    parts, z_faces, x_faces, rest = split_refs(refs, count, count, count)
    inner, outer, held = rest

    def put(f, x, values):
        held[f, x] = values

    whole_first(parts, z_faces, x_faces, put)
    pack_columns(lambda f, x, rows: held[f, x, rows], 15, inner, outer)


pairs = [(a, b) for a in range(5) for b in range(a, 5)]


def add_products(sums, rows_now, weighted):
    products = [sums[n] + rows_now[a] * rows_now[b] for n, (a, b) in enumerate(pairs)]
    return products + [sums[15 + k] + weighted[k] for k in range(5)]


def second_kernel(*refs):
    count = len(groups)
    (t, u, weight, flow_inner, flow_outer, inner, outer), parts, z_faces, x_faces, rest = split_refs(
        refs, 7, count, count, count
    )
    out, sums_out, padded, columns_in, columns_out = rest
    fill_padding(padded)

    def put(f, x, values):
        padded[f, x + 1, 8:72] = values

    whole_first(parts, z_faces, x_faces, put)

    def copy_plane(x, carry):
        for i in range(3):
            padded[15 + i, x + 1, 8:72] = u[3 + i, x]
        return carry

    lax.fori_loop(0, 4, copy_plane, 0)
    of_flow = lax.rem(lax.broadcasted_iota(jnp.int32, (64, 128), 1), 32) >= 15
    columns_in[...] = jnp.where(of_flow, flow_inner[...], inner[...])
    columns_out[...] = jnp.where(of_flow, flow_outer[...], outer[...])

    def store(f, x, rows, value):
        out[f, x, rows] = value

    section(padded, (columns_in, columns_out), 18, 0.5 * time_step, 0.5, t, store)

    sums = [jnp.zeros(tile, f32)] * 20
    for x in (1, 2):
        for i in range(3):

            def at_rows(zt, sums):
                rows = rows_of(zt)
                held = pl.ds(pl.multiple_of(zt * 8, 8) + 8, 8)
                now = [out[3 * k + i, x, rows] for k in range(5)]
                scaled = weight[i, x, rows]
                weighted = [scaled * (padded[3 * k + i, x + 1, held] + now[k]) for k in range(5)]
                return add_products(sums, now, weighted)

            sums = lax.fori_loop(0, 8, at_rows, sums)
    for n in range(20):
        sums_out[n] = sums[n]


def second_faces_kernel(*refs):
    count = len(groups)
    (part, u, weight, sums_in, z_flow, x_flow), z_first, x_first, z_in, x_in, rest = split_refs(
        refs, 6, count, count, count, count
    )
    z_out, x_out, sums_out = rest
    last = len(groups) - 1
    flow_at = 3 * len(groups[last]) + (3 if last == 0 else 0)
    scale = 0.5 * time_step
    sums = [sums_in[n] for n in range(20)]
    place = {k: (g, n) for g, members in enumerate(groups) for n, k in enumerate(members)}
    for (plane, sign), first, got, flow_got, out in zip(
        sides(), (z_first, x_first), (z_in, x_in), (z_flow, x_flow), (z_out, x_out)
    ):

        def at_rows(zt, sums):
            rows = rows_of(zt)
            flow_halo = [flow_got[flow_at + i, rows] for i in range(3)]
            speed = u[3, plane, rows]
            tangent = [(k, first[place[k][0]][3 * place[k][1], rows]) for k in range(5)]
            outer_weight, made = halo_terms(scale, sign, speed, tangent, flow_halo)
            for i in range(3):
                now, weighted = [], []
                scaled = weight[i, plane, rows]
                for k in range(5):
                    g, n = place[k]
                    j = 3 * n + i
                    value = part[3 * k + i, plane, rows] + outer_weight * got[g][j, rows] + made[k] * flow_halo[i]
                    out[3 * k + i, rows] = value
                    now.append(value)
                    weighted.append(scaled * (first[g][j, rows] + value))
                sums = add_products(sums, now, weighted)
            return sums

        sums = lax.fori_loop(0, 8, at_rows, sums)
    stacked = jnp.concatenate([jnp.sum(s, axis=0, keepdims=True) for s in sums] + [jnp.zeros((4, 128), f32)], 0)
    totals = jnp.broadcast_to(jnp.sum(stacked, axis=1, keepdims=True), (24, 128))
    diagonal = lax.broadcasted_iota(jnp.int32, (24, 128), 0) == lax.broadcasted_iota(jnp.int32, (24, 128), 1)
    line = jnp.sum(jnp.where(diagonal, totals, 0.0), axis=0, keepdims=True)
    sums_out[...] = jnp.broadcast_to(line[None], sums_out.shape)


def renorm_kernel(total_cells, part, z_faces, x_faces, gathered, out, r_out, c_out, o_out):
    line = jnp.sum(gathered[...], axis=0)
    spread = [jnp.broadcast_to(line[:, n : n + 1], tile) for n in range(20)]
    gram = {pair: spread[n] * f32(1.0 / (3.0 * total_cells)) for n, pair in enumerate(pairs)}
    lower = {}
    for c in range(4):
        value = gram[(c, c)]
        for m in range(c):
            value = value - lower[(c, m)] * lower[(c, m)]
        lower[(c, c)] = jnp.sqrt(value)
        for r in range(c + 1, 4):
            value = gram[(c, r)]
            for m in range(c):
                value = value - lower[(r, m)] * lower[(c, m)]
            lower[(r, c)] = value / lower[(c, c)]
    inverse = {}
    for r in range(4):
        for c in range(r + 1):
            value = jnp.ones(tile, f32) if r == c else jnp.zeros(tile, f32)
            for m in range(c, r):
                value = value - lower[(r, m)] * inverse[(m, c)]
            inverse[(r, c)] = value / lower[(r, r)]
    coefficient = []
    for r in range(4):
        value = inverse[(r, 0)] * gram[(0, 4)]
        for c in range(1, r + 1):
            value = value + inverse[(r, c)] * gram[(c, 4)]
        coefficient.append(value)

    row, lane = lax.broadcasted_iota(jnp.int32, tile, 0), lanes()
    factor, coefficients, objective = (jnp.zeros(tile, f32) for _ in range(3))
    for r in range(4):
        for c in range(r + 1):
            factor = jnp.where((row == c) & (lane == r), lower[(r, c)], factor)
        coefficients = jnp.where(lane == r, coefficient[r], coefficients)
    for k in range(5):
        objective = jnp.where(lane == k, spread[15 + k] * f32(0.5 / total_cells), objective)
    r_out[...] = factor[:4, :4]
    c_out[...] = coefficients[0, :4]
    o_out[...] = objective[0, :5]

    def combine(load, store):
        def at_rows(zt, carry):
            rows = rows_of(zt)
            for i in range(3):
                now = [load(3 * k + i, rows) for k in range(5)]
                last = now[4]
                for r in range(4):
                    value = inverse[(r, 0)] * now[0]
                    for c in range(1, r + 1):
                        value = value + inverse[(r, c)] * now[c]
                    store(3 * r + i, rows, value)
                    last = last - coefficient[r] * value
                store(12 + i, rows, last)
            return carry

        lax.fori_loop(0, 8, at_rows, 0)

    (z_plane, _), (x_plane, _) = sides()
    for plane, load in (
        (1, lambda f, rows: part[f, 1, rows]),
        (2, lambda f, rows: part[f, 2, rows]),
        (z_plane, lambda f, rows: z_faces[f, rows]),
        (x_plane, lambda f, rows: x_faces[f, rows]),
    ):

        def store(f, rows, value):
            out[f, plane, rows] = value

        combine(load, store)


def per_device(tangents, base_flow, objective_weight):
    count_x, count_y = lax.axis_size("gx"), lax.axis_size("gy")
    total_cells = 4 * 64 * 128 * count_x * count_y
    t = tangents.reshape(15, 4, 64, 128)
    u = base_flow.reshape(6, 4, 64, 128)
    last = len(groups) - 1

    def partner(values, axis, count):
        return lax.ppermute(values, axis, [(i, i ^ 1) for i in range(count)])

    def beyond(values, axis, count):
        return lax.ppermute(values, axis, [(i, (i + 2 * (i % 2) - 1) % count) for i in range(count)])

    sizes = [3 * len(members) for members in groups]
    sent = [s + (3 if g == 0 else 0) + (3 if g == last else 0) for g, s in enumerate(sizes)]
    faces = call(faces_kernel, tuple(shaped(s, 64, 128) for s in sent for _ in range(2)), (t, u))
    z_in = [partner(faces[2 * g], "gx", count_x) for g in range(len(groups))]
    x_in = [beyond(faces[2 * g + 1], "gx", count_x) for g in range(len(groups))]
    inner, outer = call(pack_first_kernel, (shaped(64, 128), shaped(64, 128)), (t, u))
    flow_inner = partner(inner, "gy", count_y)
    flow_outer = beyond(outer, "gy", count_y)
    parts = call(
        first_kernel,
        tuple(shaped(s, 4, 64, 128) for s in sizes),
        (t, u, flow_inner, flow_outer),
        scratch=[pltpu.VMEM((18, 6, 80, 128), f32)],
        flops=10000000,
    )
    z_first, x_first, z_next, x_next = [], [], [], []
    for g in range(len(groups)):
        z_face, x_face = call(
            functools.partial(first_faces_kernel, g),
            (shaped(sizes[g], 64, 128), shaped(sizes[g], 64, 128)),
            (parts[g], t, u, z_in[g], x_in[g], z_in[0], x_in[0]),
        )
        z_first.append(z_face)
        x_first.append(x_face)
        z_next.append(partner(z_face, "gx", count_x))
        x_next.append(beyond(x_face, "gx", count_x))
    inner, outer = call(
        pack_second_kernel,
        (shaped(64, 128), shaped(64, 128)),
        (*parts, *z_first, *x_first),
        scratch=[pltpu.VMEM((15, 4, 64, 128), f32)],
    )
    inner = partner(inner, "gy", count_y)
    outer = beyond(outer, "gy", count_y)
    part, sums = call(
        second_kernel,
        (shaped(15, 4, 64, 128), shaped(20, 8, 128)),
        (t, u, objective_weight, flow_inner, flow_outer, inner, outer, *parts, *z_first, *x_first),
        scratch=[
            pltpu.VMEM((18, 6, 80, 128), f32),
            pltpu.VMEM((64, 128), f32),
            pltpu.VMEM((64, 128), f32),
        ],
        flops=10000000,
    )
    z_second, x_second, line = call(
        second_faces_kernel,
        (shaped(15, 64, 128), shaped(15, 64, 128), shaped(count_x * count_y, 1, 128)),
        (part, u, objective_weight, sums, z_in[last], x_in[last], *z_first, *x_first, *z_next, *x_next),
    )
    gathered = lax.all_to_all(line, ("gx", "gy"), 0, 0, tiled=True)
    renormed, rfactor, coefficients, objective = call(
        functools.partial(renorm_kernel, total_cells),
        (shaped(15, 4, 64, 128), shaped(4, 4), shaped(4), shaped(5)),
        (part, z_second, x_second, gathered),
    )
    return (renormed.reshape(tangents.shape), rfactor, coefficients, objective)


def solution(mesh):
    placed = (
        P(None, None, "gx", None, "gy"),
        P(None, None, "gx", None, "gy"),
        P(None, "gx", None, "gy"),
    )
    return jax.shard_map(
        per_device,
        mesh=mesh,
        in_specs=placed,
        out_specs=(P(None, None, "gx", None, "gy"), P(), P(), P()),
        check_vma=False,
    )
```

time: 236 us -> 88.2 us (0.37)
  blocking collectives: 68.4 us -> 21.3 us
  local copies, waits for them, and re-layouts: 47.2 us -> 2.69 us
  other arithmetic: 42 us -> 0 us
  waiting for transfers between devices: 52.6 us -> 18.3 us
  Pallas kernels: 0 us -> 22.9 us
  matrix products: 13.9 us -> 0 us
  starting transfers between devices: 10.3 us -> 22.1 us
    psum x1 -> x0, blocking collectives: 68.4 us -> none  [per_device(): lax.psum((gram_local, second_local), ('gx', 'gy'))]
    ppermute x8 -> x12, waiting for transfers between devices: 52.6 us -> 18.3 us  [the longest x6 13.7 us: partner(): return lax.ppermute(values, axis, [(i, i ^ 1) for i in range(count)])]
    pallas_call x0 -> x9, Pallas kernels: none -> 22.9 us  [call(): pl.pallas_call(body, out_shape=outs, in_specs=[vmem] * len(args), out_spe...]
    all_to_all x0 -> x1, blocking collectives: none -> 21.3 us  [per_device(): gathered = lax.all_to_all(line, ('gx', 'gy'), 0, 0, tiled=True)]
    unnamed x48 -> x10, local copies, waits for them, and re-layouts: 21.9 us -> 2.69 us
    concatenate x5 -> x0, other arithmetic: 16.4 us -> none  [the longest x4 14.9 us: padded_2(): jnp.concatenate([lax.ppermute(tail, axis, [(i, (i + 1) % count) for i in...]
    dot_general x4 -> x0, matrix products: 13.9 us -> none  [the longest x1 6.8 us: per_device(): gram_local = jnp.dot(matrix, matrix.T, precision=highest)]
    ppermute x4 -> x0, local copies, waits for them, and re-layouts: 12.8 us -> none  [the longest x2 6.42 us: padded_2(): lax.ppermute(tail, axis, [(i, (i + 1) % count) for i in range(count)])]
  transfers between devices with their start and end apart: 8 -> 12, of which waited for: 6 -> 6; matrix products, arithmetic and copies ran while one was open for 6% -> 0% of each run, Pallas kernels for 0% -> 23%
where the time goes in v1:
time: 88.2 us; the launch traced here: 88 us
  Pallas kernels  22.9 us (26%)
  starting transfers between devices  22.1 us (25%)
  blocking collectives  21.3 us (24%)
  waiting for transfers between devices  18.3 us (21%)
  local copies, waits for them, and re-layouts  2.69 us (3%)
    pallas_call x9, Pallas kernels, call(): pl.pallas_call(body, out_shape=outs, in_specs=[vmem] * len(args), out_spe...  22.9 us
    all_to_all x1, blocking collectives, per_device(): gathered = lax.all_to_all(line, ('gx', 'gy'), 0, 0, tiled=True)  21.3 us
    ppermute x6, waiting for transfers between devices, partner(): return lax.ppermute(values, axis, [(i, i ^ 1) for i in range(count)])  13.7 us
    ppermute x6, starting transfers between devices, beyond(): lax.ppermute(values, axis, [(i, (i + 2 * (i % 2) - 1) % count) for i in r...  11.3 us
    ppermute x6, starting transfers between devices, partner(): return lax.ppermute(values, axis, [(i, i ^ 1) for i in range(count)])  10.8 us
    ppermute x6, waiting for transfers between devices, beyond(): lax.ppermute(values, axis, [(i, (i + 2 * (i % 2) - 1) % count) for i in r...  4.57 us
    unnamed x10, local copies, waits for them, and re-layouts  2.69 us
  transfers between devices with their start and end apart: 12, of which 6 were waited for; matrix products, arithmetic and copies ran while one was open for 0% of the time, Pallas kernels for 23%

profile of v1, /device:TPU:1, one launch (start us, length us, event | category | flops | bytes accessed | tf_op | source)
XLA Modules:
  0.0 88.0 jit_solution(14280694160762712700)
XLA Ops:
  0.6 0.0 copy-start
  0.6 1.5 %copy-done = f32[5,3,4,64,128]{4,3,2,1,0:T(8,128)S(1)} copy-done((f32[5,3,4,64,128]{4,3,2,1,0:T(8,128)S(1)}, f32[5,3,4,64,128]{4,3,2,1,0:T(8,128)}, u32[]{:S(2)}) %copy-start) | copy-done | bytes 1966104
  2.2 0.0 copy-start.2
  2.2 1.1 %copy-done.2 = f32[2,3,4,64,128]{4,3,2,1,0:T(8,128)S(1)} copy-done((f32[2,3,4,64,128]{4,3,2,1,0:T(8,128)S(1)}, f32[2,3,4,64,128]{4,3,2,1,0:T(8,128)}, u32[]{:S(2)}) %copy-start.2) | copy-done | bytes 786456
  3.3 0.1 shard_map.68
  3.4 2.5 %collective-permute-start.2 = (f32[12,64,128]{2,1,0:T(8,128)S(1)}, f32[12,64,128]{2,1,0:T(8,128)S(1)}, u32[]{:S(2)}, u32[]{:S(2)}) collective-permute-start(f32[12,64,128]{2,1,0:T(8,128)S(1)} %get-tuple-element.31), channel_id=1, source_target_pairs={{0,16},{16,0},{32,48},{48,32},{64,80},{80,64},{96,112},{112,96},{1... | collective-permute-start | bytes 1179656 | tf_op jit(solution)/shard_map/ppermute | solution.py:422
  6.0 2.3 %collective-permute-start.3 = (f32[12,64,128]{2,1,0:T(8,128)S(1)}, f32[12,64,128]{2,1,0:T(8,128)S(1)}, u32[]{:S(2)}, u32[]{:S(2)}) collective-permute-start(f32[12,64,128]{2,1,0:T(8,128)S(1)} %get-tuple-element.32), channel_id=1, source_target_pairs={{0,112},{16,32},{32,16},{48,64},{64,48},{80,96},{96,80},{112,0},{1... | collective-permute-start | bytes 1179656 | tf_op jit(solution)/shard_map/ppermute | solution.py:425
  8.2 0.1 collective-permute-start.4
  8.3 1.6 %collective-permute-start.5 = (f32[9,64,128]{2,1,0:T(8,128)S(1)}, f32[9,64,128]{2,1,0:T(8,128)S(1)}, u32[]{:S(2)}, u32[]{:S(2)}) collective-permute-start(f32[9,64,128]{2,1,0:T(8,128)S(1)} %get-tuple-element.35), channel_id=1, source_target_pairs={{0,112},{16,32},{32,16},{48,64},{64,48},{80,96},{96,80},{112,0},{1... | collective-permute-start | bytes 884744 | tf_op jit(solution)/shard_map/ppermute | solution.py:425
  10.0 3.7 %shard_map.66 = (f32[64,128]{1,0:T(8,128)S(1)}, f32[64,128]{1,0:T(8,128)S(1)}) custom-call(f32[15,4,64,128]{3,2,1,0:T(8,128)S(1)} %bitcast.4, f32[6,4,64,128]{3,2,1,0:T(8,128)S(1)} %bitcast.10), custom_call_target="tpu_custom_call" | custom-call | flops 1000000 | bytes 4000000 | tf_op jit(solution)/shard_map/pallas_call | solution.py:25
  13.6 1.6 %collective-permute-start = (f32[64,128]{1,0:T(8,128)S(1)}, f32[64,128]{1,0:T(8,128)S(1)}, u32[]{:S(2)}, u32[]{:S(2)}) collective-permute-start(f32[64,128]{1,0:T(8,128)S(1)} %get-tuple-element.27), channel_id=1, source_target_pairs={{0,1},{1,0},{2,3},{3,2},{4,5},{5,4},{6,7},{7,6},{8,9},{9,8},{10,11... | collective-permute-start | bytes 98312 | tf_op jit(solution)/shard_map/ppermute | solution.py:422
  15.2 0.9 collective-permute-done.inner.refs_3_
  16.1 1.5 %collective-permute-start.1 = (f32[64,128]{1,0:T(8,128)S(1)}, f32[64,128]{1,0:T(8,128)S(1)}, u32[]{:S(2)}, u32[]{:S(2)}) collective-permute-start(f32[64,128]{1,0:T(8,128)S(1)} %get-tuple-element.28), channel_id=1, source_target_pairs={{0,15},{1,2},{2,1},{3,4},{4,3},{5,6},{6,5},{7,8},{8,7},{9,10},{10,... | collective-permute-start | bytes 98312 | tf_op jit(solution)/shard_map/ppermute | solution.py:425
  17.6 2.1 %collective-permute-done.1.outer.refs_4_ = f32[64,128]{1,0:T(8,128)S(1)} collective-permute-done((f32[64,128]{1,0:T(8,128)S(1)}, f32[64,128]{1,0:T(8,128)S(1)}, u32[]{:S(2)}, u32[]{:S(2)}) %collective-permute-start.1) | collective-permute-done | bytes 32800 | tf_op jit(solution)/shard_map/ppermute | solution.py:425
  19.7 5.9 %shard_map.67 = (f32[9,4,64,128]{3,2,1,0:T(8,128)S(1)}, f32[6,4,64,128]{3,2,1,0:T(8,128)S(1)}) custom-call(f32[15,4,64,128]{3,2,1,0:T(8,128)S(1)} %bitcast.5, f32[6,4,64,128]{3,2,1,0:T(8,128)S(1)} %bitcast.11, f32[64,128]{1,0:T(8,128)S(1)} %collective-permute-done.inner.refs_3_, f32[64,128]{1,0:T(8,128)S(1)} %collective-permute-done.1.outer.refs_4_), custom_call_target="tpu_custom_call" | custom-call | flops 10000000 | bytes 4000000 | tf_op jit(solution)/shard_map/pallas_call | solution.py:25
  25.6 4.3 %collective-permute-done.2.z_in.z_flow = f32[12,64,128]{2,1,0:T(8,128)S(1)} collective-permute-done((f32[12,64,128]{2,1,0:T(8,128)S(1)}, f32[12,64,128]{2,1,0:T(8,128)S(1)}, u32[]{:S(2)}, u32[]{:S(2)}) %collective-permute-start.2) | collective-permute-done | bytes 393248 | tf_op jit(solution)/shard_map/ppermute | solution.py:422
  29.9 0.0 collective-permute-done.3.x_in.x_flow
  29.9 0.3 shard_map.69
  30.2 1.3 %collective-permute-start.8 = (f32[9,64,128]{2,1,0:T(8,128)S(1)}, f32[9,64,128]{2,1,0:T(8,128)S(1)}, u32[]{:S(2)}, u32[]{:S(2)}) collective-permute-start(f32[9,64,128]{2,1,0:T(8,128)S(1)} %get-tuple-element.33.refs_2_.refs_9_.refs_6_), channel_id=1, source_target_pairs={{0,16},{16,0},{32,48},{48,32},{64,80},{80,64},{96,112},{112,96},{1... | collective-permute-start | bytes 884744 | tf_op jit(solution)/shard_map/ppermute | solution.py:422
  31.4 2.4 %collective-permute-start.10 = (f32[9,64,128]{2,1,0:T(8,128)S(1)}, f32[9,64,128]{2,1,0:T(8,128)S(1)}, u32[]{:S(2)}, u32[]{:S(2)}) collective-permute-start(f32[9,64,128]{2,1,0:T(8,128)S(1)} %get-tuple-element.37.refs_4_.refs_11_.refs_8_), channel_id=1, source_target_pairs={{0,112},{16,32},{32,16},{48,64},{64,48},{80,96},{96,80},{112,0},{1... | collective-permute-start | bytes 884744 | tf_op jit(solution)/shard_map/ppermute | solution.py:425
  33.8 7.7 %collective-permute-done.4.z_in.refs_4_ = f32[9,64,128]{2,1,0:T(8,128)S(1)} collective-permute-done((f32[9,64,128]{2,1,0:T(8,128)S(1)}, f32[9,64,128]{2,1,0:T(8,128)S(1)}, u32[]{:S(2)}, u32[]{:S(2)}) %collective-permute-start.4) | collective-permute-done | bytes 294944 | tf_op jit(solution)/shard_map/ppermute | solution.py:422
  41.5 0.0 collective-permute-done.5.x_in.refs_5_
  41.5 0.0 copy-start.4
  41.5 0.2 shard_map.70
  41.7 0.0 copy-start.1
  41.8 0.0 copy-start.3
  41.8 2.3 %collective-permute-start.9 = (f32[6,64,128]{2,1,0:T(8,128)S(1)}, f32[6,64,128]{2,1,0:T(8,128)S(1)}, u32[]{:S(2)}, u32[]{:S(2)}) collective-permute-start(f32[6,64,128]{2,1,0:T(8,128)S(1)} %get-tuple-element.36.refs_3_.refs_10_.refs_7_), channel_id=1, source_target_pairs={{0,16},{16,0},{32,48},{48,32},{64,80},{80,64},{96,112},{112,96},{1... | collective-permute-start | bytes 589832 | tf_op jit(solution)/shard_map/ppermute | solution.py:422
  44.0 2.4 %collective-permute-start.11 = (f32[6,64,128]{2,1,0:T(8,128)S(1)}, f32[6,64,128]{2,1,0:T(8,128)S(1)}, u32[]{:S(2)}, u32[]{:S(2)}) collective-permute-start(f32[6,64,128]{2,1,0:T(8,128)S(1)} %get-tuple-element.38.refs_5_.refs_12_.refs_9_), channel_id=1, source_target_pairs={{0,112},{16,32},{32,16},{48,64},{64,48},{80,96},{96,80},{112,0},{1... | collective-permute-start | bytes 589832 | tf_op jit(solution)/shard_map/ppermute | solution.py:425
  46.4 3.4 %shard_map.71 = (f32[64,128]{1,0:T(8,128)S(1)}, f32[64,128]{1,0:T(8,128)S(1)}) custom-call(f32[9,4,64,128]{3,2,1,0:T(8,128)S(1)} %get-tuple-element.29.part.refs_0_.refs_7_, f32[6,4,64,128]{3,2,1,0:T(8,128)S(1)} %get-tuple-element.30.part.refs_1_.refs_8_, f32[9,64,128]{2,1,0:T(8,128)S(1)} %get-tuple-element.33.refs_2_.refs_9_.refs_6_, ...), custom_call_target="tpu_custom_call" | custom-call | flops 1000000 | bytes 4000000 | tf_op jit(solution)/shard_map/pallas_call | solution.py:25
  49.8 2.9 %collective-permute-start.6 = (f32[64,128]{1,0:T(8,128)S(1)}, f32[64,128]{1,0:T(8,128)S(1)}, u32[]{:S(2)}, u32[]{:S(2)}) collective-permute-start(f32[64,128]{1,0:T(8,128)S(1)} %get-tuple-element.39), channel_id=1, source_target_pairs={{0,1},{1,0},{2,3},{3,2},{4,5},{5,4},{6,7},{7,6},{8,9},{9,8},{10,11... | collective-permute-start | bytes 98312 | tf_op jit(solution)/shard_map/ppermute | solution.py:422
  52.8 0.9 collective-permute-done.6.refs_5_
  53.6 1.2 %collective-permute-start.7 = (f32[64,128]{1,0:T(8,128)S(1)}, f32[64,128]{1,0:T(8,128)S(1)}, u32[]{:S(2)}, u32[]{:S(2)}) collective-permute-start(f32[64,128]{1,0:T(8,128)S(1)} %get-tuple-element.40), channel_id=1, source_target_pairs={{0,15},{1,2},{2,1},{3,4},{4,3},{5,6},{6,5},{7,8},{8,7},{9,10},{10,... | collective-permute-start | bytes 98312 | tf_op jit(solution)/shard_map/ppermute | solution.py:425
  54.8 2.5 %collective-permute-done.7.refs_6_ = f32[64,128]{1,0:T(8,128)S(1)} collective-permute-done((f32[64,128]{1,0:T(8,128)S(1)}, f32[64,128]{1,0:T(8,128)S(1)}, u32[]{:S(2)}, u32[]{:S(2)}) %collective-permute-start.7) | collective-permute-done | bytes 32800 | tf_op jit(solution)/shard_map/ppermute | solution.py:425
  57.3 0.0 copy-done.4
  57.3 0.0 copy-done.1
  57.3 0.0 copy-done.3
  57.3 6.5 %shard_map.72 = (f32[15,4,64,128]{3,2,1,0:T(8,128)S(1)}, f32[20,8,128]{2,1,0:T(8,128)S(1)}) custom-call(f32[15,4,64,128]{3,2,1,0:T(8,128)S(1)} %bitcast.8, f32[6,4,64,128]{3,2,1,0:T(8,128)S(1)} %bitcast.14, f32[3,4,64,128]{3,2,1,0:T(8,128)S(1)} %copy-done.4, f32[64,128]{1,0:T(8,128)S(1)} %collective-permute-done.inner.refs_3_, ...), custom_call_target="tpu_custom_call" | custom-call | flops 10000000 | bytes 4000000 | tf_op jit(solution)/shard_map/pallas_call | solution.py:25
  63.8 0.0 collective-permute-done.9.refs_11_
  63.8 0.0 collective-permute-done.11.refs_13_
  63.8 0.0 collective-permute-done.8.refs_10_
  63.8 0.0 collective-permute-done.10.refs_12_
  63.8 0.8 shard_map.73
  64.6 21.3 %all_to_all.5.gathered = f32[128,1,128]{2,1,0:T(1,128)S(1)} all-to-all(f32[128,1,128]{2,1,0:T(1,128)S(1)} %get-tuple-element.45), channel_id=1, replica_groups=mesh['gx'=8,'gy'=16] {'gx','gy'}, dimensions={0} | all-to-all | bytes 131072 | tf_op jit(solution)/shard_map/all_to_all | solution.py:477
  85.9 2.1 %shard_map.74 = (f32[15,4,64,128]{3,2,1,0:T(8,128)}, f32[4,4]{1,0:T(4,128)}, f32[4]{0:T(128)}, f32[5]{0:T(128)}) custom-call(f32[15,4,64,128]{3,2,1,0:T(8,128)S(1)} %get-tuple-element.41.refs_0_.part, f32[15,64,128]{2,1,0:T(8,128)S(1)} %get-tuple-element.43.z_faces, f32[15,64,128]{2,1,0:T(8,128)S(1)} %get-tuple-element.44.x_faces, ...), custom_call_target="tpu_custom_call" | custom-call | flops 1000000 | bytes 4000000 | tf_op jit(solution)/shard_map/pallas_call | solution.py:25
Async XLA Ops:
  0.6 1.5 %copy-start = (f32[5,3,4,64,128]{4,3,2,1,0:T(8,128)S(1)}, f32[5,3,4,64,128]{4,3,2,1,0:T(8,128)}, u32[]{:S(2)}) copy-start(f32[5,3,4,64,128]{4,3,2,1,0:T(8,128)} %param.3) | copy-start | bytes 5898244
  2.2 1.1 %copy-start.2 = (f32[2,3,4,64,128]{4,3,2,1,0:T(8,128)S(1)}, f32[2,3,4,64,128]{4,3,2,1,0:T(8,128)}, u32[]{:S(2)}) copy-start(f32[2,3,4,64,128]{4,3,2,1,0:T(8,128)} %param.4) | copy-start | bytes 2359300
  3.4 26.5 %collective-permute-start.2 = (f32[12,64,128]{2,1,0:T(8,128)S(1)}, f32[12,64,128]{2,1,0:T(8,128)S(1)}, u32[]{:S(2)}, u32[]{:S(2)}) collective-permute-start(f32[12,64,128]{2,1,0:T(8,128)S(1)} %get-tuple-element.31), channel_id=1, source_target_pairs={{0,16},{16,0},{32,48},{48,32},{64,80},{80,64},{96,112},{112,96},{1... | collective-permute-start | bytes 1179656 | tf_op jit(solution)/shard_map/ppermute | solution.py:422
  6.0 23.9 %collective-permute-start.3 = (f32[12,64,128]{2,1,0:T(8,128)S(1)}, f32[12,64,128]{2,1,0:T(8,128)S(1)}, u32[]{:S(2)}, u32[]{:S(2)}) collective-permute-start(f32[12,64,128]{2,1,0:T(8,128)S(1)} %get-tuple-element.32), channel_id=1, source_target_pairs={{0,112},{16,32},{32,16},{48,64},{64,48},{80,96},{96,80},{112,0},{1... | collective-permute-start | bytes 1179656 | tf_op jit(solution)/shard_map/ppermute | solution.py:425
  8.2 33.3 %collective-permute-start.4 = (f32[9,64,128]{2,1,0:T(8,128)S(1)}, f32[9,64,128]{2,1,0:T(8,128)S(1)}, u32[]{:S(2)}, u32[]{:S(2)}) collective-permute-start(f32[9,64,128]{2,1,0:T(8,128)S(1)} %get-tuple-element.34), channel_id=1, source_target_pairs={{0,16},{16,0},{32,48},{48,32},{64,80},{80,64},{96,112},{112,96},{1... | collective-permute-start | bytes 884744 | tf_op jit(solution)/shard_map/ppermute | solution.py:422
  8.3 33.2 %collective-permute-start.5 = (f32[9,64,128]{2,1,0:T(8,128)S(1)}, f32[9,64,128]{2,1,0:T(8,128)S(1)}, u32[]{:S(2)}, u32[]{:S(2)}) collective-permute-start(f32[9,64,128]{2,1,0:T(8,128)S(1)} %get-tuple-element.35), channel_id=1, source_target_pairs={{0,112},{16,32},{32,16},{48,64},{64,48},{80,96},{96,80},{112,0},{1... | collective-permute-start | bytes 884744 | tf_op jit(solution)/shard_map/ppermute | solution.py:425
  13.6 2.5 %collective-permute-start = (f32[64,128]{1,0:T(8,128)S(1)}, f32[64,128]{1,0:T(8,128)S(1)}, u32[]{:S(2)}, u32[]{:S(2)}) collective-permute-start(f32[64,128]{1,0:T(8,128)S(1)} %get-tuple-element.27), channel_id=1, source_target_pairs={{0,1},{1,0},{2,3},{3,2},{4,5},{5,4},{6,7},{7,6},{8,9},{9,8},{10,11... | collective-permute-start | bytes 98312 | tf_op jit(solution)/shard_map/ppermute | solution.py:422
  16.1 3.6 %collective-permute-start.1 = (f32[64,128]{1,0:T(8,128)S(1)}, f32[64,128]{1,0:T(8,128)S(1)}, u32[]{:S(2)}, u32[]{:S(2)}) collective-permute-start(f32[64,128]{1,0:T(8,128)S(1)} %get-tuple-element.28), channel_id=1, source_target_pairs={{0,15},{1,2},{2,1},{3,4},{4,3},{5,6},{6,5},{7,8},{8,7},{9,10},{10,... | collective-permute-start | bytes 98312 | tf_op jit(solution)/shard_map/ppermute | solution.py:425
  30.2 33.7 %collective-permute-start.8 = (f32[9,64,128]{2,1,0:T(8,128)S(1)}, f32[9,64,128]{2,1,0:T(8,128)S(1)}, u32[]{:S(2)}, u32[]{:S(2)}) collective-permute-start(f32[9,64,128]{2,1,0:T(8,128)S(1)} %get-tuple-element.33.refs_2_.refs_9_.refs_6_), channel_id=1, source_target_pairs={{0,16},{16,0},{32,48},{48,32},{64,80},{80,64},{96,112},{112,96},{1... | collective-permute-start | bytes 884744 | tf_op jit(solution)/shard_map/ppermute | solution.py:422
  31.4 32.4 %collective-permute-start.10 = (f32[9,64,128]{2,1,0:T(8,128)S(1)}, f32[9,64,128]{2,1,0:T(8,128)S(1)}, u32[]{:S(2)}, u32[]{:S(2)}) collective-permute-start(f32[9,64,128]{2,1,0:T(8,128)S(1)} %get-tuple-element.37.refs_4_.refs_11_.refs_8_), channel_id=1, source_target_pairs={{0,112},{16,32},{32,16},{48,64},{64,48},{80,96},{96,80},{112,0},{1... | collective-permute-start | bytes 884744 | tf_op jit(solution)/shard_map/ppermute | solution.py:425
  41.5 15.8 %copy-start.4 = (f32[3,4,64,128]{3,2,1,0:T(8,128)S(1)}, f32[3,4,64,128]{3,2,1,0:T(8,128)}, u32[]{:S(2)}) copy-start(f32[3,4,64,128]{3,2,1,0:T(8,128)} %refs_2_.3) | copy-start | bytes 1179652
  41.7 15.5 %copy-start.1 = (f32[5,3,4,64,128]{4,3,2,1,0:T(8,128)S(1)}, f32[5,3,4,64,128]{4,3,2,1,0:T(8,128)}, u32[]{:S(2)}) copy-start(f32[5,3,4,64,128]{4,3,2,1,0:T(8,128)} %param.3) | copy-start | bytes 5898244
  41.8 15.5 %copy-start.3 = (f32[2,3,4,64,128]{4,3,2,1,0:T(8,128)S(1)}, f32[2,3,4,64,128]{4,3,2,1,0:T(8,128)}, u32[]{:S(2)}) copy-start(f32[2,3,4,64,128]{4,3,2,1,0:T(8,128)} %param.4) | copy-start | bytes 2359300
  41.8 22.0 %collective-permute-start.9 = (f32[6,64,128]{2,1,0:T(8,128)S(1)}, f32[6,64,128]{2,1,0:T(8,128)S(1)}, u32[]{:S(2)}, u32[]{:S(2)}) collective-permute-start(f32[6,64,128]{2,1,0:T(8,128)S(1)} %get-tuple-element.36.refs_3_.refs_10_.refs_7_), channel_id=1, source_target_pairs={{0,16},{16,0},{32,48},{48,32},{64,80},{80,64},{96,112},{112,96},{1... | collective-permute-start | bytes 589832 | tf_op jit(solution)/shard_map/ppermute | solution.py:422
  44.0 19.8 %collective-permute-start.11 = (f32[6,64,128]{2,1,0:T(8,128)S(1)}, f32[6,64,128]{2,1,0:T(8,128)S(1)}, u32[]{:S(2)}, u32[]{:S(2)}) collective-permute-start(f32[6,64,128]{2,1,0:T(8,128)S(1)} %get-tuple-element.38.refs_5_.refs_12_.refs_9_), channel_id=1, source_target_pairs={{0,112},{16,32},{32,16},{48,64},{64,48},{80,96},{96,80},{112,0},{1... | collective-permute-start | bytes 589832 | tf_op jit(solution)/shard_map/ppermute | solution.py:425
  49.8 3.8 %collective-permute-start.6 = (f32[64,128]{1,0:T(8,128)S(1)}, f32[64,128]{1,0:T(8,128)S(1)}, u32[]{:S(2)}, u32[]{:S(2)}) collective-permute-start(f32[64,128]{1,0:T(8,128)S(1)} %get-tuple-element.39), channel_id=1, source_target_pairs={{0,1},{1,0},{2,3},{3,2},{4,5},{5,4},{6,7},{7,6},{8,9},{9,8},{10,11... | collective-permute-start | bytes 98312 | tf_op jit(solution)/shard_map/ppermute | solution.py:422
  53.6 3.6 %collective-permute-start.7 = (f32[64,128]{1,0:T(8,128)S(1)}, f32[64,128]{1,0:T(8,128)S(1)}, u32[]{:S(2)}, u32[]{:S(2)}) collective-permute-start(f32[64,128]{1,0:T(8,128)S(1)} %get-tuple-element.40), channel_id=1, source_target_pairs={{0,15},{1,2},{2,1},{3,4},{4,3},{5,6},{6,5},{7,8},{8,7},{9,10},{10,... | collective-permute-start | bytes 98312 | tf_op jit(solution)/shard_map/ppermute | solution.py:425

commit v2 on v1

v2 whole, which is shorter than its diff:
```python
import functools

import jax
import jax.numpy as jnp
from jax import lax
from jax.experimental import pallas as pl
from jax.experimental.pallas import tpu as pltpu
from jax.sharding import PartitionSpec as P

time_step = 0.2
viscosity = 0.05

groups = ((0, 1, 2), (3, 4))

f32 = jnp.float32
vmem = pl.BlockSpec(memory_space=pltpu.VMEM)
tile = (8, 128)


def shaped(*dims):
    return jax.ShapeDtypeStruct(dims, f32)


def call(body, outs, args, scratch=(), flops=1000000, limit=24):
    return pl.pallas_call(
        body,
        out_shape=outs,
        in_specs=[vmem] * len(args),
        out_specs=jax.tree.map(lambda _: vmem, outs),
        scratch_shapes=list(scratch),
        compiler_params=pltpu.CompilerParams(vmem_limit_bytes=limit << 20),
        cost_estimate=pl.CostEstimate(flops=flops, bytes_accessed=4000000, transcendentals=0),
    )(*args)


def lanes():
    return lax.broadcasted_iota(jnp.int32, tile, 1)


def rows_of(zt):
    return pl.ds(pl.multiple_of(zt * 8, 8), 8)


def sides():
    even = lax.rem(lax.axis_index("gx"), 2) == 0
    z_plane = jnp.where(even, 3, 0)
    z_sign = jnp.where(even, f32(-1), f32(1))
    return ((z_plane, z_sign), (3 - z_plane, -z_sign))


def gy_even():
    return lax.rem(lax.axis_index("gy"), 2) == 0


def faces_kernel(t, u, *refs):
    outs, sem = refs[:-1], refs[-1]
    (z_plane, _), (x_plane, _) = sides()
    last = len(groups) - 1
    copies = []
    for g, members in enumerate(groups):
        sources = [(t, 3 * members[0], 3 * len(members))]
        sources += [(u, 0, 3)] if g == 0 else []
        sources += [(u, 3, 3)] if g == last else []
        for side, plane in ((0, z_plane), (1, x_plane)):
            at = 0
            for ref, start, count in sources:
                copies.append(
                    pltpu.make_async_copy(
                        ref.at[pl.ds(start, count), plane],
                        outs[2 * g + side].at[pl.ds(at, count)],
                        sem.at[len(copies)],
                    )
                )
                at += count
    for copy in copies:
        copy.start()
    for copy in copies:
        copy.wait()


def pack_tile(load, fields, x, packed, even_lane, plane_lane):
    own = jnp.zeros(tile, f32)
    for f in fields:
        own = jnp.where(even_lane == 2 * f, pltpu.roll(load(f), 2 * f + 1, axis=1), own)
    return jnp.where(plane_lane == x, pltpu.roll(own, 32 * x, axis=1), packed)


def lane_parts():
    lane = lanes()
    return lane & -2, lane >> 5


def pack_first_kernel(t, u, out):
    parts = lane_parts()

    def at_rows(zt, carry):
        rows = rows_of(zt)
        tangent = flow = jnp.zeros(tile, f32)
        for x in range(4):
            tangent = pack_tile(lambda f: t[f, x, rows], range(15), x, tangent, *parts)
            flow = pack_tile(lambda f: u[f, x, rows], range(6), x, flow, *parts)
        out[0, rows] = tangent
        out[1, rows] = flow
        return carry

    lax.fori_loop(0, 8, at_rows, 0)


class PackedLanes:
    def __init__(self):
        lane = lanes()
        field = (lane & 31) >> 1
        tangent = sum(jnp.where(field >= 3 * k, 1, 0) for k in range(1, 5))
        self.high = (lane & 1) == 0
        self.sign = jnp.where(self.high, f32(-1), f32(1))
        self.tangent = tangent
        self.component = field - 3 * tangent
        self.even = gy_even()

    def from_neighbours(self, inner, outer):
        high = jnp.where(self.even, inner, outer)
        low = jnp.where(self.even, outer, inner)
        return jnp.where(self.high, pltpu.roll(high, 127, axis=1), pltpu.roll(low, 1, axis=1))

    def spread_flow(self, flow, at):
        out = None
        for k in range(5):
            turn = (6 * k - 2 * at) % 128
            moved = pltpu.roll(flow, turn, axis=1) if turn else flow
            out = moved if out is None else jnp.where(self.tangent == k, moved, out)
        return out

    def of_component(self, packed, component):
        out = packed
        for i in range(3):
            if i != component:
                out = jnp.where(self.component == i, pltpu.roll(packed, (2 * (i - component)) % 128, axis=1), out)
        return out

    def column_terms(self, scale, tangent, flow, halo, halo_flow, flow_at):
        flag = jnp.where(self.tangent == 4, f32(scale), f32(0))
        speed = self.of_component(self.spread_flow(flow, flow_at), 1)
        weight = scale * viscosity + (0.5 * scale) * self.sign * speed
        made = (0.5 * scale) * self.sign * self.of_component(tangent, 1) + flag
        return weight * halo + made * self.spread_flow(halo_flow, flow_at)


def edge_part(terms, f, edges):
    return jnp.where(edges, pltpu.roll(terms, (127 - 2 * f) % 128, axis=1), 0.0)


def at_edges():
    lane = lanes()
    return (lane == 0) | (lane == 127)


def fill_padding(padded, count):
    for f in range(count):
        padded[f, 0] = jnp.zeros((80, 128), f32)
        padded[f, 5] = jnp.zeros((80, 128), f32)

        def at_plane(x, carry):
            padded[f, x, 0:8] = jnp.zeros(tile, f32)
            padded[f, x, 72:80] = jnp.zeros(tile, f32)
            return carry

        lax.fori_loop(1, 5, at_plane, 0)


def section(padded, members, scale, base, extra, store):
    lane = lanes()
    not_low = jnp.where(lane == 0, f32(0), f32(1))
    not_high = jnp.where(lane == 127, f32(0), f32(1))
    flow_at = 3 * len(members)

    def at_plane(x, carry):
        for zt in range(8):
            first_row = 8 + 8 * zt
            rows = slice(8 * zt, 8 * zt + 8)

            def stencil(f):
                def load(dx, dz):
                    return padded[f, x + 1 + dx, first_row + dz : first_row + dz + 8]

                centre = load(0, 0)
                up, down = pltpu.roll(centre, 127, axis=1), pltpu.roll(centre, 1, axis=1)
                return centre, load(1, 0), load(-1, 0), up, down, load(0, 1), load(0, -1)

            speed, made, bulk = [], [], []
            for i in range(3):
                flow = list(stencil(flow_at + i))
                flow[3], flow[4] = flow[3] * not_high, flow[4] * not_low
                speed.append(flow[0])
                made.append([(-0.5 * scale) * (flow[1 + 2 * j] - flow[2 + 2 * j]) for j in range(3)])
                if 4 in members:
                    total = flow[1] + flow[2] + flow[3] + flow[4] + flow[5] + flow[6]
                    bulk.append(scale * (total - 6.0 * flow[0]))
            halves = [(0.5 * scale) * u for u in speed]
            ahead = [scale * viscosity - h for h in halves]
            behind = [scale * viscosity + h for h in halves]
            ahead[1], behind[1] = ahead[1] * not_high, behind[1] * not_low
            for n, k in enumerate(members):
                around = [stencil(3 * n + i) for i in range(3)]
                for i in range(3):
                    own = around[i]
                    value = (base - 6.0 * viscosity * scale) * own[0]
                    for j in range(3):
                        value += ahead[j] * own[1 + 2 * j] + behind[j] * own[2 + 2 * j]
                        value += made[i][j] * around[j][0]
                    if k == 4:
                        value += bulk[i]
                    if extra is not None:
                        value += 0.5 * extra[3 * k + i, x, rows]
                    store(3 * n + i, x, rows, value)
        return carry

    lax.fori_loop(0, 4, at_plane, 0)


def first_kernel(t, u, columns, *rest):
    outs, padded = rest[:-1], rest[-1]
    fill_padding(padded, 18)

    def copy_plane(x, carry):
        for f in range(15):
            padded[f, x + 1, 8:72] = t[f, x]
        for i in range(3):
            padded[15 + i, x + 1, 8:72] = u[i, x]
        return carry

    lax.fori_loop(0, 4, copy_plane, 0)
    place = {k: (g, n) for g, members in enumerate(groups) for n, k in enumerate(members)}

    def store(f, x, rows, value):
        g, n = place[f // 3]
        outs[g][3 * n + f % 3, x, rows] = value

    section(padded, range(5), time_step, 1.0, None, store)


def halo_terms(scale, sign, speed, tangent):
    weight = scale * viscosity + (0.5 * scale) * sign * speed
    return weight, [(0.5 * scale) * sign * v + (scale if k == 4 else 0.0) for k, v in tangent]


def first_terms_kernel(columns, inner, outer, terms):
    layout = PackedLanes()
    for zt in range(8):
        rows = slice(8 * zt, 8 * zt + 8)
        halo = [layout.from_neighbours(inner[n, rows], outer[n, rows]) for n in range(2)]
        turned = layout.column_terms(time_step, columns[0, rows], columns[1, rows], halo[0], halo[1], 0)
        for x in range(4):
            terms[x, rows] = pltpu.roll(turned, 128 - 32 * x, axis=1) if x else turned


def first_faces_kernel(g, part, terms, t, u, z_in, x_in, z_flow, x_flow, z_out, x_out):
    members = groups[g]
    flow_at = 3 * len(groups[0])
    edges = at_edges()
    for (plane, sign), got, flow_got, out in zip(sides(), (z_in, x_in), (z_flow, x_flow), (z_out, x_out)):
        for zt in range(8):
            rows = slice(8 * zt, 8 * zt + 8)
            here = terms[plane, rows]
            flow_halo = [flow_got[flow_at + i, rows] for i in range(3)]
            tangent = [(k, t[3 * k, plane, rows]) for k in members]
            weight, made = halo_terms(time_step, sign, u[0, plane, rows], tangent)
            for n, k in enumerate(members):
                for i in range(3):
                    j = 3 * n + i
                    value = part[j, plane, rows] + edge_part(here, 3 * k + i, edges)
                    out[j, rows] = value + weight * got[j, rows] + made[n] * flow_halo[i]


def first_whole_kernel(g, part, terms, z_face, x_face, *refs):
    whole, packed = refs[-2:]
    fields = [3 * k + i for k in groups[g] for i in range(3)]
    edges = at_edges()
    lane_facts = lane_parts()
    (z_plane, _), (x_plane, _) = sides()

    def at_rows(zt, carry):
        rows = rows_of(zt)
        total = jnp.zeros(tile, f32)
        for x in (1, 2):
            values = {}
            for j, f in enumerate(fields):
                values[f] = part[j, x, rows] + edge_part(terms[x, rows], f, edges)
                whole[j, x, rows] = values[f]
            total = pack_tile(lambda f: values[f], fields, x, total, *lane_facts)
        for plane, face in ((z_plane, z_face), (x_plane, x_face)):
            values = {}
            for j, f in enumerate(fields):
                values[f] = face[j, rows]
                whole[j, plane, rows] = values[f]
            total = pack_tile(lambda f: values[f], fields, plane, total, *lane_facts)
        packed[rows] = total + refs[0][rows] if g else total
        return carry

    lax.fori_loop(0, 8, at_rows, 0, unroll=2)


def split_refs(refs, *counts):
    pieces, at = [], 0
    for count in counts:
        pieces.append(refs[at : at + count])
        at += count
    pieces.append(refs[at:])
    return pieces


def second_kernel(g, t, u, first, out, padded):
    members = groups[g]
    count = 3 * len(members)
    fill_padding(padded, count + 3)

    def copy_plane(x, carry):
        for j in range(count):
            padded[j, x + 1, 8:72] = first[j, x]
        for i in range(3):
            padded[count + i, x + 1, 8:72] = u[3 + i, x]
        return carry

    lax.fori_loop(0, 4, copy_plane, 0)

    def store(j, x, rows, value):
        out[j, x, rows] = value

    section(padded, members, 0.5 * time_step, 0.5, t, store)


pairs = [(a, b) for a in range(5) for b in range(a, 5)]


def add_products(sums, rows_now, weighted):
    products = [sums[n] + rows_now[a] * rows_now[b] for n, (a, b) in enumerate(pairs)]
    return products + [sums[15 + k] + weighted[k] for k in range(5)]


def second_terms_kernel(packed, columns, inner_flow, outer_flow, inner, outer, terms):
    layout = PackedLanes()
    for zt in range(8):
        rows = slice(8 * zt, 8 * zt + 8)
        halo = layout.from_neighbours(inner[rows], outer[rows])
        halo_flow = layout.from_neighbours(inner_flow[1, rows], outer_flow[1, rows])
        turned = layout.column_terms(0.5 * time_step, packed[rows], columns[1, rows], halo, halo_flow, 3)
        for x in range(4):
            terms[x, rows] = pltpu.roll(turned, 128 - 32 * x, axis=1) if x else turned


def places():
    return {k: (g, 3 * n) for g, members in enumerate(groups) for n, k in enumerate(members)}


def second_inside_kernel(terms, weight, *refs):
    parts, first, (out, sums_out) = split_refs(refs, len(groups), len(groups))
    edges = at_edges()
    place = places()
    sums = [jnp.zeros(tile, f32)] * 20
    for x in (1, 2):

        def at_rows(zt, sums):
            rows = rows_of(zt)
            here = terms[x, rows]
            for i in range(3):
                now, weighted = [], []
                scaled = weight[i, x, rows]
                for k in range(5):
                    g, j = place[k][0], place[k][1] + i
                    value = parts[g][j, x, rows] + edge_part(here, 3 * k + i, edges)
                    out[3 * k + i, x - 1, rows] = value
                    now.append(value)
                    weighted.append(scaled * (first[g][j, x, rows] + value))
                sums = add_products(sums, now, weighted)
            return sums

        sums = lax.fori_loop(0, 8, at_rows, sums, unroll=4)
    for n in range(20):
        sums_out[n] = sums[n]


def second_outer_kernel(u, weight, terms, sums_in, z_flow, x_flow, *refs):
    count = len(groups)
    parts, first, z_in, x_in, (z_out, x_out, sums_out) = split_refs(refs, count, count, count, count)
    last = len(groups) - 1
    flow_at = 3 * len(groups[last]) + (3 if last == 0 else 0)
    scale = 0.5 * time_step
    edges = at_edges()
    place = places()
    sums = [sums_in[n] for n in range(20)]
    for (plane, sign), got, flow_got, out in zip(sides(), (z_in, x_in), (z_flow, x_flow), (z_out, x_out)):

        def at_rows(zt, sums):
            rows = rows_of(zt)
            here = terms[plane, rows]
            flow_halo = [flow_got[flow_at + i, rows] for i in range(3)]
            tangent = [(k, first[place[k][0]][place[k][1], plane, rows]) for k in range(5)]
            outer_weight, made = halo_terms(scale, sign, u[3, plane, rows], tangent)
            for i in range(3):
                now, weighted = [], []
                scaled = weight[i, plane, rows]
                for k in range(5):
                    g, j = place[k][0], place[k][1] + i
                    value = parts[g][j, plane, rows] + edge_part(here, 3 * k + i, edges)
                    value += outer_weight * got[g][j, rows] + made[k] * flow_halo[i]
                    out[3 * k + i, rows] = value
                    now.append(value)
                    weighted.append(scaled * (first[g][j, plane, rows] + value))
                sums = add_products(sums, now, weighted)
            return sums

        sums = lax.fori_loop(0, 8, at_rows, sums, unroll=4)
    stacked = jnp.concatenate([jnp.sum(s, axis=0, keepdims=True) for s in sums] + [jnp.zeros((4, 128), f32)], 0)
    totals = jnp.broadcast_to(jnp.sum(stacked, axis=1, keepdims=True), (24, 128))
    diagonal = lax.broadcasted_iota(jnp.int32, (24, 128), 0) == lax.broadcasted_iota(jnp.int32, (24, 128), 1)
    line = jnp.sum(jnp.where(diagonal, totals, 0.0), axis=0, keepdims=True)
    sums_out[...] = jnp.broadcast_to(line[None], sums_out.shape)


def renorm_kernel(total_cells, inside, z_face, x_face, gathered, out, r_out, c_out, o_out):
    line = jnp.sum(gathered[...], axis=0)
    spread = [jnp.broadcast_to(line[:, n : n + 1], tile) for n in range(20)]
    gram = {pair: spread[n] * f32(1.0 / (3.0 * total_cells)) for n, pair in enumerate(pairs)}
    lower = {}
    for c in range(4):
        value = gram[(c, c)]
        for m in range(c):
            value = value - lower[(c, m)] * lower[(c, m)]
        lower[(c, c)] = jnp.sqrt(value)
        for r in range(c + 1, 4):
            value = gram[(c, r)]
            for m in range(c):
                value = value - lower[(r, m)] * lower[(c, m)]
            lower[(r, c)] = value / lower[(c, c)]
    inverse = {}
    for r in range(4):
        for c in range(r + 1):
            value = jnp.ones(tile, f32) if r == c else jnp.zeros(tile, f32)
            for m in range(c, r):
                value = value - lower[(r, m)] * inverse[(m, c)]
            inverse[(r, c)] = value / lower[(r, r)]
    coefficient = []
    for r in range(4):
        value = inverse[(r, 0)] * gram[(0, 4)]
        for c in range(1, r + 1):
            value = value + inverse[(r, c)] * gram[(c, 4)]
        coefficient.append(value)

    row, lane = lax.broadcasted_iota(jnp.int32, tile, 0), lanes()
    factor, coefficients, objective = (jnp.zeros(tile, f32) for _ in range(3))
    for r in range(4):
        for c in range(r + 1):
            factor = jnp.where((row == c) & (lane == r), lower[(r, c)], factor)
        coefficients = jnp.where(lane == r, coefficient[r], coefficients)
    for k in range(5):
        objective = jnp.where(lane == k, spread[15 + k] * f32(0.5 / total_cells), objective)
    r_out[...] = factor[:4, :4]
    c_out[...] = coefficients[0, :4]
    o_out[...] = objective[0, :5]

    (z_plane, _), (x_plane, _) = sides()
    for plane, load in (
        (1, lambda f, rows: inside[f, 0, rows]),
        (2, lambda f, rows: inside[f, 1, rows]),
        (z_plane, lambda f, rows: z_face[f, rows]),
        (x_plane, lambda f, rows: x_face[f, rows]),
    ):

        def at_rows(zt, carry):
            rows = rows_of(zt)
            for i in range(3):
                now = [load(3 * k + i, rows) for k in range(5)]
                last = now[4]
                for r in range(4):
                    value = inverse[(r, 0)] * now[0]
                    for c in range(1, r + 1):
                        value = value + inverse[(r, c)] * now[c]
                    out[3 * r + i, plane, rows] = value
                    last = last - coefficient[r] * value
                out[12 + i, plane, rows] = last
            return carry

        lax.fori_loop(0, 8, at_rows, 0)


def per_device(tangents, base_flow, objective_weight):
    count_x, count_y = lax.axis_size("gx"), lax.axis_size("gy")
    total_cells = 4 * 64 * 128 * count_x * count_y
    t = tangents.reshape(15, 4, 64, 128)
    u = base_flow.reshape(6, 4, 64, 128)
    last = len(groups) - 1

    def partner(values, axis, count):
        return lax.ppermute(values, axis, [(i, i ^ 1) for i in range(count)])

    def beyond(values, axis, count):
        return lax.ppermute(values, axis, [(i, (i + 2 * (i % 2) - 1) % count) for i in range(count)])

    def after(values, other):
        return lax.optimization_barrier((values, other))[0]

    sizes = [3 * len(members) for members in groups]
    sent = [s + (3 if g == 0 else 0) + (3 if g == last else 0) for g, s in enumerate(sizes)]
    faces = pl.pallas_call(
        faces_kernel,
        out_shape=tuple(shaped(s, 64, 128) for s in sent for _ in range(2)),
        in_specs=[pl.BlockSpec(memory_space=pltpu.HBM)] * 2,
        out_specs=(vmem,) * (2 * len(groups)),
        scratch_shapes=[pltpu.SemaphoreType.DMA((2 * len(groups) + 4,))],
        compiler_params=pltpu.CompilerParams(vmem_limit_bytes=8 << 20),
    )(t, u)
    z_in = [partner(faces[0], "gx", count_x)]
    x_in = [beyond(faces[1], "gx", count_x)]
    columns = call(pack_first_kernel, shaped(2, 64, 128), (t, u))
    inner_in = partner(columns, "gy", count_y)
    outer_in = beyond(after(columns, inner_in), "gy", count_y)
    parts = call(
        first_kernel,
        tuple(shaped(s, 4, 64, 128) for s in sizes),
        (t, u, columns),
        scratch=[pltpu.VMEM((18, 6, 80, 128), f32)],
        flops=10000000,
    )
    for g in range(1, len(groups)):
        z_in.append(partner(after(faces[2 * g], outer_in), "gx", count_x))
        x_in.append(beyond(after(faces[2 * g + 1], outer_in), "gx", count_x))
    terms = call(first_terms_kernel, shaped(4, 64, 128), (columns, inner_in, outer_in))
    first, halves, z_next, x_next = [], [], [], []
    packed = ()
    for g in range(len(groups)):
        if g:
            z_in[g] = after(z_in[g], halves[-1])
        z_face, x_face = call(
            functools.partial(first_faces_kernel, g),
            (shaped(sizes[g], 64, 128), shaped(sizes[g], 64, 128)),
            (parts[g], terms, t, u, z_in[g], x_in[g], z_in[0], x_in[0]),
        )
        z_next.append(partner(z_face, "gx", count_x))
        x_next.append(beyond(x_face, "gx", count_x))
        whole, *packed = call(
            functools.partial(first_whole_kernel, g),
            (shaped(sizes[g], 4, 64, 128), shaped(64, 128)),
            (parts[g], terms, z_face, x_face, *packed),
        )
        first.append(whole)
        halves.append(
            call(
                functools.partial(second_kernel, g),
                shaped(sizes[g], 4, 64, 128),
                (t, u, whole),
                scratch=[pltpu.VMEM((sizes[g] + 3, 6, 80, 128), f32)],
                flops=5000000,
            )
        )
    inner = partner(packed[0], "gy", count_y)
    outer = beyond(after(packed[0], inner), "gy", count_y)
    terms = call(second_terms_kernel, shaped(4, 64, 128), (packed[0], columns, inner_in, outer_in, inner, outer))
    inside, sums = call(
        second_inside_kernel,
        (shaped(15, 2, 64, 128), shaped(20, 8, 128)),
        (terms, objective_weight, *halves, *first),
    )
    z_face, x_face, line = call(
        second_outer_kernel,
        (shaped(15, 64, 128), shaped(15, 64, 128), shaped(count_x * count_y, 1, 128)),
        (u, objective_weight, terms, sums, z_in[last], x_in[last], *halves, *first, *z_next, *x_next),
    )
    gathered = lax.all_to_all(line, ("gx", "gy"), 0, 0, tiled=True)
    renormed, rfactor, coefficients, objective = call(
        functools.partial(renorm_kernel, total_cells),
        (shaped(15, 4, 64, 128), shaped(4, 4), shaped(4), shaped(5)),
        (inside, z_face, x_face, gathered),
    )
    return (renormed.reshape(tangents.shape), rfactor, coefficients, objective)


def solution(mesh):
    placed = (
        P(None, None, "gx", None, "gy"),
        P(None, None, "gx", None, "gy"),
        P(None, "gx", None, "gy"),
    )
    return jax.shard_map(
        per_device,
        mesh=mesh,
        in_specs=placed,
        out_specs=(P(None, None, "gx", None, "gy"), P(), P(), P()),
        check_vma=False,
    )
```

time: 88.2 us -> 81.9 us (0.929)
  Pallas kernels: 22.9 us -> 14.2 us
  waiting for transfers between devices: 18.3 us -> 22.1 us
  starting transfers between devices: 22.1 us -> 21.1 us
    pallas_call x9 -> x13, Pallas kernels: 22.9 us -> 13.9 us  [call(): pl.pallas_call(body, out_shape=outs, in_specs=[vmem] * len(args), out_spe...]
    ppermute x6, waiting for transfers between devices: 13.7 us -> 18.2 us  [partner(): return lax.ppermute(values, axis, [(i, i ^ 1) for i in range(count)])]
  transfers between devices with their start and end apart: 12 -> 12, of which waited for: 6 -> 7; matrix products, arithmetic and copies ran while one was open for 0% -> 0% of each run, Pallas kernels for 23% -> 13%
where the time goes in v2:
time: 81.9 us; the launch traced here: 81.7 us
  waiting for transfers between devices  22.1 us (27%)
  starting transfers between devices  21.1 us (26%)
  blocking collectives  20.8 us (25%)
  Pallas kernels  14.2 us (17%)
  local copies, waits for them, and re-layouts  2.68 us (3%)
    all_to_all x1, blocking collectives, per_device(): gathered = lax.all_to_all(line, ('gx', 'gy'), 0, 0, tiled=True)  20.8 us
    ppermute x6, waiting for transfers between devices, partner(): return lax.ppermute(values, axis, [(i, i ^ 1) for i in range(count)])  18.2 us
    pallas_call x13, Pallas kernels, call(): pl.pallas_call(body, out_shape=outs, in_specs=[vmem] * len(args), out_spe...  13.9 us
    ppermute x6, starting transfers between devices, beyond(): lax.ppermute(values, axis, [(i, (i + 2 * (i % 2) - 1) % count) for i in r...  10.7 us
    ppermute x6, starting transfers between devices, partner(): return lax.ppermute(values, axis, [(i, i ^ 1) for i in range(count)])  10.4 us
    ppermute x6, waiting for transfers between devices, beyond(): lax.ppermute(values, axis, [(i, (i + 2 * (i % 2) - 1) % count) for i in r...  3.91 us
    unnamed x10, local copies, waits for them, and re-layouts  2.68 us
  transfers between devices with their start and end apart: 12, of which 7 were waited for; matrix products, arithmetic and copies ran while one was open for 0% of the time, Pallas kernels for 13%

profile of v2, /device:TPU:1, one launch (start us, length us, event | category | flops | bytes accessed | tf_op | source)
XLA Modules:
  0.0 81.7 jit_solution(17649594582883321224)
XLA Ops:
  0.6 0.0 copy-start
  0.6 1.5 %copy-done = f32[5,3,4,64,128]{4,3,2,1,0:T(8,128)S(1)} copy-done((f32[5,3,4,64,128]{4,3,2,1,0:T(8,128)S(1)}, f32[5,3,4,64,128]{4,3,2,1,0:T(8,128)}, u32[]{:S(2)}) %copy-start) | copy-done | bytes 1966104
  2.2 0.0 copy-start.2
  2.2 1.1 %copy-done.2 = f32[2,3,4,64,128]{4,3,2,1,0:T(8,128)S(1)} copy-done((f32[2,3,4,64,128]{4,3,2,1,0:T(8,128)S(1)}, f32[2,3,4,64,128]{4,3,2,1,0:T(8,128)}, u32[]{:S(2)}) %copy-start.2) | copy-done | bytes 786456
  3.3 0.0 copy-start.1
  3.3 0.0 copy-start.3
  3.3 0.4 shard_map.69
  3.7 2.5 %collective-permute-start.3 = (f32[12,64,128]{2,1,0:T(8,128)S(1)}, f32[12,64,128]{2,1,0:T(8,128)S(1)}, u32[]{:S(2)}, u32[]{:S(2)}) collective-permute-start(f32[12,64,128]{2,1,0:T(8,128)S(1)} %get-tuple-element.37), channel_id=1, source_target_pairs={{0,16},{16,0},{32,48},{48,32},{64,80},{80,64},{96,112},{112,96},{1... | collective-permute-start | bytes 1179656 | tf_op jit(solution)/shard_map/ppermute | solution.py:493
  6.2 2.3 %collective-permute-start.4 = (f32[12,64,128]{2,1,0:T(8,128)S(1)}, f32[12,64,128]{2,1,0:T(8,128)S(1)}, u32[]{:S(2)}, u32[]{:S(2)}) collective-permute-start(f32[12,64,128]{2,1,0:T(8,128)S(1)} %get-tuple-element.38), channel_id=1, source_target_pairs={{0,112},{16,32},{32,16},{48,64},{64,48},{80,96},{96,80},{112,0},{1... | collective-permute-start | bytes 1179656 | tf_op jit(solution)/shard_map/ppermute | solution.py:496
  8.5 0.0 copy-done.1
  8.5 0.0 copy-done.3
  8.5 1.8 %shard_map.66.columns = f32[2,64,128]{2,1,0:T(8,128)S(1)} custom-call(f32[15,4,64,128]{3,2,1,0:T(8,128)S(1)} %bitcast.4, f32[6,4,64,128]{3,2,1,0:T(8,128)S(1)} %bitcast.11), custom_call_target="tpu_custom_call" | custom-call | flops 1000000 | bytes 4000000 | tf_op jit(solution)/shard_map/pallas_call | solution.py:25
  10.3 1.0 %collective-permute-start = (f32[2,64,128]{2,1,0:T(8,128)S(1)}, f32[2,64,128]{2,1,0:T(8,128)S(1)}, u32[]{:S(2)}, u32[]{:S(2)}) collective-permute-start(f32[2,64,128]{2,1,0:T(8,128)S(1)} %shard_map.66.columns), channel_id=1, source_target_pairs={{0,1},{1,0},{2,3},{3,2},{4,5},{5,4},{6,7},{7,6},{8,9},{9,8},{10,11... | collective-permute-start | bytes 196616 | tf_op jit(solution)/shard_map/ppermute | solution.py:493
  11.3 0.9 %collective-permute-done.inner.inner_flow = f32[2,64,128]{2,1,0:T(8,128)S(1)} collective-permute-done((f32[2,64,128]{2,1,0:T(8,128)S(1)}, f32[2,64,128]{2,1,0:T(8,128)S(1)}, u32[]{:S(2)}, u32[]{:S(2)}) %collective-permute-start) | collective-permute-done | bytes 65568 | tf_op jit(solution)/shard_map/ppermute | solution.py:493
  12.2 1.5 %collective-permute-start.1 = (f32[2,64,128]{2,1,0:T(8,128)S(1)}, f32[2,64,128]{2,1,0:T(8,128)S(1)}, u32[]{:S(2)}, u32[]{:S(2)}) collective-permute-start(f32[2,64,128]{2,1,0:T(8,128)S(1)} %shard_map.66.columns), channel_id=1, source_target_pairs={{0,15},{1,2},{2,1},{3,4},{4,3},{5,6},{6,5},{7,8},{8,7},{9,10},{10,... | collective-permute-start | bytes 196616 | tf_op jit(solution)/shard_map/ppermute | solution.py:496
  13.7 2.5 %collective-permute-done.1.outer.outer_flow = f32[2,64,128]{2,1,0:T(8,128)S(1)} collective-permute-done((f32[2,64,128]{2,1,0:T(8,128)S(1)}, f32[2,64,128]{2,1,0:T(8,128)S(1)}, u32[]{:S(2)}, u32[]{:S(2)}) %collective-permute-start.1) | collective-permute-done | bytes 65568 | tf_op jit(solution)/shard_map/ppermute | solution.py:496
  16.2 0.4 collective-permute-start.2
  16.6 1.4 %collective-permute-start.5 = (f32[9,64,128]{2,1,0:T(8,128)S(1)}, f32[9,64,128]{2,1,0:T(8,128)S(1)}, u32[]{:S(2)}, u32[]{:S(2)}) collective-permute-start(f32[9,64,128]{2,1,0:T(8,128)S(1)} %get-tuple-element.44), channel_id=1, source_target_pairs={{0,112},{16,32},{32,16},{48,64},{64,48},{80,96},{96,80},{112,0},{1... | collective-permute-start | bytes 884744 | tf_op jit(solution)/shard_map/ppermute | solution.py:496
  17.9 2.4 %shard_map.67 = (f32[9,4,64,128]{3,2,1,0:T(8,128)S(1)}, f32[6,4,64,128]{3,2,1,0:T(8,128)S(1)}) custom-call(f32[15,4,64,128]{3,2,1,0:T(8,128)S(1)} %bitcast.5, f32[6,4,64,128]{3,2,1,0:T(8,128)S(1)} %bitcast.12, f32[2,64,128]{2,1,0:T(8,128)S(1)} %shard_map.66.columns), custom_call_target="tpu_custom_call" | custom-call | flops 10000000 | bytes 4000000 | tf_op jit(solution)/shard_map/pallas_call | solution.py:25
  20.3 0.3 shard_map.68.terms
  20.6 9.9 %collective-permute-done.3.z_in.z_flow = f32[12,64,128]{2,1,0:T(8,128)S(1)} collective-permute-done((f32[12,64,128]{2,1,0:T(8,128)S(1)}, f32[12,64,128]{2,1,0:T(8,128)S(1)}, u32[]{:S(2)}, u32[]{:S(2)}) %collective-permute-start.3) | collective-permute-done | bytes 393248 | tf_op jit(solution)/shard_map/ppermute | solution.py:493
  30.5 0.0 collective-permute-done.4.x_in.x_flow
  30.5 0.2 shard_map.70
  30.8 1.3 %collective-permute-start.8 = (f32[9,64,128]{2,1,0:T(8,128)S(1)}, f32[9,64,128]{2,1,0:T(8,128)S(1)}, u32[]{:S(2)}, u32[]{:S(2)}) collective-permute-start(f32[9,64,128]{2,1,0:T(8,128)S(1)} %get-tuple-element.39.z_face), channel_id=1, source_target_pairs={{0,16},{16,0},{32,48},{48,32},{64,80},{80,64},{96,112},{112,96},{1... | collective-permute-start | bytes 884744 | tf_op jit(solution)/shard_map/ppermute | solution.py:493
  32.0 2.4 %collective-permute-start.10 = (f32[9,64,128]{2,1,0:T(8,128)S(1)}, f32[9,64,128]{2,1,0:T(8,128)S(1)}, u32[]{:S(2)}, u32[]{:S(2)}) collective-permute-start(f32[9,64,128]{2,1,0:T(8,128)S(1)} %get-tuple-element.40.x_face), channel_id=1, source_target_pairs={{0,112},{16,32},{32,16},{48,64},{64,48},{80,96},{96,80},{112,0},{1... | collective-permute-start | bytes 884744 | tf_op jit(solution)/shard_map/ppermute | solution.py:496
  34.4 1.1 %shard_map.71 = (f32[9,4,64,128]{3,2,1,0:T(8,128)S(1)}, f32[64,128]{1,0:T(8,128)S(1)}) custom-call(f32[9,4,64,128]{3,2,1,0:T(8,128)S(1)} %get-tuple-element.36.part, f32[4,64,128]{2,1,0:T(8,128)S(1)} %shard_map.68.terms, f32[9,64,128]{2,1,0:T(8,128)S(1)} %get-tuple-element.39.z_face, f32[9,64,128]{2,1,0:T(8,128)S(1)} %get-tuple-element.40.x_face), custom_call_target="tpu_custom_call" | custom-call | flops 1000000 | bytes 4000000 | tf_op jit(solution)/shard_map/pallas_call | solution.py:25
  35.5 1.7 %shard_map.72.refs_0_ = f32[9,4,64,128]{3,2,1,0:T(8,128)S(1)} custom-call(f32[15,4,64,128]{3,2,1,0:T(8,128)S(1)} %bitcast.7, f32[6,4,64,128]{3,2,1,0:T(8,128)S(1)} %bitcast.14, f32[9,4,64,128]{3,2,1,0:T(8,128)S(1)} %get-tuple-element.41.first.refs_2_), custom_call_target="tpu_custom_call" | custom-call | flops 5000000 | bytes 4000000 | tf_op jit(solution)/shard_map/pallas_call | solution.py:25
  37.2 5.0 %collective-permute-done.2.z_in.z_flow = f32[9,64,128]{2,1,0:T(8,128)S(1)} collective-permute-done((f32[9,64,128]{2,1,0:T(8,128)S(1)}, f32[9,64,128]{2,1,0:T(8,128)S(1)}, u32[]{:S(2)}, u32[]{:S(2)}) %collective-permute-start.2) | collective-permute-done | bytes 294944 | tf_op jit(solution)/shard_map/ppermute | solution.py:493
  42.2 0.0 collective-permute-done.5.x_in.x_flow
  42.2 0.2 shard_map.73
  42.3 2.3 %collective-permute-start.9 = (f32[6,64,128]{2,1,0:T(8,128)S(1)}, f32[6,64,128]{2,1,0:T(8,128)S(1)}, u32[]{:S(2)}, u32[]{:S(2)}) collective-permute-start(f32[6,64,128]{2,1,0:T(8,128)S(1)} %get-tuple-element.45.z_face), channel_id=1, source_target_pairs={{0,16},{16,0},{32,48},{48,32},{64,80},{80,64},{96,112},{112,96},{1... | collective-permute-start | bytes 589832 | tf_op jit(solution)/shard_map/ppermute | solution.py:493
  44.6 2.4 %collective-permute-start.11 = (f32[6,64,128]{2,1,0:T(8,128)S(1)}, f32[6,64,128]{2,1,0:T(8,128)S(1)}, u32[]{:S(2)}, u32[]{:S(2)}) collective-permute-start(f32[6,64,128]{2,1,0:T(8,128)S(1)} %get-tuple-element.46.x_face), channel_id=1, source_target_pairs={{0,112},{16,32},{32,16},{48,64},{64,48},{80,96},{96,80},{112,0},{1... | collective-permute-start | bytes 589832 | tf_op jit(solution)/shard_map/ppermute | solution.py:496
  47.0 0.9 %shard_map.74 = (f32[6,4,64,128]{3,2,1,0:T(8,128)S(1)}, f32[64,128]{1,0:T(8,128)S(1)}) custom-call(f32[6,4,64,128]{3,2,1,0:T(8,128)S(1)} %get-tuple-element.32.part, f32[4,64,128]{2,1,0:T(8,128)S(1)} %shard_map.68.terms, f32[6,64,128]{2,1,0:T(8,128)S(1)} %get-tuple-element.45.z_face, f32[6,64,128]{2,1,0:T(8,128)S(1)} %get-tuple-element.46.x_face, ...), custom_call_target="tpu_custom_call" | custom-call | flops 1000000 | bytes 4000000 | tf_op jit(solution)/shard_map/pallas_call | solution.py:25
  47.9 2.9 %collective-permute-start.6 = (f32[64,128]{1,0:T(8,128)S(1)}, f32[64,128]{1,0:T(8,128)S(1)}, u32[]{:S(2)}, u32[]{:S(2)}) collective-permute-start(f32[64,128]{1,0:T(8,128)S(1)} %get-tuple-element.49.packed), channel_id=1, source_target_pairs={{0,1},{1,0},{2,3},{3,2},{4,5},{5,4},{6,7},{7,6},{8,9},{9,8},{10,11... | collective-permute-start | bytes 98312 | tf_op jit(solution)/shard_map/ppermute | solution.py:493
  50.8 0.9 %collective-permute-done.6.inner = f32[64,128]{1,0:T(8,128)S(1)} collective-permute-done((f32[64,128]{1,0:T(8,128)S(1)}, f32[64,128]{1,0:T(8,128)S(1)}, u32[]{:S(2)}, u32[]{:S(2)}) %collective-permute-start.6) | collective-permute-done | bytes 32800 | tf_op jit(solution)/shard_map/ppermute | solution.py:493
  51.7 0.8 %collective-permute-start.7 = (f32[64,128]{1,0:T(8,128)S(1)}, f32[64,128]{1,0:T(8,128)S(1)}, u32[]{:S(2)}, u32[]{:S(2)}) collective-permute-start(f32[64,128]{1,0:T(8,128)S(1)} %get-tuple-element.49.packed), channel_id=1, source_target_pairs={{0,15},{1,2},{2,1},{3,4},{4,3},{5,6},{6,5},{7,8},{8,7},{9,10},{10,... | collective-permute-start | bytes 98312 | tf_op jit(solution)/shard_map/ppermute | solution.py:496
  52.5 1.3 %shard_map.76.refs_1_ = f32[6,4,64,128]{3,2,1,0:T(8,128)S(1)} custom-call(f32[15,4,64,128]{3,2,1,0:T(8,128)S(1)} %bitcast.9, f32[6,4,64,128]{3,2,1,0:T(8,128)S(1)} %bitcast.16, f32[6,4,64,128]{3,2,1,0:T(8,128)S(1)} %get-tuple-element.50.first.refs_3_), custom_call_target="tpu_custom_call" | custom-call | flops 5000000 | bytes 4000000 | tf_op jit(solution)/shard_map/pallas_call | solution.py:25
  53.9 1.4 %collective-permute-done.7.outer = f32[64,128]{1,0:T(8,128)S(1)} collective-permute-done((f32[64,128]{1,0:T(8,128)S(1)}, f32[64,128]{1,0:T(8,128)S(1)}, u32[]{:S(2)}, u32[]{:S(2)}) %collective-permute-start.7) | collective-permute-done | bytes 32800 | tf_op jit(solution)/shard_map/ppermute | solution.py:496
  55.3 0.3 shard_map.75.terms
  55.6 0.0 copy-done.4
  55.6 0.6 shard_map.77
  56.3 1.6 %collective-permute-done.9.refs_5_ = f32[6,64,128]{2,1,0:T(8,128)S(1)} collective-permute-done((f32[6,64,128]{2,1,0:T(8,128)S(1)}, f32[6,64,128]{2,1,0:T(8,128)S(1)}, u32[]{:S(2)}, u32[]{:S(2)}) %collective-permute-start.9) | collective-permute-done | bytes 196640 | tf_op jit(solution)/shard_map/ppermute | solution.py:493
  57.9 0.0 collective-permute-done.11.refs_7_
  57.9 0.0 collective-permute-done.8.refs_4_
  57.9 0.0 collective-permute-done.10.refs_6_
  57.9 0.9 %shard_map.78 = (f32[15,64,128]{2,1,0:T(8,128)S(1)}, f32[15,64,128]{2,1,0:T(8,128)S(1)}, f32[128,1,128]{2,1,0:T(1,128)S(1)}) custom-call(f32[6,4,64,128]{3,2,1,0:T(8,128)S(1)} %bitcast.17, f32[3,4,64,128]{3,2,1,0:T(8,128)S(1)} %copy-done.4, f32[4,64,128]{2,1,0:T(8,128)S(1)} %shard_map.75.terms, f32[20,8,128]{2,1,0:T(8,128)S(1)} %get-tuple-element.52.sums_in, ...), custom_call_target="tpu_custom_call" | custom-call | flops 1000000 | bytes 4000000 | tf_op jit(solution)/shard_map/pallas_call | solution.py:25
  58.8 20.8 %all_to_all.5.gathered = f32[128,1,128]{2,1,0:T(1,128)S(1)} all-to-all(f32[128,1,128]{2,1,0:T(1,128)S(1)} %get-tuple-element.55), channel_id=1, replica_groups=mesh['gx'=8,'gy'=16] {'gx','gy'}, dimensions={0} | all-to-all | bytes 131072 | tf_op jit(solution)/shard_map/all_to_all | solution.py:567
  79.6 2.1 %shard_map.79 = (f32[15,4,64,128]{3,2,1,0:T(8,128)}, f32[4,4]{1,0:T(4,128)}, f32[4]{0:T(128)}, f32[5]{0:T(128)}) custom-call(f32[15,2,64,128]{3,2,1,0:T(8,128)S(1)} %get-tuple-element.51.inside, f32[15,64,128]{2,1,0:T(8,128)S(1)} %get-tuple-element.53.z_face, f32[15,64,128]{2,1,0:T(8,128)S(1)} %get-tuple-element.54.x_face, f32[128,1,128]{2,1,0:T(1,128)S(1)} %all_to_all.5.gathered), custom_call_target="tpu_custom_call" | custom-call | flops 1000000 | bytes 4000000 | tf_op jit(solution)/shard_map/pallas_call | solution.py:25
  (1 shorter events, 0.0 us)
Async XLA Ops:
  0.6 1.5 %copy-start = (f32[5,3,4,64,128]{4,3,2,1,0:T(8,128)S(1)}, f32[5,3,4,64,128]{4,3,2,1,0:T(8,128)}, u32[]{:S(2)}) copy-start(f32[5,3,4,64,128]{4,3,2,1,0:T(8,128)} %param.3) | copy-start | bytes 5898244
  2.2 1.1 %copy-start.2 = (f32[2,3,4,64,128]{4,3,2,1,0:T(8,128)S(1)}, f32[2,3,4,64,128]{4,3,2,1,0:T(8,128)}, u32[]{:S(2)}) copy-start(f32[2,3,4,64,128]{4,3,2,1,0:T(8,128)} %param.4) | copy-start | bytes 2359300
  3.3 5.2 %copy-start.1 = (f32[5,3,4,64,128]{4,3,2,1,0:T(8,128)S(1)}, f32[5,3,4,64,128]{4,3,2,1,0:T(8,128)}, u32[]{:S(2)}) copy-start(f32[5,3,4,64,128]{4,3,2,1,0:T(8,128)} %param.3) | copy-start | bytes 5898244
  3.3 5.2 %copy-start.3 = (f32[2,3,4,64,128]{4,3,2,1,0:T(8,128)S(1)}, f32[2,3,4,64,128]{4,3,2,1,0:T(8,128)}, u32[]{:S(2)}) copy-start(f32[2,3,4,64,128]{4,3,2,1,0:T(8,128)} %param.4) | copy-start | bytes 2359300
  3.7 26.8 %collective-permute-start.3 = (f32[12,64,128]{2,1,0:T(8,128)S(1)}, f32[12,64,128]{2,1,0:T(8,128)S(1)}, u32[]{:S(2)}, u32[]{:S(2)}) collective-permute-start(f32[12,64,128]{2,1,0:T(8,128)S(1)} %get-tuple-element.37), channel_id=1, source_target_pairs={{0,16},{16,0},{32,48},{48,32},{64,80},{80,64},{96,112},{112,96},{1... | collective-permute-start | bytes 1179656 | tf_op jit(solution)/shard_map/ppermute | solution.py:493
  6.2 24.3 %collective-permute-start.4 = (f32[12,64,128]{2,1,0:T(8,128)S(1)}, f32[12,64,128]{2,1,0:T(8,128)S(1)}, u32[]{:S(2)}, u32[]{:S(2)}) collective-permute-start(f32[12,64,128]{2,1,0:T(8,128)S(1)} %get-tuple-element.38), channel_id=1, source_target_pairs={{0,112},{16,32},{32,16},{48,64},{64,48},{80,96},{96,80},{112,0},{1... | collective-permute-start | bytes 1179656 | tf_op jit(solution)/shard_map/ppermute | solution.py:496
  10.3 1.9 %collective-permute-start = (f32[2,64,128]{2,1,0:T(8,128)S(1)}, f32[2,64,128]{2,1,0:T(8,128)S(1)}, u32[]{:S(2)}, u32[]{:S(2)}) collective-permute-start(f32[2,64,128]{2,1,0:T(8,128)S(1)} %shard_map.66.columns), channel_id=1, source_target_pairs={{0,1},{1,0},{2,3},{3,2},{4,5},{5,4},{6,7},{7,6},{8,9},{9,8},{10,11... | collective-permute-start | bytes 196616 | tf_op jit(solution)/shard_map/ppermute | solution.py:493
  12.2 4.0 %collective-permute-start.1 = (f32[2,64,128]{2,1,0:T(8,128)S(1)}, f32[2,64,128]{2,1,0:T(8,128)S(1)}, u32[]{:S(2)}, u32[]{:S(2)}) collective-permute-start(f32[2,64,128]{2,1,0:T(8,128)S(1)} %shard_map.66.columns), channel_id=1, source_target_pairs={{0,15},{1,2},{2,1},{3,4},{4,3},{5,6},{6,5},{7,8},{8,7},{9,10},{10,... | collective-permute-start | bytes 196616 | tf_op jit(solution)/shard_map/ppermute | solution.py:496
  16.2 26.0 %collective-permute-start.2 = (f32[9,64,128]{2,1,0:T(8,128)S(1)}, f32[9,64,128]{2,1,0:T(8,128)S(1)}, u32[]{:S(2)}, u32[]{:S(2)}) collective-permute-start(f32[9,64,128]{2,1,0:T(8,128)S(1)} %get-tuple-element.35), channel_id=1, source_target_pairs={{0,16},{16,0},{32,48},{48,32},{64,80},{80,64},{96,112},{112,96},{1... | collective-permute-start | bytes 884744 | tf_op jit(solution)/shard_map/ppermute | solution.py:493
  16.6 25.6 %collective-permute-start.5 = (f32[9,64,128]{2,1,0:T(8,128)S(1)}, f32[9,64,128]{2,1,0:T(8,128)S(1)}, u32[]{:S(2)}, u32[]{:S(2)}) collective-permute-start(f32[9,64,128]{2,1,0:T(8,128)S(1)} %get-tuple-element.44), channel_id=1, source_target_pairs={{0,112},{16,32},{32,16},{48,64},{64,48},{80,96},{96,80},{112,0},{1... | collective-permute-start | bytes 884744 | tf_op jit(solution)/shard_map/ppermute | solution.py:496
  30.8 27.2 %collective-permute-start.8 = (f32[9,64,128]{2,1,0:T(8,128)S(1)}, f32[9,64,128]{2,1,0:T(8,128)S(1)}, u32[]{:S(2)}, u32[]{:S(2)}) collective-permute-start(f32[9,64,128]{2,1,0:T(8,128)S(1)} %get-tuple-element.39.z_face), channel_id=1, source_target_pairs={{0,16},{16,0},{32,48},{48,32},{64,80},{80,64},{96,112},{112,96},{1... | collective-permute-start | bytes 884744 | tf_op jit(solution)/shard_map/ppermute | solution.py:493
  32.0 25.9 %collective-permute-start.10 = (f32[9,64,128]{2,1,0:T(8,128)S(1)}, f32[9,64,128]{2,1,0:T(8,128)S(1)}, u32[]{:S(2)}, u32[]{:S(2)}) collective-permute-start(f32[9,64,128]{2,1,0:T(8,128)S(1)} %get-tuple-element.40.x_face), channel_id=1, source_target_pairs={{0,112},{16,32},{32,16},{48,64},{64,48},{80,96},{96,80},{112,0},{1... | collective-permute-start | bytes 884744 | tf_op jit(solution)/shard_map/ppermute | solution.py:496
  42.3 15.6 %collective-permute-start.9 = (f32[6,64,128]{2,1,0:T(8,128)S(1)}, f32[6,64,128]{2,1,0:T(8,128)S(1)}, u32[]{:S(2)}, u32[]{:S(2)}) collective-permute-start(f32[6,64,128]{2,1,0:T(8,128)S(1)} %get-tuple-element.45.z_face), channel_id=1, source_target_pairs={{0,16},{16,0},{32,48},{48,32},{64,80},{80,64},{96,112},{112,96},{1... | collective-permute-start | bytes 589832 | tf_op jit(solution)/shard_map/ppermute | solution.py:493
  44.6 13.3 %collective-permute-start.11 = (f32[6,64,128]{2,1,0:T(8,128)S(1)}, f32[6,64,128]{2,1,0:T(8,128)S(1)}, u32[]{:S(2)}, u32[]{:S(2)}) collective-permute-start(f32[6,64,128]{2,1,0:T(8,128)S(1)} %get-tuple-element.46.x_face), channel_id=1, source_target_pairs={{0,112},{16,32},{32,16},{48,64},{64,48},{80,96},{96,80},{112,0},{1... | collective-permute-start | bytes 589832 | tf_op jit(solution)/shard_map/ppermute | solution.py:496
  47.9 3.8 %collective-permute-start.6 = (f32[64,128]{1,0:T(8,128)S(1)}, f32[64,128]{1,0:T(8,128)S(1)}, u32[]{:S(2)}, u32[]{:S(2)}) collective-permute-start(f32[64,128]{1,0:T(8,128)S(1)} %get-tuple-element.49.packed), channel_id=1, source_target_pairs={{0,1},{1,0},{2,3},{3,2},{4,5},{5,4},{6,7},{7,6},{8,9},{9,8},{10,11... | collective-permute-start | bytes 98312 | tf_op jit(solution)/shard_map/ppermute | solution.py:493
  51.7 3.6 %collective-permute-start.7 = (f32[64,128]{1,0:T(8,128)S(1)}, f32[64,128]{1,0:T(8,128)S(1)}, u32[]{:S(2)}, u32[]{:S(2)}) collective-permute-start(f32[64,128]{1,0:T(8,128)S(1)} %get-tuple-element.49.packed), channel_id=1, source_target_pairs={{0,15},{1,2},{2,1},{3,4},{4,3},{5,6},{6,5},{7,8},{8,7},{9,10},{10,... | collective-permute-start | bytes 98312 | tf_op jit(solution)/shard_map/ppermute | solution.py:496
  52.5 3.1 %copy-start.4 = (f32[3,4,64,128]{3,2,1,0:T(8,128)S(1)}, f32[3,4,64,128]{3,2,1,0:T(8,128)}, u32[]{:S(2)}) copy-start(f32[3,4,64,128]{3,2,1,0:T(8,128)} %weight.3) | copy-start | bytes 1179652

commit v3 on v2

--- a/solution.py
+++ b/solution.py
@@ -52,12 +52,13 @@
     return lax.rem(lax.axis_index("gy"), 2) == 0
 
 
-def faces_kernel(t, u, *refs):
+def faces_kernel(chosen, t, u, *refs):
     outs, sem = refs[:-1], refs[-1]
     (z_plane, _), (x_plane, _) = sides()
     last = len(groups) - 1
     copies = []
-    for g, members in enumerate(groups):
+    for slot, g in enumerate(chosen):
+        members = groups[g]
         sources = [(t, 3 * members[0], 3 * len(members))]
         sources += [(u, 0, 3)] if g == 0 else []
         sources += [(u, 3, 3)] if g == last else []
@@ -67,7 +68,7 @@
                 copies.append(
                     pltpu.make_async_copy(
                         ref.at[pl.ds(start, count), plane],
-                        outs[2 * g + side].at[pl.ds(at, count)],
+                        outs[2 * slot + side].at[pl.ds(at, count)],
                         sem.at[len(copies)],
                     )
                 )
@@ -90,7 +91,7 @@
     return lane & -2, lane >> 5
 
 
-def pack_first_kernel(t, u, out):
+def pack_first_kernel(t, u, face, out):
     parts = lane_parts()
 
     def at_rows(zt, carry):
@@ -416,28 +417,37 @@
     sums_out[...] = jnp.broadcast_to(line[None], sums_out.shape)
 
 
-def renorm_kernel(total_cells, inside, z_face, x_face, gathered, out, r_out, c_out, o_out):
-    line = jnp.sum(gathered[...], axis=0)
+def renorm_kernel(total_cells, inside, z_face, x_face, gathered, out, r_out, c_out, o_out, ready, sem):
+    chains = []
+    for first in range(8):
+        chain = gathered[first]
+        for device in range(first + 8, gathered.shape[0], 8):
+            chain = chain + gathered[device]
+        chains.append(chain)
+    while len(chains) > 1:
+        chains = [chains[n] + chains[n + 1] for n in range(0, len(chains), 2)]
+    line = chains[0]
     spread = [jnp.broadcast_to(line[:, n : n + 1], tile) for n in range(20)]
     gram = {pair: spread[n] * f32(1.0 / (3.0 * total_cells)) for n, pair in enumerate(pairs)}
-    lower = {}
+    lower, below = {}, {}
     for c in range(4):
         value = gram[(c, c)]
         for m in range(c):
             value = value - lower[(c, m)] * lower[(c, m)]
         lower[(c, c)] = jnp.sqrt(value)
+        below[c] = 1.0 / lower[(c, c)]
         for r in range(c + 1, 4):
             value = gram[(c, r)]
             for m in range(c):
                 value = value - lower[(r, m)] * lower[(c, m)]
-            lower[(r, c)] = value / lower[(c, c)]
+            lower[(r, c)] = value * below[c]
     inverse = {}
     for r in range(4):
         for c in range(r + 1):
             value = jnp.ones(tile, f32) if r == c else jnp.zeros(tile, f32)
             for m in range(c, r):
                 value = value - lower[(r, m)] * inverse[(m, c)]
-            inverse[(r, c)] = value / lower[(r, r)]
+            inverse[(r, c)] = value * below[r]
     coefficient = []
     for r in range(4):
         value = inverse[(r, 0)] * gram[(0, 4)]
@@ -458,6 +468,7 @@
     o_out[...] = objective[0, :5]
 
     (z_plane, _), (x_plane, _) = sides()
+    copies = []
     for plane, load in (
         (1, lambda f, rows: inside[f, 0, rows]),
         (2, lambda f, rows: inside[f, 1, rows]),
@@ -474,12 +485,17 @@
                     value = inverse[(r, 0)] * now[0]
                     for c in range(1, r + 1):
                         value = value + inverse[(r, c)] * now[c]
-                    out[3 * r + i, plane, rows] = value
+                    ready[3 * r + i, plane, rows] = value
                     last = last - coefficient[r] * value
-                out[12 + i, plane, rows] = last
+                ready[12 + i, plane, rows] = last
             return carry
 
-        lax.fori_loop(0, 8, at_rows, 0)
+        lax.fori_loop(0, 8, at_rows, 0, unroll=4)
+        copy = pltpu.make_async_copy(ready.at[:, plane], out.at[:, plane], sem.at[len(copies)])
+        copy.start()
+        copies.append(copy)
+    for copy in copies:
+        copy.wait()
 
 
 def per_device(tangents, base_flow, objective_weight):
@@ -500,17 +516,20 @@
 
     sizes = [3 * len(members) for members in groups]
     sent = [s + (3 if g == 0 else 0) + (3 if g == last else 0) for g, s in enumerate(sizes)]
-    faces = pl.pallas_call(
-        faces_kernel,
-        out_shape=tuple(shaped(s, 64, 128) for s in sent for _ in range(2)),
-        in_specs=[pl.BlockSpec(memory_space=pltpu.HBM)] * 2,
-        out_specs=(vmem,) * (2 * len(groups)),
-        scratch_shapes=[pltpu.SemaphoreType.DMA((2 * len(groups) + 4,))],
-        compiler_params=pltpu.CompilerParams(vmem_limit_bytes=8 << 20),
-    )(t, u)
+    def send_buffers(chosen, limit):
+        return pl.pallas_call(
+            functools.partial(faces_kernel, chosen),
+            out_shape=tuple(shaped(sent[g], 64, 128) for g in chosen for _ in range(2)),
+            in_specs=[pl.BlockSpec(memory_space=pltpu.HBM)] * 2,
+            out_specs=(vmem,) * (2 * len(chosen)),
+            scratch_shapes=[pltpu.SemaphoreType.DMA((2 * len(chosen) + 4,))],
+            compiler_params=pltpu.CompilerParams(vmem_limit_bytes=limit),
+        )(t, u)
+
+    faces = [*send_buffers((0,), None), *send_buffers(tuple(range(1, len(groups))), 8 << 20)]
     z_in = [partner(faces[0], "gx", count_x)]
     x_in = [beyond(faces[1], "gx", count_x)]
-    columns = call(pack_first_kernel, shaped(2, 64, 128), (t, u))
+    columns = call(pack_first_kernel, shaped(2, 64, 128), (t, u, faces[1]))
     inner_in = partner(columns, "gy", count_y)
     outer_in = beyond(after(columns, inner_in), "gy", count_y)
     parts = call(
@@ -565,11 +584,14 @@
         (u, objective_weight, terms, sums, z_in[last], x_in[last], *halves, *first, *z_next, *x_next),
     )
     gathered = lax.all_to_all(line, ("gx", "gy"), 0, 0, tiled=True)
-    renormed, rfactor, coefficients, objective = call(
+    renormed, rfactor, coefficients, objective = pl.pallas_call(
         functools.partial(renorm_kernel, total_cells),
-        (shaped(15, 4, 64, 128), shaped(4, 4), shaped(4), shaped(5)),
-        (inside, z_face, x_face, gathered),
-    )
+        out_shape=(shaped(15, 4, 64, 128), shaped(4, 4), shaped(4), shaped(5)),
+        in_specs=[vmem] * 4,
+        out_specs=(pl.BlockSpec(memory_space=pl.ANY), vmem, vmem, vmem),
+        scratch_shapes=[pltpu.VMEM((15, 4, 64, 128), f32), pltpu.SemaphoreType.DMA((4,))],
+        compiler_params=pltpu.CompilerParams(vmem_limit_bytes=24 << 20),
+    )(inside, z_face, x_face, gathered)
     return (renormed.reshape(tangents.shape), rfactor, coefficients, objective)
 
 

time: 81.9 us -> 81.3 us (level)
  Pallas kernels: 14.2 us -> 16.3 us
  waiting for transfers between devices: 22.1 us -> 20.2 us
  local copies, waits for them, and re-layouts: 2.68 us -> 1.04 us
  starting transfers between devices: 21.1 us -> 22 us
    pallas_call x1 -> x3, Pallas kernels: 0.38 us -> 4.57 us  [the longest x2 2.42 us: send_buffers(): pl.pallas_call(functools.partial(faces_kernel, chosen), out_shape=tuple((...]
    pallas_call x13 -> x12, Pallas kernels: 13.9 us -> 11.8 us  [call(): pl.pallas_call(body, out_shape=outs, in_specs=[vmem] * len(args), out_spe...]
    ppermute x6, waiting for transfers between devices: 18.2 us -> 16.5 us  [partner(): return lax.ppermute(values, axis, [(i, i ^ 1) for i in range(count)])]
    unnamed x10 -> x8, local copies, waits for them, and re-layouts: 2.68 us -> 1.04 us
    ppermute x6, starting transfers between devices: 10.4 us -> 11.3 us  [partner(): return lax.ppermute(values, axis, [(i, i ^ 1) for i in range(count)])]
  transfers between devices with their start and end apart: 12 -> 12, of which waited for: 7 -> 7; matrix products, arithmetic and copies ran while one was open for 0% -> 0% of each run, Pallas kernels for 13% -> 14%
where the time goes in v3:
time: 81.3 us; the launch traced here: 81.1 us
  starting transfers between devices  22 us (27%)
  blocking collectives  20.8 us (26%)
  waiting for transfers between devices  20.2 us (25%)
  Pallas kernels  16.3 us (20%)
  local copies, waits for them, and re-layouts  1.04 us (1%)
    all_to_all x1, blocking collectives, per_device(): gathered = lax.all_to_all(line, ('gx', 'gy'), 0, 0, tiled=True)  20.8 us
    ppermute x6, waiting for transfers between devices, partner(): return lax.ppermute(values, axis, [(i, i ^ 1) for i in range(count)])  16.5 us
    pallas_call x12, Pallas kernels, call(): pl.pallas_call(body, out_shape=outs, in_specs=[vmem] * len(args), out_spe...  11.8 us
    ppermute x6, starting transfers between devices, partner(): return lax.ppermute(values, axis, [(i, i ^ 1) for i in range(count)])  11.3 us
    ppermute x6, starting transfers between devices, beyond(): lax.ppermute(values, axis, [(i, (i + 2 * (i % 2) - 1) % count) for i in r...  10.7 us
    ppermute x6, waiting for transfers between devices, beyond(): lax.ppermute(values, axis, [(i, (i + 2 * (i % 2) - 1) % count) for i in r...  3.68 us
    pallas_call x2, Pallas kernels, send_buffers(): pl.pallas_call(functools.partial(faces_kernel, chosen), out_shape=tuple((...  2.42 us
    pallas_call x1, Pallas kernels, per_device(): pl.pallas_call(functools.partial(renorm_kernel, total_cells), out_shape=(...  2.14 us
  transfers between devices with their start and end apart: 12, of which 7 were waited for; matrix products, arithmetic and copies ran while one was open for 0% of the time, Pallas kernels for 14%

profile of v3, /device:TPU:1, one launch (start us, length us, event | category | flops | bytes accessed | tf_op | source)
XLA Modules:
  0.0 81.1 jit_solution(5479953254171508156)
XLA Ops:
  0.6 0.0 copy-start
  0.6 0.0 copy-start.1
  0.7 2.2 %shard_map.66 = (f32[12,64,128]{2,1,0:T(8,128)}, f32[12,64,128]{2,1,0:T(8,128)}) custom-call(f32[15,4,64,128]{3,2,1,0:T(8,128)} %bitcast.3, f32[6,4,64,128]{3,2,1,0:T(8,128)} %bitcast.11), custom_call_target="tpu_custom_call" | custom-call | tf_op jit(solution)/shard_map/pallas_call | solution.py:520
  2.9 2.5 %collective-permute-start.3 = (f32[12,64,128]{2,1,0:T(8,128)}, f32[12,64,128]{2,1,0:T(8,128)S(1)}, u32[]{:S(2)}, u32[]{:S(2)}) collective-permute-start(f32[12,64,128]{2,1,0:T(8,128)} %get-tuple-element.38), channel_id=1, source_target_pairs={{0,16},{16,0},{32,48},{48,32},{64,80},{80,64},{96,112},{112,96},{1... | collective-permute-start | bytes 1179656 | tf_op jit(solution)/shard_map/ppermute | solution.py:509
  5.4 2.3 %collective-permute-start.4 = (f32[12,64,128]{2,1,0:T(8,128)}, f32[12,64,128]{2,1,0:T(8,128)S(1)}, u32[]{:S(2)}, u32[]{:S(2)}) collective-permute-start(f32[12,64,128]{2,1,0:T(8,128)} %get-tuple-element.32.face), channel_id=1, source_target_pairs={{0,112},{16,32},{32,16},{48,64},{64,48},{80,96},{96,80},{112,0},{1... | collective-permute-start | bytes 1179656 | tf_op jit(solution)/shard_map/ppermute | solution.py:512
  7.7 0.0 copy-done
  7.7 0.0 copy-done.1
  7.7 0.0 copy-start.3
  7.7 1.0 %copy-done.3 = f32[12,64,128]{2,1,0:T(8,128)S(1)} copy-done((f32[12,64,128]{2,1,0:T(8,128)S(1)}, f32[12,64,128]{2,1,0:T(8,128)}, u32[]{:S(2)}) %copy-start.3) | copy-done | bytes 393240
  8.7 1.8 %shard_map.67.columns = f32[2,64,128]{2,1,0:T(8,128)S(1)} custom-call(f32[15,4,64,128]{3,2,1,0:T(8,128)S(1)} %bitcast.4, f32[6,4,64,128]{3,2,1,0:T(8,128)S(1)} %bitcast.12, f32[12,64,128]{2,1,0:T(8,128)S(1)} %copy-done.3), custom_call_target="tpu_custom_call" | custom-call | flops 1000000 | bytes 4000000 | tf_op jit(solution)/shard_map/pallas_call | solution.py:25
  10.5 1.0 %collective-permute-start = (f32[2,64,128]{2,1,0:T(8,128)S(1)}, f32[2,64,128]{2,1,0:T(8,128)S(1)}, u32[]{:S(2)}, u32[]{:S(2)}) collective-permute-start(f32[2,64,128]{2,1,0:T(8,128)S(1)} %shard_map.67.columns), channel_id=1, source_target_pairs={{0,1},{1,0},{2,3},{3,2},{4,5},{5,4},{6,7},{7,6},{8,9},{9,8},{10,11... | collective-permute-start | bytes 196616 | tf_op jit(solution)/shard_map/ppermute | solution.py:509
  11.5 0.9 %collective-permute-done.inner.inner_flow = f32[2,64,128]{2,1,0:T(8,128)S(1)} collective-permute-done((f32[2,64,128]{2,1,0:T(8,128)S(1)}, f32[2,64,128]{2,1,0:T(8,128)S(1)}, u32[]{:S(2)}, u32[]{:S(2)}) %collective-permute-start) | collective-permute-done | bytes 65568 | tf_op jit(solution)/shard_map/ppermute | solution.py:509
  12.4 1.5 %collective-permute-start.1 = (f32[2,64,128]{2,1,0:T(8,128)S(1)}, f32[2,64,128]{2,1,0:T(8,128)S(1)}, u32[]{:S(2)}, u32[]{:S(2)}) collective-permute-start(f32[2,64,128]{2,1,0:T(8,128)S(1)} %shard_map.67.columns), channel_id=1, source_target_pairs={{0,15},{1,2},{2,1},{3,4},{4,3},{5,6},{6,5},{7,8},{8,7},{9,10},{10,... | collective-permute-start | bytes 196616 | tf_op jit(solution)/shard_map/ppermute | solution.py:512
  13.9 0.2 shard_map.70
  14.2 2.2 %collective-permute-done.1.outer.outer_flow = f32[2,64,128]{2,1,0:T(8,128)S(1)} collective-permute-done((f32[2,64,128]{2,1,0:T(8,128)S(1)}, f32[2,64,128]{2,1,0:T(8,128)S(1)}, u32[]{:S(2)}, u32[]{:S(2)}) %collective-permute-start.1) | collective-permute-done | bytes 65568 | tf_op jit(solution)/shard_map/ppermute | solution.py:512
  16.4 0.4 collective-permute-start.2
  16.7 1.4 %collective-permute-start.5 = (f32[9,64,128]{2,1,0:T(8,128)S(1)}, f32[9,64,128]{2,1,0:T(8,128)S(1)}, u32[]{:S(2)}, u32[]{:S(2)}) collective-permute-start(f32[9,64,128]{2,1,0:T(8,128)S(1)} %get-tuple-element.44), channel_id=1, source_target_pairs={{0,112},{16,32},{32,16},{48,64},{64,48},{80,96},{96,80},{112,0},{1... | collective-permute-start | bytes 884744 | tf_op jit(solution)/shard_map/ppermute | solution.py:512
  18.1 2.4 %shard_map.68 = (f32[9,4,64,128]{3,2,1,0:T(8,128)S(1)}, f32[6,4,64,128]{3,2,1,0:T(8,128)S(1)}) custom-call(f32[15,4,64,128]{3,2,1,0:T(8,128)S(1)} %bitcast.6, f32[6,4,64,128]{3,2,1,0:T(8,128)S(1)} %bitcast.14, f32[2,64,128]{2,1,0:T(8,128)S(1)} %shard_map.67.columns), custom_call_target="tpu_custom_call" | custom-call | flops 10000000 | bytes 4000000 | tf_op jit(solution)/shard_map/pallas_call | solution.py:25
  20.5 0.3 shard_map.69.terms
  20.8 8.2 %collective-permute-done.3.z_in.z_flow = f32[12,64,128]{2,1,0:T(8,128)S(1)} collective-permute-done((f32[12,64,128]{2,1,0:T(8,128)}, f32[12,64,128]{2,1,0:T(8,128)S(1)}, u32[]{:S(2)}, u32[]{:S(2)}) %collective-permute-start.3) | collective-permute-done | bytes 393248 | tf_op jit(solution)/shard_map/ppermute | solution.py:509
  29.0 0.0 collective-permute-done.4.x_in.x_flow
  29.0 0.2 shard_map.71
  29.2 2.2 %collective-permute-start.8 = (f32[9,64,128]{2,1,0:T(8,128)S(1)}, f32[9,64,128]{2,1,0:T(8,128)S(1)}, u32[]{:S(2)}, u32[]{:S(2)}) collective-permute-start(f32[9,64,128]{2,1,0:T(8,128)S(1)} %get-tuple-element.39.z_face), channel_id=1, source_target_pairs={{0,16},{16,0},{32,48},{48,32},{64,80},{80,64},{96,112},{112,96},{1... | collective-permute-start | bytes 884744 | tf_op jit(solution)/shard_map/ppermute | solution.py:509
  31.4 2.4 %collective-permute-start.10 = (f32[9,64,128]{2,1,0:T(8,128)S(1)}, f32[9,64,128]{2,1,0:T(8,128)S(1)}, u32[]{:S(2)}, u32[]{:S(2)}) collective-permute-start(f32[9,64,128]{2,1,0:T(8,128)S(1)} %get-tuple-element.40.x_face), channel_id=1, source_target_pairs={{0,112},{16,32},{32,16},{48,64},{64,48},{80,96},{96,80},{112,0},{1... | collective-permute-start | bytes 884744 | tf_op jit(solution)/shard_map/ppermute | solution.py:512
  33.8 1.1 %shard_map.72 = (f32[9,4,64,128]{3,2,1,0:T(8,128)S(1)}, f32[64,128]{1,0:T(8,128)S(1)}) custom-call(f32[9,4,64,128]{3,2,1,0:T(8,128)S(1)} %get-tuple-element.37.part, f32[4,64,128]{2,1,0:T(8,128)S(1)} %shard_map.69.terms, f32[9,64,128]{2,1,0:T(8,128)S(1)} %get-tuple-element.39.z_face, f32[9,64,128]{2,1,0:T(8,128)S(1)} %get-tuple-element.40.x_face), custom_call_target="tpu_custom_call" | custom-call | flops 1000000 | bytes 4000000 | tf_op jit(solution)/shard_map/pallas_call | solution.py:25
  34.9 1.7 %shard_map.73.refs_0_ = f32[9,4,64,128]{3,2,1,0:T(8,128)S(1)} custom-call(f32[15,4,64,128]{3,2,1,0:T(8,128)S(1)} %bitcast.8, f32[6,4,64,128]{3,2,1,0:T(8,128)S(1)} %bitcast.16, f32[9,4,64,128]{3,2,1,0:T(8,128)S(1)} %get-tuple-element.41.first.refs_2_), custom_call_target="tpu_custom_call" | custom-call | flops 5000000 | bytes 4000000 | tf_op jit(solution)/shard_map/pallas_call | solution.py:25
  36.6 5.0 %collective-permute-done.2.z_in.z_flow = f32[9,64,128]{2,1,0:T(8,128)S(1)} collective-permute-done((f32[9,64,128]{2,1,0:T(8,128)S(1)}, f32[9,64,128]{2,1,0:T(8,128)S(1)}, u32[]{:S(2)}, u32[]{:S(2)}) %collective-permute-start.2) | collective-permute-done | bytes 294944 | tf_op jit(solution)/shard_map/ppermute | solution.py:509
  41.5 0.0 collective-permute-done.5.x_in.x_flow
  41.5 0.2 shard_map.74
  41.7 2.3 %collective-permute-start.9 = (f32[6,64,128]{2,1,0:T(8,128)S(1)}, f32[6,64,128]{2,1,0:T(8,128)S(1)}, u32[]{:S(2)}, u32[]{:S(2)}) collective-permute-start(f32[6,64,128]{2,1,0:T(8,128)S(1)} %get-tuple-element.45.z_face), channel_id=1, source_target_pairs={{0,16},{16,0},{32,48},{48,32},{64,80},{80,64},{96,112},{112,96},{1... | collective-permute-start | bytes 589832 | tf_op jit(solution)/shard_map/ppermute | solution.py:509
  44.0 2.4 %collective-permute-start.11 = (f32[6,64,128]{2,1,0:T(8,128)S(1)}, f32[6,64,128]{2,1,0:T(8,128)S(1)}, u32[]{:S(2)}, u32[]{:S(2)}) collective-permute-start(f32[6,64,128]{2,1,0:T(8,128)S(1)} %get-tuple-element.46.x_face), channel_id=1, source_target_pairs={{0,112},{16,32},{32,16},{48,64},{64,48},{80,96},{96,80},{112,0},{1... | collective-permute-start | bytes 589832 | tf_op jit(solution)/shard_map/ppermute | solution.py:512
  46.4 0.9 %shard_map.75 = (f32[6,4,64,128]{3,2,1,0:T(8,128)S(1)}, f32[64,128]{1,0:T(8,128)S(1)}) custom-call(f32[6,4,64,128]{3,2,1,0:T(8,128)S(1)} %get-tuple-element.33.part, f32[4,64,128]{2,1,0:T(8,128)S(1)} %shard_map.69.terms, f32[6,64,128]{2,1,0:T(8,128)S(1)} %get-tuple-element.45.z_face, f32[6,64,128]{2,1,0:T(8,128)S(1)} %get-tuple-element.46.x_face, ...), custom_call_target="tpu_custom_call" | custom-call | flops 1000000 | bytes 4000000 | tf_op jit(solution)/shard_map/pallas_call | solution.py:25
  47.3 2.9 %collective-permute-start.6 = (f32[64,128]{1,0:T(8,128)S(1)}, f32[64,128]{1,0:T(8,128)S(1)}, u32[]{:S(2)}, u32[]{:S(2)}) collective-permute-start(f32[64,128]{1,0:T(8,128)S(1)} %get-tuple-element.49.packed), channel_id=1, source_target_pairs={{0,1},{1,0},{2,3},{3,2},{4,5},{5,4},{6,7},{7,6},{8,9},{9,8},{10,11... | collective-permute-start | bytes 98312 | tf_op jit(solution)/shard_map/ppermute | solution.py:509
  50.2 0.9 %collective-permute-done.6.inner = f32[64,128]{1,0:T(8,128)S(1)} collective-permute-done((f32[64,128]{1,0:T(8,128)S(1)}, f32[64,128]{1,0:T(8,128)S(1)}, u32[]{:S(2)}, u32[]{:S(2)}) %collective-permute-start.6) | collective-permute-done | bytes 32800 | tf_op jit(solution)/shard_map/ppermute | solution.py:509
  51.1 0.8 %collective-permute-start.7 = (f32[64,128]{1,0:T(8,128)S(1)}, f32[64,128]{1,0:T(8,128)S(1)}, u32[]{:S(2)}, u32[]{:S(2)}) collective-permute-start(f32[64,128]{1,0:T(8,128)S(1)} %get-tuple-element.49.packed), channel_id=1, source_target_pairs={{0,15},{1,2},{2,1},{3,4},{4,3},{5,6},{6,5},{7,8},{8,7},{9,10},{10,... | collective-permute-start | bytes 98312 | tf_op jit(solution)/shard_map/ppermute | solution.py:512
  51.9 0.0 copy-start.2
  51.9 1.3 %shard_map.77.refs_1_ = f32[6,4,64,128]{3,2,1,0:T(8,128)S(1)} custom-call(f32[15,4,64,128]{3,2,1,0:T(8,128)S(1)} %bitcast.10, f32[6,4,64,128]{3,2,1,0:T(8,128)S(1)} %bitcast.18, f32[6,4,64,128]{3,2,1,0:T(8,128)S(1)} %get-tuple-element.50.first.refs_3_), custom_call_target="tpu_custom_call" | custom-call | flops 5000000 | bytes 4000000 | tf_op jit(solution)/shard_map/pallas_call | solution.py:25
  53.2 1.4 %collective-permute-done.7.outer = f32[64,128]{1,0:T(8,128)S(1)} collective-permute-done((f32[64,128]{1,0:T(8,128)S(1)}, f32[64,128]{1,0:T(8,128)S(1)}, u32[]{:S(2)}, u32[]{:S(2)}) %collective-permute-start.7) | collective-permute-done | bytes 32800 | tf_op jit(solution)/shard_map/ppermute | solution.py:512
  54.7 0.3 shard_map.76.terms
  55.0 0.0 copy-done.2
  55.0 0.6 shard_map.78
  55.7 1.6 %collective-permute-done.9.refs_5_ = f32[6,64,128]{2,1,0:T(8,128)S(1)} collective-permute-done((f32[6,64,128]{2,1,0:T(8,128)S(1)}, f32[6,64,128]{2,1,0:T(8,128)S(1)}, u32[]{:S(2)}, u32[]{:S(2)}) %collective-permute-start.9) | collective-permute-done | bytes 196640 | tf_op jit(solution)/shard_map/ppermute | solution.py:509
  57.3 0.0 collective-permute-done.11.refs_7_
  57.3 0.0 collective-permute-done.8.refs_4_
  57.3 0.0 collective-permute-done.10.refs_6_
  57.3 0.9 %shard_map.79 = (f32[15,64,128]{2,1,0:T(8,128)S(1)}, f32[15,64,128]{2,1,0:T(8,128)S(1)}, f32[128,1,128]{2,1,0:T(1,128)S(1)}) custom-call(f32[6,4,64,128]{3,2,1,0:T(8,128)S(1)} %bitcast.19, f32[3,4,64,128]{3,2,1,0:T(8,128)S(1)} %copy-done.2, f32[4,64,128]{2,1,0:T(8,128)S(1)} %shard_map.76.terms, f32[20,8,128]{2,1,0:T(8,128)S(1)} %get-tuple-element.52.sums_in, ...), custom_call_target="tpu_custom_call" | custom-call | flops 1000000 | bytes 4000000 | tf_op jit(solution)/shard_map/pallas_call | solution.py:25
  58.2 20.8 %all_to_all.5.gathered = f32[128,1,128]{2,1,0:T(1,128)S(1)} all-to-all(f32[128,1,128]{2,1,0:T(1,128)S(1)} %get-tuple-element.55), channel_id=1, replica_groups=mesh['gx'=8,'gy'=16] {'gx','gy'}, dimensions={0} | all-to-all | bytes 131072 | tf_op jit(solution)/shard_map/all_to_all | solution.py:586
  79.0 2.1 %shard_map.80 = (f32[15,4,64,128]{3,2,1,0:T(8,128)}, f32[4,4]{1,0:T(4,128)}, f32[4]{0:T(128)}, f32[5]{0:T(128)}) custom-call(f32[15,2,64,128]{3,2,1,0:T(8,128)S(1)} %get-tuple-element.51.inside, f32[15,64,128]{2,1,0:T(8,128)S(1)} %get-tuple-element.53.z_face, f32[15,64,128]{2,1,0:T(8,128)S(1)} %get-tuple-element.54.x_face, f32[128,1,128]{2,1,0:T(1,128)S(1)} %all_to_all.5.gathered), custom_call_target="tpu_custom_call" | custom-call | tf_op jit(solution)/shard_map/pallas_call | solution.py:587
Async XLA Ops:
  0.6 7.1 %copy-start = (f32[5,3,4,64,128]{4,3,2,1,0:T(8,128)S(1)}, f32[5,3,4,64,128]{4,3,2,1,0:T(8,128)}, u32[]{:S(2)}) copy-start(f32[5,3,4,64,128]{4,3,2,1,0:T(8,128)} %param.3) | copy-start | bytes 5898244
  0.6 7.1 %copy-start.1 = (f32[2,3,4,64,128]{4,3,2,1,0:T(8,128)S(1)}, f32[2,3,4,64,128]{4,3,2,1,0:T(8,128)}, u32[]{:S(2)}) copy-start(f32[2,3,4,64,128]{4,3,2,1,0:T(8,128)} %param.4) | copy-start | bytes 2359300
  2.9 26.1 %collective-permute-start.3 = (f32[12,64,128]{2,1,0:T(8,128)}, f32[12,64,128]{2,1,0:T(8,128)S(1)}, u32[]{:S(2)}, u32[]{:S(2)}) collective-permute-start(f32[12,64,128]{2,1,0:T(8,128)} %get-tuple-element.38), channel_id=1, source_target_pairs={{0,16},{16,0},{32,48},{48,32},{64,80},{80,64},{96,112},{112,96},{1... | collective-permute-start | bytes 1179656 | tf_op jit(solution)/shard_map/ppermute | solution.py:509
  5.4 23.6 %collective-permute-start.4 = (f32[12,64,128]{2,1,0:T(8,128)}, f32[12,64,128]{2,1,0:T(8,128)S(1)}, u32[]{:S(2)}, u32[]{:S(2)}) collective-permute-start(f32[12,64,128]{2,1,0:T(8,128)} %get-tuple-element.32.face), channel_id=1, source_target_pairs={{0,112},{16,32},{32,16},{48,64},{64,48},{80,96},{96,80},{112,0},{1... | collective-permute-start | bytes 1179656 | tf_op jit(solution)/shard_map/ppermute | solution.py:512
  7.7 1.0 %copy-start.3 = (f32[12,64,128]{2,1,0:T(8,128)S(1)}, f32[12,64,128]{2,1,0:T(8,128)}, u32[]{:S(2)}) copy-start(f32[12,64,128]{2,1,0:T(8,128)} %get-tuple-element.32.face) | copy-start | bytes 1179652
  10.5 1.9 %collective-permute-start = (f32[2,64,128]{2,1,0:T(8,128)S(1)}, f32[2,64,128]{2,1,0:T(8,128)S(1)}, u32[]{:S(2)}, u32[]{:S(2)}) collective-permute-start(f32[2,64,128]{2,1,0:T(8,128)S(1)} %shard_map.67.columns), channel_id=1, source_target_pairs={{0,1},{1,0},{2,3},{3,2},{4,5},{5,4},{6,7},{7,6},{8,9},{9,8},{10,11... | collective-permute-start | bytes 196616 | tf_op jit(solution)/shard_map/ppermute | solution.py:509
  12.4 4.0 %collective-permute-start.1 = (f32[2,64,128]{2,1,0:T(8,128)S(1)}, f32[2,64,128]{2,1,0:T(8,128)S(1)}, u32[]{:S(2)}, u32[]{:S(2)}) collective-permute-start(f32[2,64,128]{2,1,0:T(8,128)S(1)} %shard_map.67.columns), channel_id=1, source_target_pairs={{0,15},{1,2},{2,1},{3,4},{4,3},{5,6},{6,5},{7,8},{8,7},{9,10},{10,... | collective-permute-start | bytes 196616 | tf_op jit(solution)/shard_map/ppermute | solution.py:512
  16.4 25.2 %collective-permute-start.2 = (f32[9,64,128]{2,1,0:T(8,128)S(1)}, f32[9,64,128]{2,1,0:T(8,128)S(1)}, u32[]{:S(2)}, u32[]{:S(2)}) collective-permute-start(f32[9,64,128]{2,1,0:T(8,128)S(1)} %get-tuple-element.36), channel_id=1, source_target_pairs={{0,16},{16,0},{32,48},{48,32},{64,80},{80,64},{96,112},{112,96},{1... | collective-permute-start | bytes 884744 | tf_op jit(solution)/shard_map/ppermute | solution.py:509
  16.7 24.8 %collective-permute-start.5 = (f32[9,64,128]{2,1,0:T(8,128)S(1)}, f32[9,64,128]{2,1,0:T(8,128)S(1)}, u32[]{:S(2)}, u32[]{:S(2)}) collective-permute-start(f32[9,64,128]{2,1,0:T(8,128)S(1)} %get-tuple-element.44), channel_id=1, source_target_pairs={{0,112},{16,32},{32,16},{48,64},{64,48},{80,96},{96,80},{112,0},{1... | collective-permute-start | bytes 884744 | tf_op jit(solution)/shard_map/ppermute | solution.py:512
  29.2 28.0 %collective-permute-start.8 = (f32[9,64,128]{2,1,0:T(8,128)S(1)}, f32[9,64,128]{2,1,0:T(8,128)S(1)}, u32[]{:S(2)}, u32[]{:S(2)}) collective-permute-start(f32[9,64,128]{2,1,0:T(8,128)S(1)} %get-tuple-element.39.z_face), channel_id=1, source_target_pairs={{0,16},{16,0},{32,48},{48,32},{64,80},{80,64},{96,112},{112,96},{1... | collective-permute-start | bytes 884744 | tf_op jit(solution)/shard_map/ppermute | solution.py:509
  31.4 25.9 %collective-permute-start.10 = (f32[9,64,128]{2,1,0:T(8,128)S(1)}, f32[9,64,128]{2,1,0:T(8,128)S(1)}, u32[]{:S(2)}, u32[]{:S(2)}) collective-permute-start(f32[9,64,128]{2,1,0:T(8,128)S(1)} %get-tuple-element.40.x_face), channel_id=1, source_target_pairs={{0,112},{16,32},{32,16},{48,64},{64,48},{80,96},{96,80},{112,0},{1... | collective-permute-start | bytes 884744 | tf_op jit(solution)/shard_map/ppermute | solution.py:512
  41.7 15.6 %collective-permute-start.9 = (f32[6,64,128]{2,1,0:T(8,128)S(1)}, f32[6,64,128]{2,1,0:T(8,128)S(1)}, u32[]{:S(2)}, u32[]{:S(2)}) collective-permute-start(f32[6,64,128]{2,1,0:T(8,128)S(1)} %get-tuple-element.45.z_face), channel_id=1, source_target_pairs={{0,16},{16,0},{32,48},{48,32},{64,80},{80,64},{96,112},{112,96},{1... | collective-permute-start | bytes 589832 | tf_op jit(solution)/shard_map/ppermute | solution.py:509
  44.0 13.3 %collective-permute-start.11 = (f32[6,64,128]{2,1,0:T(8,128)S(1)}, f32[6,64,128]{2,1,0:T(8,128)S(1)}, u32[]{:S(2)}, u32[]{:S(2)}) collective-permute-start(f32[6,64,128]{2,1,0:T(8,128)S(1)} %get-tuple-element.46.x_face), channel_id=1, source_target_pairs={{0,112},{16,32},{32,16},{48,64},{64,48},{80,96},{96,80},{112,0},{1... | collective-permute-start | bytes 589832 | tf_op jit(solution)/shard_map/ppermute | solution.py:512
  47.3 3.8 %collective-permute-start.6 = (f32[64,128]{1,0:T(8,128)S(1)}, f32[64,128]{1,0:T(8,128)S(1)}, u32[]{:S(2)}, u32[]{:S(2)}) collective-permute-start(f32[64,128]{1,0:T(8,128)S(1)} %get-tuple-element.49.packed), channel_id=1, source_target_pairs={{0,1},{1,0},{2,3},{3,2},{4,5},{5,4},{6,7},{7,6},{8,9},{9,8},{10,11... | collective-permute-start | bytes 98312 | tf_op jit(solution)/shard_map/ppermute | solution.py:509
  51.1 3.6 %collective-permute-start.7 = (f32[64,128]{1,0:T(8,128)S(1)}, f32[64,128]{1,0:T(8,128)S(1)}, u32[]{:S(2)}, u32[]{:S(2)}) collective-permute-start(f32[64,128]{1,0:T(8,128)S(1)} %get-tuple-element.49.packed), channel_id=1, source_target_pairs={{0,15},{1,2},{2,1},{3,4},{4,3},{5,6},{6,5},{7,8},{8,7},{9,10},{10,... | collective-permute-start | bytes 98312 | tf_op jit(solution)/shard_map/ppermute | solution.py:512
  51.9 3.1 %copy-start.2 = (f32[3,4,64,128]{3,2,1,0:T(8,128)S(1)}, f32[3,4,64,128]{3,2,1,0:T(8,128)}, u32[]{:S(2)}) copy-start(f32[3,4,64,128]{3,2,1,0:T(8,128)} %weight.3) | copy-start | bytes 1179652

commit v4 on v3

--- a/solution.py
+++ b/solution.py
@@ -55,13 +55,11 @@
 def faces_kernel(chosen, t, u, *refs):
     outs, sem = refs[:-1], refs[-1]
     (z_plane, _), (x_plane, _) = sides()
-    last = len(groups) - 1
     copies = []
     for slot, g in enumerate(chosen):
         members = groups[g]
         sources = [(t, 3 * members[0], 3 * len(members))]
         sources += [(u, 0, 3)] if g == 0 else []
-        sources += [(u, 3, 3)] if g == last else []
         for side, plane in ((0, z_plane), (1, x_plane)):
             at = 0
             for ref, start, count in sources:
@@ -259,6 +257,9 @@
     flow_at = 3 * len(groups[0])
     edges = at_edges()
     for (plane, sign), got, flow_got, out in zip(sides(), (z_in, x_in), (z_flow, x_flow), (z_out, x_out)):
+        if g == 0:
+            for i in range(3):
+                out[flow_at + i] = u[3 + i, plane]
         for zt in range(8):
             rows = slice(8 * zt, 8 * zt + 8)
             here = terms[plane, rows]
@@ -382,8 +383,7 @@
 def second_outer_kernel(u, weight, terms, sums_in, z_flow, x_flow, *refs):
     count = len(groups)
     parts, first, z_in, x_in, (z_out, x_out, sums_out) = split_refs(refs, count, count, count, count)
-    last = len(groups) - 1
-    flow_at = 3 * len(groups[last]) + (3 if last == 0 else 0)
+    flow_at = 3 * len(groups[0])
     scale = 0.5 * time_step
     edges = at_edges()
     place = places()
@@ -515,7 +515,7 @@
         return lax.optimization_barrier((values, other))[0]
 
     sizes = [3 * len(members) for members in groups]
-    sent = [s + (3 if g == 0 else 0) + (3 if g == last else 0) for g, s in enumerate(sizes)]
+    sent = [s + (3 if g == 0 else 0) for g, s in enumerate(sizes)]
     def send_buffers(chosen, limit):
         return pl.pallas_call(
             functools.partial(faces_kernel, chosen),
@@ -550,7 +550,7 @@
             z_in[g] = after(z_in[g], halves[-1])
         z_face, x_face = call(
             functools.partial(first_faces_kernel, g),
-            (shaped(sizes[g], 64, 128), shaped(sizes[g], 64, 128)),
+            (shaped(sent[g], 64, 128), shaped(sent[g], 64, 128)),
             (parts[g], terms, t, u, z_in[g], x_in[g], z_in[0], x_in[0]),
         )
         z_next.append(partner(z_face, "gx", count_x))
@@ -581,7 +581,7 @@
     z_face, x_face, line = call(
         second_outer_kernel,
         (shaped(15, 64, 128), shaped(15, 64, 128), shaped(count_x * count_y, 1, 128)),
-        (u, objective_weight, terms, sums, z_in[last], x_in[last], *halves, *first, *z_next, *x_next),
+        (u, objective_weight, terms, sums, z_next[0], x_next[0], *halves, *first, *z_next, *x_next),
     )
     gathered = lax.all_to_all(line, ("gx", "gy"), 0, 0, tiled=True)
     renormed, rfactor, coefficients, objective = pl.pallas_call(

time: 81.3 us -> 81.3 us (level)
  starting transfers between devices: 22 us -> 28.2 us
  waiting for transfers between devices: 20.2 us -> 14.4 us
    ppermute x6, starting transfers between devices: 11.3 us -> 17.8 us  [partner(): return lax.ppermute(values, axis, [(i, i ^ 1) for i in range(count)])]
    ppermute x6, waiting for transfers between devices: 16.5 us -> 12.9 us  [partner(): return lax.ppermute(values, axis, [(i, i ^ 1) for i in range(count)])]
    ppermute x6, waiting for transfers between devices: 3.68 us -> 1.46 us  [beyond(): lax.ppermute(values, axis, [(i, (i + 2 * (i % 2) - 1) % count) for i in r...]
  transfers between devices with their start and end apart: 12 -> 12, of which waited for: 7 -> 5; matrix products, arithmetic and copies ran while one was open for 0% -> 0% of each run, Pallas kernels for 14% -> 14%
where the time goes in v4:
time: 81.3 us; the launch traced here: 81.1 us
  starting transfers between devices  28.2 us (35%)
  blocking collectives  20.5 us (25%)
  Pallas kernels  16.3 us (20%)
  waiting for transfers between devices  14.4 us (18%)
  local copies, waits for them, and re-layouts  1.04 us (1%)
    all_to_all x1, blocking collectives, per_device(): gathered = lax.all_to_all(line, ('gx', 'gy'), 0, 0, tiled=True)  20.5 us
    ppermute x6, starting transfers between devices, partner(): return lax.ppermute(values, axis, [(i, i ^ 1) for i in range(count)])  17.8 us
    ppermute x6, waiting for transfers between devices, partner(): return lax.ppermute(values, axis, [(i, i ^ 1) for i in range(count)])  12.9 us
    pallas_call x12, Pallas kernels, call(): pl.pallas_call(body, out_shape=outs, in_specs=[vmem] * len(args), out_spe...  11.8 us
    ppermute x6, starting transfers between devices, beyond(): lax.ppermute(values, axis, [(i, (i + 2 * (i % 2) - 1) % count) for i in r...  10.5 us
    pallas_call x2, Pallas kernels, send_buffers(): pl.pallas_call(functools.partial(faces_kernel, chosen), out_shape=tuple((...  2.34 us
    pallas_call x1, Pallas kernels, per_device(): pl.pallas_call(functools.partial(renorm_kernel, total_cells), out_shape=(...  2.14 us
  transfers between devices with their start and end apart: 12, of which 5 were waited for; matrix products, arithmetic and copies ran while one was open for 0% of the time, Pallas kernels for 14%

profile of v4, /device:TPU:1, one launch (start us, length us, event | category | flops | bytes accessed | tf_op | source)
XLA Modules:
  0.0 81.1 jit_solution(1497962717518736513)
XLA Ops:
  0.6 0.0 copy-start
  0.6 0.0 copy-start.1
  0.7 2.2 %shard_map.66 = (f32[12,64,128]{2,1,0:T(8,128)}, f32[12,64,128]{2,1,0:T(8,128)}) custom-call(f32[15,4,64,128]{3,2,1,0:T(8,128)} %bitcast.3, f32[6,4,64,128]{3,2,1,0:T(8,128)} %bitcast.11), custom_call_target="tpu_custom_call" | custom-call | tf_op jit(solution)/shard_map/pallas_call | solution.py:520
  2.9 2.5 %collective-permute-start.3 = (f32[12,64,128]{2,1,0:T(8,128)}, f32[12,64,128]{2,1,0:T(8,128)S(1)}, u32[]{:S(2)}, u32[]{:S(2)}) collective-permute-start(f32[12,64,128]{2,1,0:T(8,128)} %get-tuple-element.38), channel_id=1, source_target_pairs={{0,16},{16,0},{32,48},{48,32},{64,80},{80,64},{96,112},{112,96},{1... | collective-permute-start | bytes 1179656 | tf_op jit(solution)/shard_map/ppermute | solution.py:509
  5.4 2.3 %collective-permute-start.4 = (f32[12,64,128]{2,1,0:T(8,128)}, f32[12,64,128]{2,1,0:T(8,128)S(1)}, u32[]{:S(2)}, u32[]{:S(2)}) collective-permute-start(f32[12,64,128]{2,1,0:T(8,128)} %get-tuple-element.32.face), channel_id=1, source_target_pairs={{0,112},{16,32},{32,16},{48,64},{64,48},{80,96},{96,80},{112,0},{1... | collective-permute-start | bytes 1179656 | tf_op jit(solution)/shard_map/ppermute | solution.py:512
  7.7 0.0 copy-done
  7.7 0.0 copy-done.1
  7.7 0.0 copy-start.3
  7.7 1.0 %copy-done.3 = f32[12,64,128]{2,1,0:T(8,128)S(1)} copy-done((f32[12,64,128]{2,1,0:T(8,128)S(1)}, f32[12,64,128]{2,1,0:T(8,128)}, u32[]{:S(2)}) %copy-start.3) | copy-done | bytes 393240
  8.7 1.8 %shard_map.67.columns = f32[2,64,128]{2,1,0:T(8,128)S(1)} custom-call(f32[15,4,64,128]{3,2,1,0:T(8,128)S(1)} %bitcast.4, f32[6,4,64,128]{3,2,1,0:T(8,128)S(1)} %bitcast.12, f32[12,64,128]{2,1,0:T(8,128)S(1)} %copy-done.3), custom_call_target="tpu_custom_call" | custom-call | flops 1000000 | bytes 4000000 | tf_op jit(solution)/shard_map/pallas_call | solution.py:25
  10.5 1.0 %collective-permute-start = (f32[2,64,128]{2,1,0:T(8,128)S(1)}, f32[2,64,128]{2,1,0:T(8,128)S(1)}, u32[]{:S(2)}, u32[]{:S(2)}) collective-permute-start(f32[2,64,128]{2,1,0:T(8,128)S(1)} %shard_map.67.columns), channel_id=1, source_target_pairs={{0,1},{1,0},{2,3},{3,2},{4,5},{5,4},{6,7},{7,6},{8,9},{9,8},{10,11... | collective-permute-start | bytes 196616 | tf_op jit(solution)/shard_map/ppermute | solution.py:509
  11.5 0.9 %collective-permute-done.inner.inner_flow = f32[2,64,128]{2,1,0:T(8,128)S(1)} collective-permute-done((f32[2,64,128]{2,1,0:T(8,128)S(1)}, f32[2,64,128]{2,1,0:T(8,128)S(1)}, u32[]{:S(2)}, u32[]{:S(2)}) %collective-permute-start) | collective-permute-done | bytes 65568 | tf_op jit(solution)/shard_map/ppermute | solution.py:509
  12.4 1.5 %collective-permute-start.1 = (f32[2,64,128]{2,1,0:T(8,128)S(1)}, f32[2,64,128]{2,1,0:T(8,128)S(1)}, u32[]{:S(2)}, u32[]{:S(2)}) collective-permute-start(f32[2,64,128]{2,1,0:T(8,128)S(1)} %shard_map.67.columns), channel_id=1, source_target_pairs={{0,15},{1,2},{2,1},{3,4},{4,3},{5,6},{6,5},{7,8},{8,7},{9,10},{10,... | collective-permute-start | bytes 196616 | tf_op jit(solution)/shard_map/ppermute | solution.py:512
  13.9 0.1 shard_map.70
  14.1 2.4 %shard_map.68 = (f32[9,4,64,128]{3,2,1,0:T(8,128)S(1)}, f32[6,4,64,128]{3,2,1,0:T(8,128)S(1)}) custom-call(f32[15,4,64,128]{3,2,1,0:T(8,128)S(1)} %bitcast.6, f32[6,4,64,128]{3,2,1,0:T(8,128)S(1)} %bitcast.14, f32[2,64,128]{2,1,0:T(8,128)S(1)} %shard_map.67.columns), custom_call_target="tpu_custom_call" | custom-call | flops 10000000 | bytes 4000000 | tf_op jit(solution)/shard_map/pallas_call | solution.py:25
  16.4 0.0 collective-permute-done.1.outer.outer_flow
  16.5 0.4 collective-permute-start.2
  16.9 1.4 %collective-permute-start.5 = (f32[6,64,128]{2,1,0:T(8,128)S(1)}, f32[6,64,128]{2,1,0:T(8,128)S(1)}, u32[]{:S(2)}, u32[]{:S(2)}) collective-permute-start(f32[6,64,128]{2,1,0:T(8,128)S(1)} %get-tuple-element.44), channel_id=1, source_target_pairs={{0,112},{16,32},{32,16},{48,64},{64,48},{80,96},{96,80},{112,0},{1... | collective-permute-start | bytes 589832 | tf_op jit(solution)/shard_map/ppermute | solution.py:512
  18.3 0.3 shard_map.69.terms
  18.6 7.1 %collective-permute-done.3.z_in.z_flow = f32[12,64,128]{2,1,0:T(8,128)S(1)} collective-permute-done((f32[12,64,128]{2,1,0:T(8,128)}, f32[12,64,128]{2,1,0:T(8,128)S(1)}, u32[]{:S(2)}, u32[]{:S(2)}) %collective-permute-start.3) | collective-permute-done | bytes 393248 | tf_op jit(solution)/shard_map/ppermute | solution.py:509
  25.7 0.0 collective-permute-done.4.x_in.x_flow
  25.7 0.2 shard_map.71
  25.9 1.3 %collective-permute-start.8 = (f32[12,64,128]{2,1,0:T(8,128)S(1)}, f32[12,64,128]{2,1,0:T(8,128)S(1)}, u32[]{:S(2)}, u32[]{:S(2)}) collective-permute-start(f32[12,64,128]{2,1,0:T(8,128)S(1)} %get-tuple-element.39.z_face), channel_id=1, source_target_pairs={{0,16},{16,0},{32,48},{48,32},{64,80},{80,64},{96,112},{112,96},{1... | collective-permute-start | bytes 1179656 | tf_op jit(solution)/shard_map/ppermute | solution.py:509
  27.2 4.5 %collective-permute-start.9 = (f32[12,64,128]{2,1,0:T(8,128)S(1)}, f32[12,64,128]{2,1,0:T(8,128)S(1)}, u32[]{:S(2)}, u32[]{:S(2)}) collective-permute-start(f32[12,64,128]{2,1,0:T(8,128)S(1)} %get-tuple-element.40.x_face), channel_id=1, source_target_pairs={{0,112},{16,32},{32,16},{48,64},{64,48},{80,96},{96,80},{112,0},{1... | collective-permute-start | bytes 1179656 | tf_op jit(solution)/shard_map/ppermute | solution.py:512
  31.7 1.1 %shard_map.72 = (f32[9,4,64,128]{3,2,1,0:T(8,128)S(1)}, f32[64,128]{1,0:T(8,128)S(1)}) custom-call(f32[9,4,64,128]{3,2,1,0:T(8,128)S(1)} %get-tuple-element.37.part, f32[4,64,128]{2,1,0:T(8,128)S(1)} %shard_map.69.terms, f32[12,64,128]{2,1,0:T(8,128)S(1)} %get-tuple-element.39.z_face, f32[12,64,128]{2,1,0:T(8,128)S(1)} %get-tuple-element.40.x_face), custom_call_target="tpu_custom_call" | custom-call | flops 1000000 | bytes 4000000 | tf_op jit(solution)/shard_map/pallas_call | solution.py:25
  32.8 1.7 %shard_map.73.refs_0_ = f32[9,4,64,128]{3,2,1,0:T(8,128)S(1)} custom-call(f32[15,4,64,128]{3,2,1,0:T(8,128)S(1)} %bitcast.8, f32[6,4,64,128]{3,2,1,0:T(8,128)S(1)} %bitcast.16, f32[9,4,64,128]{3,2,1,0:T(8,128)S(1)} %get-tuple-element.41.first.refs_2_), custom_call_target="tpu_custom_call" | custom-call | flops 5000000 | bytes 4000000 | tf_op jit(solution)/shard_map/pallas_call | solution.py:25
  34.5 0.0 collective-permute-done.2.z_in
  34.5 0.0 collective-permute-done.5.x_in
  34.5 0.2 shard_map.74
  34.7 7.2 %collective-permute-start.10 = (f32[6,64,128]{2,1,0:T(8,128)S(1)}, f32[6,64,128]{2,1,0:T(8,128)S(1)}, u32[]{:S(2)}, u32[]{:S(2)}) collective-permute-start(f32[6,64,128]{2,1,0:T(8,128)S(1)} %get-tuple-element.45.z_face), channel_id=1, source_target_pairs={{0,16},{16,0},{32,48},{48,32},{64,80},{80,64},{96,112},{112,96},{1... | collective-permute-start | bytes 589832 | tf_op jit(solution)/shard_map/ppermute | solution.py:509
  41.9 0.0 collective-permute-start.11
  41.9 0.9 %shard_map.75 = (f32[6,4,64,128]{3,2,1,0:T(8,128)S(1)}, f32[64,128]{1,0:T(8,128)S(1)}) custom-call(f32[6,4,64,128]{3,2,1,0:T(8,128)S(1)} %get-tuple-element.33.part, f32[4,64,128]{2,1,0:T(8,128)S(1)} %shard_map.69.terms, f32[6,64,128]{2,1,0:T(8,128)S(1)} %get-tuple-element.45.z_face, f32[6,64,128]{2,1,0:T(8,128)S(1)} %get-tuple-element.46.x_face, ...), custom_call_target="tpu_custom_call" | custom-call | flops 1000000 | bytes 4000000 | tf_op jit(solution)/shard_map/pallas_call | solution.py:25
  42.8 5.3 %collective-permute-start.6 = (f32[64,128]{1,0:T(8,128)S(1)}, f32[64,128]{1,0:T(8,128)S(1)}, u32[]{:S(2)}, u32[]{:S(2)}) collective-permute-start(f32[64,128]{1,0:T(8,128)S(1)} %get-tuple-element.49.packed), channel_id=1, source_target_pairs={{0,1},{1,0},{2,3},{3,2},{4,5},{5,4},{6,7},{7,6},{8,9},{9,8},{10,11... | collective-permute-start | bytes 98312 | tf_op jit(solution)/shard_map/ppermute | solution.py:509
  48.1 0.9 %collective-permute-done.6.inner = f32[64,128]{1,0:T(8,128)S(1)} collective-permute-done((f32[64,128]{1,0:T(8,128)S(1)}, f32[64,128]{1,0:T(8,128)S(1)}, u32[]{:S(2)}, u32[]{:S(2)}) %collective-permute-start.6) | collective-permute-done | bytes 32800 | tf_op jit(solution)/shard_map/ppermute | solution.py:509
  49.0 0.8 %collective-permute-start.7 = (f32[64,128]{1,0:T(8,128)S(1)}, f32[64,128]{1,0:T(8,128)S(1)}, u32[]{:S(2)}, u32[]{:S(2)}) collective-permute-start(f32[64,128]{1,0:T(8,128)S(1)} %get-tuple-element.49.packed), channel_id=1, source_target_pairs={{0,15},{1,2},{2,1},{3,4},{4,3},{5,6},{6,5},{7,8},{8,7},{9,10},{10,... | collective-permute-start | bytes 98312 | tf_op jit(solution)/shard_map/ppermute | solution.py:512
  49.8 0.0 copy-start.2
  49.8 1.3 %shard_map.77.refs_1_ = f32[6,4,64,128]{3,2,1,0:T(8,128)S(1)} custom-call(f32[15,4,64,128]{3,2,1,0:T(8,128)S(1)} %bitcast.10, f32[6,4,64,128]{3,2,1,0:T(8,128)S(1)} %bitcast.18, f32[6,4,64,128]{3,2,1,0:T(8,128)S(1)} %get-tuple-element.50.first.refs_3_), custom_call_target="tpu_custom_call" | custom-call | flops 5000000 | bytes 4000000 | tf_op jit(solution)/shard_map/pallas_call | solution.py:25
  51.1 1.4 %collective-permute-done.7.outer = f32[64,128]{1,0:T(8,128)S(1)} collective-permute-done((f32[64,128]{1,0:T(8,128)S(1)}, f32[64,128]{1,0:T(8,128)S(1)}, u32[]{:S(2)}, u32[]{:S(2)}) %collective-permute-start.7) | collective-permute-done | bytes 32800 | tf_op jit(solution)/shard_map/ppermute | solution.py:512
  52.6 0.3 shard_map.76.terms
  52.9 0.0 copy-done.2
  52.9 0.6 shard_map.78
  53.6 4.1 %collective-permute-done.10.refs_5_ = f32[6,64,128]{2,1,0:T(8,128)S(1)} collective-permute-done((f32[6,64,128]{2,1,0:T(8,128)S(1)}, f32[6,64,128]{2,1,0:T(8,128)S(1)}, u32[]{:S(2)}, u32[]{:S(2)}) %collective-permute-start.10) | collective-permute-done | bytes 196640 | tf_op jit(solution)/shard_map/ppermute | solution.py:509
  57.6 0.0 collective-permute-done.11.refs_7_
  57.6 0.0 collective-permute-done.8.z_flow.refs_4_
  57.6 0.0 collective-permute-done.9.x_flow.refs_6_
  57.6 0.9 %shard_map.79 = (f32[15,64,128]{2,1,0:T(8,128)S(1)}, f32[15,64,128]{2,1,0:T(8,128)S(1)}, f32[128,1,128]{2,1,0:T(1,128)S(1)}) custom-call(f32[6,4,64,128]{3,2,1,0:T(8,128)S(1)} %bitcast.19, f32[3,4,64,128]{3,2,1,0:T(8,128)S(1)} %copy-done.2, f32[4,64,128]{2,1,0:T(8,128)S(1)} %shard_map.76.terms, f32[20,8,128]{2,1,0:T(8,128)S(1)} %get-tuple-element.52.sums_in, ...), custom_call_target="tpu_custom_call" | custom-call | flops 1000000 | bytes 4000000 | tf_op jit(solution)/shard_map/pallas_call | solution.py:25
  58.5 20.5 %all_to_all.5.gathered = f32[128,1,128]{2,1,0:T(1,128)S(1)} all-to-all(f32[128,1,128]{2,1,0:T(1,128)S(1)} %get-tuple-element.55), channel_id=1, replica_groups=mesh['gx'=8,'gy'=16] {'gx','gy'}, dimensions={0} | all-to-all | bytes 131072 | tf_op jit(solution)/shard_map/all_to_all | solution.py:586
  79.0 2.1 %shard_map.80 = (f32[15,4,64,128]{3,2,1,0:T(8,128)}, f32[4,4]{1,0:T(4,128)}, f32[4]{0:T(128)}, f32[5]{0:T(128)}) custom-call(f32[15,2,64,128]{3,2,1,0:T(8,128)S(1)} %get-tuple-element.51.inside, f32[15,64,128]{2,1,0:T(8,128)S(1)} %get-tuple-element.53.z_face, f32[15,64,128]{2,1,0:T(8,128)S(1)} %get-tuple-element.54.x_face, f32[128,1,128]{2,1,0:T(1,128)S(1)} %all_to_all.5.gathered), custom_call_target="tpu_custom_call" | custom-call | tf_op jit(solution)/shard_map/pallas_call | solution.py:587
Async XLA Ops:
  0.6 7.1 %copy-start = (f32[5,3,4,64,128]{4,3,2,1,0:T(8,128)S(1)}, f32[5,3,4,64,128]{4,3,2,1,0:T(8,128)}, u32[]{:S(2)}) copy-start(f32[5,3,4,64,128]{4,3,2,1,0:T(8,128)} %param.3) | copy-start | bytes 5898244
  0.6 7.1 %copy-start.1 = (f32[2,3,4,64,128]{4,3,2,1,0:T(8,128)S(1)}, f32[2,3,4,64,128]{4,3,2,1,0:T(8,128)}, u32[]{:S(2)}) copy-start(f32[2,3,4,64,128]{4,3,2,1,0:T(8,128)} %param.4) | copy-start | bytes 2359300
  2.9 22.8 %collective-permute-start.3 = (f32[12,64,128]{2,1,0:T(8,128)}, f32[12,64,128]{2,1,0:T(8,128)S(1)}, u32[]{:S(2)}, u32[]{:S(2)}) collective-permute-start(f32[12,64,128]{2,1,0:T(8,128)} %get-tuple-element.38), channel_id=1, source_target_pairs={{0,16},{16,0},{32,48},{48,32},{64,80},{80,64},{96,112},{112,96},{1... | collective-permute-start | bytes 1179656 | tf_op jit(solution)/shard_map/ppermute | solution.py:509
  5.4 20.3 %collective-permute-start.4 = (f32[12,64,128]{2,1,0:T(8,128)}, f32[12,64,128]{2,1,0:T(8,128)S(1)}, u32[]{:S(2)}, u32[]{:S(2)}) collective-permute-start(f32[12,64,128]{2,1,0:T(8,128)} %get-tuple-element.32.face), channel_id=1, source_target_pairs={{0,112},{16,32},{32,16},{48,64},{64,48},{80,96},{96,80},{112,0},{1... | collective-permute-start | bytes 1179656 | tf_op jit(solution)/shard_map/ppermute | solution.py:512
  7.7 1.0 %copy-start.3 = (f32[12,64,128]{2,1,0:T(8,128)S(1)}, f32[12,64,128]{2,1,0:T(8,128)}, u32[]{:S(2)}) copy-start(f32[12,64,128]{2,1,0:T(8,128)} %get-tuple-element.32.face) | copy-start | bytes 1179652
  10.5 1.9 %collective-permute-start = (f32[2,64,128]{2,1,0:T(8,128)S(1)}, f32[2,64,128]{2,1,0:T(8,128)S(1)}, u32[]{:S(2)}, u32[]{:S(2)}) collective-permute-start(f32[2,64,128]{2,1,0:T(8,128)S(1)} %shard_map.67.columns), channel_id=1, source_target_pairs={{0,1},{1,0},{2,3},{3,2},{4,5},{5,4},{6,7},{7,6},{8,9},{9,8},{10,11... | collective-permute-start | bytes 196616 | tf_op jit(solution)/shard_map/ppermute | solution.py:509
  12.4 4.1 %collective-permute-start.1 = (f32[2,64,128]{2,1,0:T(8,128)S(1)}, f32[2,64,128]{2,1,0:T(8,128)S(1)}, u32[]{:S(2)}, u32[]{:S(2)}) collective-permute-start(f32[2,64,128]{2,1,0:T(8,128)S(1)} %shard_map.67.columns), channel_id=1, source_target_pairs={{0,15},{1,2},{2,1},{3,4},{4,3},{5,6},{6,5},{7,8},{8,7},{9,10},{10,... | collective-permute-start | bytes 196616 | tf_op jit(solution)/shard_map/ppermute | solution.py:512
  16.5 18.0 %collective-permute-start.2 = (f32[6,64,128]{2,1,0:T(8,128)S(1)}, f32[6,64,128]{2,1,0:T(8,128)S(1)}, u32[]{:S(2)}, u32[]{:S(2)}) collective-permute-start(f32[6,64,128]{2,1,0:T(8,128)S(1)} %get-tuple-element.36), channel_id=1, source_target_pairs={{0,16},{16,0},{32,48},{48,32},{64,80},{80,64},{96,112},{112,96},{1... | collective-permute-start | bytes 589832 | tf_op jit(solution)/shard_map/ppermute | solution.py:509
  16.9 17.6 %collective-permute-start.5 = (f32[6,64,128]{2,1,0:T(8,128)S(1)}, f32[6,64,128]{2,1,0:T(8,128)S(1)}, u32[]{:S(2)}, u32[]{:S(2)}) collective-permute-start(f32[6,64,128]{2,1,0:T(8,128)S(1)} %get-tuple-element.44), channel_id=1, source_target_pairs={{0,112},{16,32},{32,16},{48,64},{64,48},{80,96},{96,80},{112,0},{1... | collective-permute-start | bytes 589832 | tf_op jit(solution)/shard_map/ppermute | solution.py:512
  25.9 31.7 %collective-permute-start.8 = (f32[12,64,128]{2,1,0:T(8,128)S(1)}, f32[12,64,128]{2,1,0:T(8,128)S(1)}, u32[]{:S(2)}, u32[]{:S(2)}) collective-permute-start(f32[12,64,128]{2,1,0:T(8,128)S(1)} %get-tuple-element.39.z_face), channel_id=1, source_target_pairs={{0,16},{16,0},{32,48},{48,32},{64,80},{80,64},{96,112},{112,96},{1... | collective-permute-start | bytes 1179656 | tf_op jit(solution)/shard_map/ppermute | solution.py:509
  27.2 30.4 %collective-permute-start.9 = (f32[12,64,128]{2,1,0:T(8,128)S(1)}, f32[12,64,128]{2,1,0:T(8,128)S(1)}, u32[]{:S(2)}, u32[]{:S(2)}) collective-permute-start(f32[12,64,128]{2,1,0:T(8,128)S(1)} %get-tuple-element.40.x_face), channel_id=1, source_target_pairs={{0,112},{16,32},{32,16},{48,64},{64,48},{80,96},{96,80},{112,0},{1... | collective-permute-start | bytes 1179656 | tf_op jit(solution)/shard_map/ppermute | solution.py:512
  34.7 22.9 %collective-permute-start.10 = (f32[6,64,128]{2,1,0:T(8,128)S(1)}, f32[6,64,128]{2,1,0:T(8,128)S(1)}, u32[]{:S(2)}, u32[]{:S(2)}) collective-permute-start(f32[6,64,128]{2,1,0:T(8,128)S(1)} %get-tuple-element.45.z_face), channel_id=1, source_target_pairs={{0,16},{16,0},{32,48},{48,32},{64,80},{80,64},{96,112},{112,96},{1... | collective-permute-start | bytes 589832 | tf_op jit(solution)/shard_map/ppermute | solution.py:509
  41.9 15.7 %collective-permute-start.11 = (f32[6,64,128]{2,1,0:T(8,128)S(1)}, f32[6,64,128]{2,1,0:T(8,128)S(1)}, u32[]{:S(2)}, u32[]{:S(2)}) collective-permute-start(f32[6,64,128]{2,1,0:T(8,128)S(1)} %get-tuple-element.46.x_face), channel_id=1, source_target_pairs={{0,112},{16,32},{32,16},{48,64},{64,48},{80,96},{96,80},{112,0},{1... | collective-permute-start | bytes 589832 | tf_op jit(solution)/shard_map/ppermute | solution.py:512
  42.8 6.1 %collective-permute-start.6 = (f32[64,128]{1,0:T(8,128)S(1)}, f32[64,128]{1,0:T(8,128)S(1)}, u32[]{:S(2)}, u32[]{:S(2)}) collective-permute-start(f32[64,128]{1,0:T(8,128)S(1)} %get-tuple-element.49.packed), channel_id=1, source_target_pairs={{0,1},{1,0},{2,3},{3,2},{4,5},{5,4},{6,7},{7,6},{8,9},{9,8},{10,11... | collective-permute-start | bytes 98312 | tf_op jit(solution)/shard_map/ppermute | solution.py:509
  49.0 3.6 %collective-permute-start.7 = (f32[64,128]{1,0:T(8,128)S(1)}, f32[64,128]{1,0:T(8,128)S(1)}, u32[]{:S(2)}, u32[]{:S(2)}) collective-permute-start(f32[64,128]{1,0:T(8,128)S(1)} %get-tuple-element.49.packed), channel_id=1, source_target_pairs={{0,15},{1,2},{2,1},{3,4},{4,3},{5,6},{6,5},{7,8},{8,7},{9,10},{10,... | collective-permute-start | bytes 98312 | tf_op jit(solution)/shard_map/ppermute | solution.py:512
  49.8 3.1 %copy-start.2 = (f32[3,4,64,128]{3,2,1,0:T(8,128)S(1)}, f32[3,4,64,128]{3,2,1,0:T(8,128)}, u32[]{:S(2)}) copy-start(f32[3,4,64,128]{3,2,1,0:T(8,128)} %weight.3) | copy-start | bytes 1179652

commit v5 on v4

--- a/solution.py
+++ b/solution.py
@@ -540,8 +540,8 @@
         flops=10000000,
     )
     for g in range(1, len(groups)):
-        z_in.append(partner(after(faces[2 * g], outer_in), "gx", count_x))
-        x_in.append(beyond(after(faces[2 * g + 1], outer_in), "gx", count_x))
+        z_in.append(partner(after(faces[2 * g], inner_in), "gx", count_x))
+        x_in.append(beyond(after(faces[2 * g + 1], inner_in), "gx", count_x))
     terms = call(first_terms_kernel, shaped(4, 64, 128), (columns, inner_in, outer_in))
     first, halves, z_next, x_next = [], [], [], []
     packed = ()

time: 81.3 us -> 81.3 us (level)
  no operation moved by 1% of the time
where the time goes in v5:
time: 81.3 us; the launch traced here: 81.1 us
  starting transfers between devices  28.2 us (35%)
  blocking collectives  20.5 us (25%)
  Pallas kernels  16.3 us (20%)
  waiting for transfers between devices  14.4 us (18%)
  local copies, waits for them, and re-layouts  1.04 us (1%)
    all_to_all x1, blocking collectives, per_device(): gathered = lax.all_to_all(line, ('gx', 'gy'), 0, 0, tiled=True)  20.5 us
    ppermute x6, starting transfers between devices, partner(): return lax.ppermute(values, axis, [(i, i ^ 1) for i in range(count)])  17.8 us
    ppermute x6, waiting for transfers between devices, partner(): return lax.ppermute(values, axis, [(i, i ^ 1) for i in range(count)])  12.9 us
    pallas_call x12, Pallas kernels, call(): pl.pallas_call(body, out_shape=outs, in_specs=[vmem] * len(args), out_spe...  11.8 us
    ppermute x6, starting transfers between devices, beyond(): lax.ppermute(values, axis, [(i, (i + 2 * (i % 2) - 1) % count) for i in r...  10.5 us
    pallas_call x2, Pallas kernels, send_buffers(): pl.pallas_call(functools.partial(faces_kernel, chosen), out_shape=tuple((...  2.34 us
    pallas_call x1, Pallas kernels, per_device(): pl.pallas_call(functools.partial(renorm_kernel, total_cells), out_shape=(...  2.14 us
  transfers between devices with their start and end apart: 12, of which 5 were waited for; matrix products, arithmetic and copies ran while one was open for 0% of the time, Pallas kernels for 14%

profile of v5, /device:TPU:1, one launch (start us, length us, event | category | flops | bytes accessed | tf_op | source)
XLA Modules:
  0.0 81.1 jit_solution(14295839131682291382)
XLA Ops:
  0.6 0.0 copy-start
  0.6 0.0 copy-start.1
  0.7 2.2 %shard_map.66 = (f32[12,64,128]{2,1,0:T(8,128)}, f32[12,64,128]{2,1,0:T(8,128)}) custom-call(f32[15,4,64,128]{3,2,1,0:T(8,128)} %bitcast.3, f32[6,4,64,128]{3,2,1,0:T(8,128)} %bitcast.11), custom_call_target="tpu_custom_call" | custom-call | tf_op jit(solution)/shard_map/pallas_call | solution.py:520
  2.9 2.5 %collective-permute-start.3 = (f32[12,64,128]{2,1,0:T(8,128)}, f32[12,64,128]{2,1,0:T(8,128)S(1)}, u32[]{:S(2)}, u32[]{:S(2)}) collective-permute-start(f32[12,64,128]{2,1,0:T(8,128)} %get-tuple-element.38), channel_id=1, source_target_pairs={{0,16},{16,0},{32,48},{48,32},{64,80},{80,64},{96,112},{112,96},{1... | collective-permute-start | bytes 1179656 | tf_op jit(solution)/shard_map/ppermute | solution.py:509
  5.4 2.3 %collective-permute-start.4 = (f32[12,64,128]{2,1,0:T(8,128)}, f32[12,64,128]{2,1,0:T(8,128)S(1)}, u32[]{:S(2)}, u32[]{:S(2)}) collective-permute-start(f32[12,64,128]{2,1,0:T(8,128)} %get-tuple-element.32.face), channel_id=1, source_target_pairs={{0,112},{16,32},{32,16},{48,64},{64,48},{80,96},{96,80},{112,0},{1... | collective-permute-start | bytes 1179656 | tf_op jit(solution)/shard_map/ppermute | solution.py:512
  7.7 0.0 copy-done
  7.7 0.0 copy-done.1
  7.7 0.0 copy-start.3
  7.7 1.0 %copy-done.3 = f32[12,64,128]{2,1,0:T(8,128)S(1)} copy-done((f32[12,64,128]{2,1,0:T(8,128)S(1)}, f32[12,64,128]{2,1,0:T(8,128)}, u32[]{:S(2)}) %copy-start.3) | copy-done | bytes 393240
  8.7 1.8 %shard_map.67.columns = f32[2,64,128]{2,1,0:T(8,128)S(1)} custom-call(f32[15,4,64,128]{3,2,1,0:T(8,128)S(1)} %bitcast.4, f32[6,4,64,128]{3,2,1,0:T(8,128)S(1)} %bitcast.12, f32[12,64,128]{2,1,0:T(8,128)S(1)} %copy-done.3), custom_call_target="tpu_custom_call" | custom-call | flops 1000000 | bytes 4000000 | tf_op jit(solution)/shard_map/pallas_call | solution.py:25
  10.5 1.0 %collective-permute-start = (f32[2,64,128]{2,1,0:T(8,128)S(1)}, f32[2,64,128]{2,1,0:T(8,128)S(1)}, u32[]{:S(2)}, u32[]{:S(2)}) collective-permute-start(f32[2,64,128]{2,1,0:T(8,128)S(1)} %shard_map.67.columns), channel_id=1, source_target_pairs={{0,1},{1,0},{2,3},{3,2},{4,5},{5,4},{6,7},{7,6},{8,9},{9,8},{10,11... | collective-permute-start | bytes 196616 | tf_op jit(solution)/shard_map/ppermute | solution.py:509
  11.5 0.9 %collective-permute-done.inner.inner_flow = f32[2,64,128]{2,1,0:T(8,128)S(1)} collective-permute-done((f32[2,64,128]{2,1,0:T(8,128)S(1)}, f32[2,64,128]{2,1,0:T(8,128)S(1)}, u32[]{:S(2)}, u32[]{:S(2)}) %collective-permute-start) | collective-permute-done | bytes 65568 | tf_op jit(solution)/shard_map/ppermute | solution.py:509
  12.4 1.5 %collective-permute-start.1 = (f32[2,64,128]{2,1,0:T(8,128)S(1)}, f32[2,64,128]{2,1,0:T(8,128)S(1)}, u32[]{:S(2)}, u32[]{:S(2)}) collective-permute-start(f32[2,64,128]{2,1,0:T(8,128)S(1)} %shard_map.67.columns), channel_id=1, source_target_pairs={{0,15},{1,2},{2,1},{3,4},{4,3},{5,6},{6,5},{7,8},{8,7},{9,10},{10,... | collective-permute-start | bytes 196616 | tf_op jit(solution)/shard_map/ppermute | solution.py:512
  13.9 0.1 shard_map.70
  14.1 2.4 %shard_map.68 = (f32[9,4,64,128]{3,2,1,0:T(8,128)S(1)}, f32[6,4,64,128]{3,2,1,0:T(8,128)S(1)}) custom-call(f32[15,4,64,128]{3,2,1,0:T(8,128)S(1)} %bitcast.6, f32[6,4,64,128]{3,2,1,0:T(8,128)S(1)} %bitcast.14, f32[2,64,128]{2,1,0:T(8,128)S(1)} %shard_map.67.columns), custom_call_target="tpu_custom_call" | custom-call | flops 10000000 | bytes 4000000 | tf_op jit(solution)/shard_map/pallas_call | solution.py:25
  16.4 0.4 collective-permute-start.2
  16.9 1.4 %collective-permute-start.5 = (f32[6,64,128]{2,1,0:T(8,128)S(1)}, f32[6,64,128]{2,1,0:T(8,128)S(1)}, u32[]{:S(2)}, u32[]{:S(2)}) collective-permute-start(f32[6,64,128]{2,1,0:T(8,128)S(1)} %get-tuple-element.44), channel_id=1, source_target_pairs={{0,112},{16,32},{32,16},{48,64},{64,48},{80,96},{96,80},{112,0},{1... | collective-permute-start | bytes 589832 | tf_op jit(solution)/shard_map/ppermute | solution.py:512
  18.3 0.0 collective-permute-done.1.outer.outer_flow
  18.3 0.3 shard_map.69.terms
  18.6 7.1 %collective-permute-done.3.z_in.z_flow = f32[12,64,128]{2,1,0:T(8,128)S(1)} collective-permute-done((f32[12,64,128]{2,1,0:T(8,128)}, f32[12,64,128]{2,1,0:T(8,128)S(1)}, u32[]{:S(2)}, u32[]{:S(2)}) %collective-permute-start.3) | collective-permute-done | bytes 393248 | tf_op jit(solution)/shard_map/ppermute | solution.py:509
  25.7 0.0 collective-permute-done.4.x_in.x_flow
  25.7 0.2 shard_map.71
  25.9 1.3 %collective-permute-start.8 = (f32[12,64,128]{2,1,0:T(8,128)S(1)}, f32[12,64,128]{2,1,0:T(8,128)S(1)}, u32[]{:S(2)}, u32[]{:S(2)}) collective-permute-start(f32[12,64,128]{2,1,0:T(8,128)S(1)} %get-tuple-element.39.z_face), channel_id=1, source_target_pairs={{0,16},{16,0},{32,48},{48,32},{64,80},{80,64},{96,112},{112,96},{1... | collective-permute-start | bytes 1179656 | tf_op jit(solution)/shard_map/ppermute | solution.py:509
  27.2 4.5 %collective-permute-start.9 = (f32[12,64,128]{2,1,0:T(8,128)S(1)}, f32[12,64,128]{2,1,0:T(8,128)S(1)}, u32[]{:S(2)}, u32[]{:S(2)}) collective-permute-start(f32[12,64,128]{2,1,0:T(8,128)S(1)} %get-tuple-element.40.x_face), channel_id=1, source_target_pairs={{0,112},{16,32},{32,16},{48,64},{64,48},{80,96},{96,80},{112,0},{1... | collective-permute-start | bytes 1179656 | tf_op jit(solution)/shard_map/ppermute | solution.py:512
  31.7 1.1 %shard_map.72 = (f32[9,4,64,128]{3,2,1,0:T(8,128)S(1)}, f32[64,128]{1,0:T(8,128)S(1)}) custom-call(f32[9,4,64,128]{3,2,1,0:T(8,128)S(1)} %get-tuple-element.37.part, f32[4,64,128]{2,1,0:T(8,128)S(1)} %shard_map.69.terms, f32[12,64,128]{2,1,0:T(8,128)S(1)} %get-tuple-element.39.z_face, f32[12,64,128]{2,1,0:T(8,128)S(1)} %get-tuple-element.40.x_face), custom_call_target="tpu_custom_call" | custom-call | flops 1000000 | bytes 4000000 | tf_op jit(solution)/shard_map/pallas_call | solution.py:25
  32.8 1.7 %shard_map.73.refs_0_ = f32[9,4,64,128]{3,2,1,0:T(8,128)S(1)} custom-call(f32[15,4,64,128]{3,2,1,0:T(8,128)S(1)} %bitcast.8, f32[6,4,64,128]{3,2,1,0:T(8,128)S(1)} %bitcast.16, f32[9,4,64,128]{3,2,1,0:T(8,128)S(1)} %get-tuple-element.41.first.refs_2_), custom_call_target="tpu_custom_call" | custom-call | flops 5000000 | bytes 4000000 | tf_op jit(solution)/shard_map/pallas_call | solution.py:25
  34.5 0.0 collective-permute-done.2.z_in
  34.5 0.0 collective-permute-done.5.x_in
  34.5 0.2 shard_map.74
  34.7 7.2 %collective-permute-start.10 = (f32[6,64,128]{2,1,0:T(8,128)S(1)}, f32[6,64,128]{2,1,0:T(8,128)S(1)}, u32[]{:S(2)}, u32[]{:S(2)}) collective-permute-start(f32[6,64,128]{2,1,0:T(8,128)S(1)} %get-tuple-element.45.z_face), channel_id=1, source_target_pairs={{0,16},{16,0},{32,48},{48,32},{64,80},{80,64},{96,112},{112,96},{1... | collective-permute-start | bytes 589832 | tf_op jit(solution)/shard_map/ppermute | solution.py:509
  41.9 0.0 collective-permute-start.11
  41.9 0.9 %shard_map.75 = (f32[6,4,64,128]{3,2,1,0:T(8,128)S(1)}, f32[64,128]{1,0:T(8,128)S(1)}) custom-call(f32[6,4,64,128]{3,2,1,0:T(8,128)S(1)} %get-tuple-element.33.part, f32[4,64,128]{2,1,0:T(8,128)S(1)} %shard_map.69.terms, f32[6,64,128]{2,1,0:T(8,128)S(1)} %get-tuple-element.45.z_face, f32[6,64,128]{2,1,0:T(8,128)S(1)} %get-tuple-element.46.x_face, ...), custom_call_target="tpu_custom_call" | custom-call | flops 1000000 | bytes 4000000 | tf_op jit(solution)/shard_map/pallas_call | solution.py:25
  42.8 5.3 %collective-permute-start.6 = (f32[64,128]{1,0:T(8,128)S(1)}, f32[64,128]{1,0:T(8,128)S(1)}, u32[]{:S(2)}, u32[]{:S(2)}) collective-permute-start(f32[64,128]{1,0:T(8,128)S(1)} %get-tuple-element.49.packed), channel_id=1, source_target_pairs={{0,1},{1,0},{2,3},{3,2},{4,5},{5,4},{6,7},{7,6},{8,9},{9,8},{10,11... | collective-permute-start | bytes 98312 | tf_op jit(solution)/shard_map/ppermute | solution.py:509
  48.1 0.9 %collective-permute-done.6.inner = f32[64,128]{1,0:T(8,128)S(1)} collective-permute-done((f32[64,128]{1,0:T(8,128)S(1)}, f32[64,128]{1,0:T(8,128)S(1)}, u32[]{:S(2)}, u32[]{:S(2)}) %collective-permute-start.6) | collective-permute-done | bytes 32800 | tf_op jit(solution)/shard_map/ppermute | solution.py:509
  49.0 0.8 %collective-permute-start.7 = (f32[64,128]{1,0:T(8,128)S(1)}, f32[64,128]{1,0:T(8,128)S(1)}, u32[]{:S(2)}, u32[]{:S(2)}) collective-permute-start(f32[64,128]{1,0:T(8,128)S(1)} %get-tuple-element.49.packed), channel_id=1, source_target_pairs={{0,15},{1,2},{2,1},{3,4},{4,3},{5,6},{6,5},{7,8},{8,7},{9,10},{10,... | collective-permute-start | bytes 98312 | tf_op jit(solution)/shard_map/ppermute | solution.py:512
  49.8 0.0 copy-start.2
  49.8 1.3 %shard_map.77.refs_1_ = f32[6,4,64,128]{3,2,1,0:T(8,128)S(1)} custom-call(f32[15,4,64,128]{3,2,1,0:T(8,128)S(1)} %bitcast.10, f32[6,4,64,128]{3,2,1,0:T(8,128)S(1)} %bitcast.18, f32[6,4,64,128]{3,2,1,0:T(8,128)S(1)} %get-tuple-element.50.first.refs_3_), custom_call_target="tpu_custom_call" | custom-call | flops 5000000 | bytes 4000000 | tf_op jit(solution)/shard_map/pallas_call | solution.py:25
  51.1 1.4 %collective-permute-done.7.outer = f32[64,128]{1,0:T(8,128)S(1)} collective-permute-done((f32[64,128]{1,0:T(8,128)S(1)}, f32[64,128]{1,0:T(8,128)S(1)}, u32[]{:S(2)}, u32[]{:S(2)}) %collective-permute-start.7) | collective-permute-done | bytes 32800 | tf_op jit(solution)/shard_map/ppermute | solution.py:512
  52.6 0.3 shard_map.76.terms
  52.9 0.0 copy-done.2
  52.9 0.6 shard_map.78
  53.6 4.1 %collective-permute-done.10.refs_5_ = f32[6,64,128]{2,1,0:T(8,128)S(1)} collective-permute-done((f32[6,64,128]{2,1,0:T(8,128)S(1)}, f32[6,64,128]{2,1,0:T(8,128)S(1)}, u32[]{:S(2)}, u32[]{:S(2)}) %collective-permute-start.10) | collective-permute-done | bytes 196640 | tf_op jit(solution)/shard_map/ppermute | solution.py:509
  57.6 0.0 collective-permute-done.11.refs_7_
  57.6 0.0 collective-permute-done.8.z_flow.refs_4_
  57.6 0.0 collective-permute-done.9.x_flow.refs_6_
  57.6 0.9 %shard_map.79 = (f32[15,64,128]{2,1,0:T(8,128)S(1)}, f32[15,64,128]{2,1,0:T(8,128)S(1)}, f32[128,1,128]{2,1,0:T(1,128)S(1)}) custom-call(f32[6,4,64,128]{3,2,1,0:T(8,128)S(1)} %bitcast.19, f32[3,4,64,128]{3,2,1,0:T(8,128)S(1)} %copy-done.2, f32[4,64,128]{2,1,0:T(8,128)S(1)} %shard_map.76.terms, f32[20,8,128]{2,1,0:T(8,128)S(1)} %get-tuple-element.52.sums_in, ...), custom_call_target="tpu_custom_call" | custom-call | flops 1000000 | bytes 4000000 | tf_op jit(solution)/shard_map/pallas_call | solution.py:25
  58.5 20.5 %all_to_all.5.gathered = f32[128,1,128]{2,1,0:T(1,128)S(1)} all-to-all(f32[128,1,128]{2,1,0:T(1,128)S(1)} %get-tuple-element.55), channel_id=1, replica_groups=mesh['gx'=8,'gy'=16] {'gx','gy'}, dimensions={0} | all-to-all | bytes 131072 | tf_op jit(solution)/shard_map/all_to_all | solution.py:586
  79.0 2.1 %shard_map.80 = (f32[15,4,64,128]{3,2,1,0:T(8,128)}, f32[4,4]{1,0:T(4,128)}, f32[4]{0:T(128)}, f32[5]{0:T(128)}) custom-call(f32[15,2,64,128]{3,2,1,0:T(8,128)S(1)} %get-tuple-element.51.inside, f32[15,64,128]{2,1,0:T(8,128)S(1)} %get-tuple-element.53.z_face, f32[15,64,128]{2,1,0:T(8,128)S(1)} %get-tuple-element.54.x_face, f32[128,1,128]{2,1,0:T(1,128)S(1)} %all_to_all.5.gathered), custom_call_target="tpu_custom_call" | custom-call | tf_op jit(solution)/shard_map/pallas_call | solution.py:587
Async XLA Ops:
  0.6 7.1 %copy-start = (f32[5,3,4,64,128]{4,3,2,1,0:T(8,128)S(1)}, f32[5,3,4,64,128]{4,3,2,1,0:T(8,128)}, u32[]{:S(2)}) copy-start(f32[5,3,4,64,128]{4,3,2,1,0:T(8,128)} %param.3) | copy-start | bytes 5898244
  0.6 7.1 %copy-start.1 = (f32[2,3,4,64,128]{4,3,2,1,0:T(8,128)S(1)}, f32[2,3,4,64,128]{4,3,2,1,0:T(8,128)}, u32[]{:S(2)}) copy-start(f32[2,3,4,64,128]{4,3,2,1,0:T(8,128)} %param.4) | copy-start | bytes 2359300
  2.9 22.8 %collective-permute-start.3 = (f32[12,64,128]{2,1,0:T(8,128)}, f32[12,64,128]{2,1,0:T(8,128)S(1)}, u32[]{:S(2)}, u32[]{:S(2)}) collective-permute-start(f32[12,64,128]{2,1,0:T(8,128)} %get-tuple-element.38), channel_id=1, source_target_pairs={{0,16},{16,0},{32,48},{48,32},{64,80},{80,64},{96,112},{112,96},{1... | collective-permute-start | bytes 1179656 | tf_op jit(solution)/shard_map/ppermute | solution.py:509
  5.4 20.3 %collective-permute-start.4 = (f32[12,64,128]{2,1,0:T(8,128)}, f32[12,64,128]{2,1,0:T(8,128)S(1)}, u32[]{:S(2)}, u32[]{:S(2)}) collective-permute-start(f32[12,64,128]{2,1,0:T(8,128)} %get-tuple-element.32.face), channel_id=1, source_target_pairs={{0,112},{16,32},{32,16},{48,64},{64,48},{80,96},{96,80},{112,0},{1... | collective-permute-start | bytes 1179656 | tf_op jit(solution)/shard_map/ppermute | solution.py:512
  7.7 1.0 %copy-start.3 = (f32[12,64,128]{2,1,0:T(8,128)S(1)}, f32[12,64,128]{2,1,0:T(8,128)}, u32[]{:S(2)}) copy-start(f32[12,64,128]{2,1,0:T(8,128)} %get-tuple-element.32.face) | copy-start | bytes 1179652
  10.5 1.9 %collective-permute-start = (f32[2,64,128]{2,1,0:T(8,128)S(1)}, f32[2,64,128]{2,1,0:T(8,128)S(1)}, u32[]{:S(2)}, u32[]{:S(2)}) collective-permute-start(f32[2,64,128]{2,1,0:T(8,128)S(1)} %shard_map.67.columns), channel_id=1, source_target_pairs={{0,1},{1,0},{2,3},{3,2},{4,5},{5,4},{6,7},{7,6},{8,9},{9,8},{10,11... | collective-permute-start | bytes 196616 | tf_op jit(solution)/shard_map/ppermute | solution.py:509
  12.4 5.9 %collective-permute-start.1 = (f32[2,64,128]{2,1,0:T(8,128)S(1)}, f32[2,64,128]{2,1,0:T(8,128)S(1)}, u32[]{:S(2)}, u32[]{:S(2)}) collective-permute-start(f32[2,64,128]{2,1,0:T(8,128)S(1)} %shard_map.67.columns), channel_id=1, source_target_pairs={{0,15},{1,2},{2,1},{3,4},{4,3},{5,6},{6,5},{7,8},{8,7},{9,10},{10,... | collective-permute-start | bytes 196616 | tf_op jit(solution)/shard_map/ppermute | solution.py:512
  16.4 18.0 %collective-permute-start.2 = (f32[6,64,128]{2,1,0:T(8,128)S(1)}, f32[6,64,128]{2,1,0:T(8,128)S(1)}, u32[]{:S(2)}, u32[]{:S(2)}) collective-permute-start(f32[6,64,128]{2,1,0:T(8,128)S(1)} %get-tuple-element.36), channel_id=1, source_target_pairs={{0,16},{16,0},{32,48},{48,32},{64,80},{80,64},{96,112},{112,96},{1... | collective-permute-start | bytes 589832 | tf_op jit(solution)/shard_map/ppermute | solution.py:509
  16.9 17.6 %collective-permute-start.5 = (f32[6,64,128]{2,1,0:T(8,128)S(1)}, f32[6,64,128]{2,1,0:T(8,128)S(1)}, u32[]{:S(2)}, u32[]{:S(2)}) collective-permute-start(f32[6,64,128]{2,1,0:T(8,128)S(1)} %get-tuple-element.44), channel_id=1, source_target_pairs={{0,112},{16,32},{32,16},{48,64},{64,48},{80,96},{96,80},{112,0},{1... | collective-permute-start | bytes 589832 | tf_op jit(solution)/shard_map/ppermute | solution.py:512
  25.9 31.7 %collective-permute-start.8 = (f32[12,64,128]{2,1,0:T(8,128)S(1)}, f32[12,64,128]{2,1,0:T(8,128)S(1)}, u32[]{:S(2)}, u32[]{:S(2)}) collective-permute-start(f32[12,64,128]{2,1,0:T(8,128)S(1)} %get-tuple-element.39.z_face), channel_id=1, source_target_pairs={{0,16},{16,0},{32,48},{48,32},{64,80},{80,64},{96,112},{112,96},{1... | collective-permute-start | bytes 1179656 | tf_op jit(solution)/shard_map/ppermute | solution.py:509
  27.2 30.4 %collective-permute-start.9 = (f32[12,64,128]{2,1,0:T(8,128)S(1)}, f32[12,64,128]{2,1,0:T(8,128)S(1)}, u32[]{:S(2)}, u32[]{:S(2)}) collective-permute-start(f32[12,64,128]{2,1,0:T(8,128)S(1)} %get-tuple-element.40.x_face), channel_id=1, source_target_pairs={{0,112},{16,32},{32,16},{48,64},{64,48},{80,96},{96,80},{112,0},{1... | collective-permute-start | bytes 1179656 | tf_op jit(solution)/shard_map/ppermute | solution.py:512
  34.7 22.9 %collective-permute-start.10 = (f32[6,64,128]{2,1,0:T(8,128)S(1)}, f32[6,64,128]{2,1,0:T(8,128)S(1)}, u32[]{:S(2)}, u32[]{:S(2)}) collective-permute-start(f32[6,64,128]{2,1,0:T(8,128)S(1)} %get-tuple-element.45.z_face), channel_id=1, source_target_pairs={{0,16},{16,0},{32,48},{48,32},{64,80},{80,64},{96,112},{112,96},{1... | collective-permute-start | bytes 589832 | tf_op jit(solution)/shard_map/ppermute | solution.py:509
  41.9 15.7 %collective-permute-start.11 = (f32[6,64,128]{2,1,0:T(8,128)S(1)}, f32[6,64,128]{2,1,0:T(8,128)S(1)}, u32[]{:S(2)}, u32[]{:S(2)}) collective-permute-start(f32[6,64,128]{2,1,0:T(8,128)S(1)} %get-tuple-element.46.x_face), channel_id=1, source_target_pairs={{0,112},{16,32},{32,16},{48,64},{64,48},{80,96},{96,80},{112,0},{1... | collective-permute-start | bytes 589832 | tf_op jit(solution)/shard_map/ppermute | solution.py:512
  42.8 6.1 %collective-permute-start.6 = (f32[64,128]{1,0:T(8,128)S(1)}, f32[64,128]{1,0:T(8,128)S(1)}, u32[]{:S(2)}, u32[]{:S(2)}) collective-permute-start(f32[64,128]{1,0:T(8,128)S(1)} %get-tuple-element.49.packed), channel_id=1, source_target_pairs={{0,1},{1,0},{2,3},{3,2},{4,5},{5,4},{6,7},{7,6},{8,9},{9,8},{10,11... | collective-permute-start | bytes 98312 | tf_op jit(solution)/shard_map/ppermute | solution.py:509
  49.0 3.6 %collective-permute-start.7 = (f32[64,128]{1,0:T(8,128)S(1)}, f32[64,128]{1,0:T(8,128)S(1)}, u32[]{:S(2)}, u32[]{:S(2)}) collective-permute-start(f32[64,128]{1,0:T(8,128)S(1)} %get-tuple-element.49.packed), channel_id=1, source_target_pairs={{0,15},{1,2},{2,1},{3,4},{4,3},{5,6},{6,5},{7,8},{8,7},{9,10},{10,... | collective-permute-start | bytes 98312 | tf_op jit(solution)/shard_map/ppermute | solution.py:512
  49.8 3.1 %copy-start.2 = (f32[3,4,64,128]{3,2,1,0:T(8,128)S(1)}, f32[3,4,64,128]{3,2,1,0:T(8,128)}, u32[]{:S(2)}) copy-start(f32[3,4,64,128]{3,2,1,0:T(8,128)} %weight.3) | copy-start | bytes 1179652
